TPU v7x, 256 devices: a whole 4x4x8 slice. The times are simulated.
256 devices in a mesh: tgt: 8 (over x, core), dp: 8 (over y, z_hi), vocab: 4 (over z_lo).
Axes of the slice: x: 4, y: 4, z: 8 (z_hi: 2, z_lo: 4; z = z_hi * 4 + z_lo), core: 2. Of those that a mesh axis runs over, the one named last changes fastest.
Arguments:
- hidden_rows: bfloat16 [3, 1024, 8192], P(None, 'dp', 'tgt'), may hold values from -384 to 384
- fc_weight: bfloat16 [3, 8192, 8192], P(None, 'tgt', ('dp', 'vocab')), may hold values from -0.0390625 to 0.0390625
- head_weight: bfloat16 [8192, 16384], P(('dp', 'vocab'), 'tgt'), may hold values from -0.0625 to 0.0625
- target_probs: bfloat16 [1024, 16384], P('dp', ('tgt', 'vocab')), may hold values from 0 to 1, as said below
- token_ids: int32 [1024], replicated, may hold values from 0 to 128255
- vocab_map: int32 [128256], replicated, may hold values from 0 to 16383
- segment_ids: int32 [1024], replicated, may hold values from 0 to 3, never falling along the last dimension, each value on 1 to 512 neighbouring positions
- loss_mask: int32 [1024], replicated, may hold values 0 or 1
Outputs:
- fc_step: float32 [3, 8192, 8192], P(None, 'tgt', ('dp', 'vocab'))
- head_step: float32 [8192, 16384], P(('dp', 'vocab'), 'tgt')
- loss: float32 [], replicated
Inputs may be any that keep to these rules, and one draw needn't show every extreme that they name: `target_probs`: each row is a probability distribution over the 16384 draft tokens.
All inputs are finite; a program needn't handle non-finite values.
Results may differ from a plain program's by a relative error of at most 0.006.
Values may be sent and summed in bfloat16 or wider, within the bound.
No kernel may reach another device: no remote copies, remote signals or barrier semaphores. Data moves between devices by JAX's collectives and lax.ppermute only.
A program may use at most 128 MiB of HBM per device.

v0:
```python
import jax
import jax.numpy as jnp
from jax import lax
from jax.sharding import PartitionSpec as P

D = 8192
VD = 16384


def per_device(
    hidden_rows, fc_weight, head_weight, target_probs, token_ids, vocab_map, segment_ids, loss_mask
):
    group_rows = hidden_rows.shape[1]
    gathered = lax.all_gather(hidden_rows, "dp", axis=1, tiled=True)
    partial_value = jnp.einsum(
        "jnk,jkc->nc", gathered, fc_weight, preferred_element_type=jnp.float32
    )
    joined_rows = lax.psum(partial_value, "tgt").astype(jnp.bfloat16)
    whole_term = jnp.dot(joined_rows, head_weight, preferred_element_type=jnp.float32)
    split_term = lax.psum_scatter(whole_term, "vocab", scatter_dimension=1, tiled=True)
    logits = lax.psum_scatter(split_term, "dp", scatter_dimension=0, tiled=True)
    first_row = lax.axis_index("dp") * group_rows
    next_segment = jnp.concatenate([segment_ids[1:], jnp.full((1,), -1, jnp.int32)])
    kept_all = loss_mask * (segment_ids == next_segment).astype(jnp.int32)
    kept_count = jnp.maximum(jnp.sum(kept_all), 1).astype(jnp.float32)
    kept_tokens = lax.dynamic_slice_in_dim(kept_all, first_row, group_rows, 0).astype(jnp.float32)
    labels = vocab_map[lax.dynamic_slice_in_dim(token_ids, first_row, group_rows, 0)]
    local_vocab = logits.shape[1]
    offset = lax.axis_index(("tgt", "vocab")) * local_vocab
    onehot = (labels[:, None] - offset == jnp.arange(local_vocab, dtype=jnp.int32)[None, :]).astype(
        jnp.float32
    )
    targets = target_probs.astype(jnp.float32)
    local_max = jnp.max(logits, axis=1)
    picked = jnp.sum(onehot * logits, axis=1)
    dotted = jnp.sum(targets * logits, axis=1)
    prob_mass = jnp.sum(targets, axis=1)
    row_peak = lax.pmax(local_max, ("tgt", "vocab"))
    local_total = jnp.sum(jnp.exp(logits - row_peak[:, None]), axis=1)
    exp_total, dotted, prob_mass, picked = lax.psum(
        (local_total, dotted, prob_mass, picked), ("tgt", "vocab")
    )
    log_total = row_peak + jnp.log(exp_total)
    token_loss = kept_tokens * (log_total * prob_mass - dotted + log_total - picked)
    draft_probs = jnp.exp(logits - log_total[:, None])
    dlogits = (
        kept_tokens[:, None] * (draft_probs * (prob_mass[:, None] + 1.0) - targets - onehot)
    ).astype(jnp.bfloat16)
    shard_grads = lax.all_gather(dlogits, "vocab", axis=1, tiled=True)
    shard_piece = lax.all_gather(shard_grads, "dp", axis=0, tiled=True)
    head_part = jnp.einsum(
        "nc,nv->cv", joined_rows, shard_piece, preferred_element_type=jnp.float32
    )
    feature_rows = jnp.einsum(
        "nv,cv->nc", shard_piece, head_weight, preferred_element_type=jnp.float32
    )
    feature_part = feature_rows
    head_grad, feature_part = (head_part, feature_part)
    feature_grad = lax.psum(feature_part, "tgt").astype(jnp.bfloat16)
    fc_grad = jnp.einsum("jnk,nc->jkc", gathered, feature_grad, preferred_element_type=jnp.float32)
    squares = jnp.sum(head_grad * head_grad) + jnp.sum(fc_grad * fc_grad)
    loss_part = jnp.sum(token_loss) / kept_count / (lax.axis_size("tgt") * lax.axis_size("vocab"))
    squares, loss = lax.psum((squares, loss_part), ("tgt", "dp", "vocab"))
    entries = 3.0 * D * D + 1.0 * D * VD
    scale = lax.rsqrt(squares / entries + 1e-06)
    return (fc_grad * scale, head_grad * scale, loss)


def solution(mesh):
    in_specs = (
        P(None, "dp", "tgt"),
        P(None, "tgt", ("dp", "vocab")),
        P(("dp", "vocab"), "tgt"),
        P("dp", ("tgt", "vocab")),
        P(),
        P(),
        P(),
        P(),
    )
    out_specs = (P(None, "tgt", ("dp", "vocab")), P(("dp", "vocab"), "tgt"), P())
    return jax.shard_map(
        per_device, mesh=mesh, in_specs=in_specs, out_specs=out_specs, check_vma=False
    )
```

profile of v0, /device:TPU:2, one launch (start us, length us, event | category | flops | bytes accessed | tf_op | source)
XLA Modules:
  0.0 879.4 jit_solution(13864409800282045760)
XLA Ops:
  7.2 0.0 all-gather.3.cloned.1.call-start
  7.2 0.7 all-gather.3.cloned.1.call-update
  7.9 0.0 reduce-scatter.3.cloned.1.call-start
  8.0 145.4 %all-gather.3.cloned.1.call-done = bf16[3,1024,1024]{2,1,0:T(8,128)(2,1)} async-done(((bf16[3,128,1024]{2,1,0:T(8,128)(2,1)}), bf16[3,1024,1024]{2,1,0:T(8,128)(2,1)}) %all-gather.3.cloned.1.call-update) | async-done | bytes 6291472 | tf_op jit(solution)/shard_map/all_gather | solution.py:14
  153.4 5.5 convolution_bitcast_fusion
  159.0 49.0 %all-reduce.4 = bf16[1024,256]{1,0:T(8,128)(2,1)S(1)} all-reduce(f32[1024,256]{1,0:T(8,128)} %convolution_bitcast_fusion), channel_id=1, replica_groups=mesh['tgt'=8,'dp'=8,'vocab'=4] {'tgt'}, use_global_device_ids=true, to_apply=%region_0.0 | all-reduce | flops 262144 | bytes 1572864 | tf_op jit(solution)/shard_map/psum | solution.py:18
  208.0 4.5 fusion.15
  212.5 0.0 reduce-scatter.5.cloned.1.call-start
  212.6 146.3 %reduce-scatter.3.cloned.1.call-done = f32[1024,512]{1,0:T(8,128)} async-done(((f32[1024,2048]{1,0:T(8,128)}), f32[1024,512]{1,0:T(8,128)}) %reduce-scatter.3.cloned.1.call-update) | async-done | bytes 2097168 | tf_op jit(solution)/shard_map/reduce_scatter | solution.py:20
  358.9 0.0 all-gather.5.cloned.1.call-start
  358.9 0.1 slice.3
  359.0 0.8 compare_select_fusion
  359.8 2.0 gather_fusion
  361.8 0.7 fusion.12
  362.5 97.0 %reduce-scatter.5.cloned.1.call-done = f32[128,512]{1,0:T(8,128)} async-done(((f32[1024,512]{1,0:T(8,128)}), f32[128,512]{1,0:T(8,128)}) %reduce-scatter.5.cloned.1.call-update) | async-done | bytes 262160 | tf_op jit(solution)/shard_map/reduce_scatter | solution.py:21
  459.4 1.1 reduce_max.9
  460.5 58.7 %pmax.7 = f32[128]{0:T(128)S(1)} all-reduce(f32[128]{0:T(128)S(1)} %reduce_max.9), channel_id=1, replica_groups=mesh['tgt'=8,'dp'=8,'vocab'=4] {'tgt','vocab'}, use_global_device_ids=true, to_apply=%region_4.0 | all-reduce | flops 128 | bytes 1024 | tf_op jit(solution)/shard_map/pmax | solution.py:38
  519.2 1.2 fusion.6
  520.4 65.0 %all-reduce.1 = (f32[128]{0:T(128)S(1)}, f32[128]{0:T(128)S(1)}, f32[128]{0:T(128)S(1)}, f32[128]{0:T(128)S(1)}) all-reduce(f32[128]{0:T(128)S(1)} %get-tuple-element.12, f32[128]{0:T(128)S(1)} %get-tuple-element.11, f32[128]{0:T(128)S(1)} %get-tuple-element.10, ...), channel_id=1, replica_groups=mesh['tgt'=8,'dp'=8,'vocab'=4] {'tgt','vocab'}, use_global_device_ids=true, to_apply=%region_8.0 | all-reduce | flops 512 | bytes 4096 | tf_op jit(solution)/shard_map/psum | solution.py:40
  585.4 0.7 multiply_reduce_fusion.2
  586.1 1.1 fusion.5
  587.2 16.6 %all_gather.10 = bf16[128,2048]{1,0:T(8,128)(2,1)} all-gather(bf16[128,512]{1,0:T(8,128)(2,1)S(1)} %fusion.5), channel_id=1, replica_groups=mesh['tgt'=8,'dp'=8,'vocab'=4] {'vocab'}, dimensions={1}, use_global_device_ids=true | all-gather | bytes 655360 | tf_op jit(solution)/shard_map/all_gather | solution.py:49
  603.8 0.0 all-gather.5.cloned.1.call-update
  605.1 113.2 %all-gather.5.cloned.1.call-done = bf16[1024,2048]{1,0:T(8,128)(2,1)} async-done(((bf16[128,2048]{1,0:T(8,128)(2,1)}), bf16[1024,2048]{1,0:T(8,128)(2,1)}) %all-gather.5.cloned.1.call-update) | async-done | bytes 4194320 | tf_op jit(solution)/shard_map/all_gather | solution.py:50
  718.3 4.4 fusion.14
  722.8 49.0 %all-reduce.5 = bf16[1024,256]{0,1:T(8,128)(2,1)S(1)} all-reduce(f32[1024,256]{0,1:T(8,128)} %fusion.14), channel_id=1, replica_groups=mesh['tgt'=8,'dp'=8,'vocab'=4] {'tgt'}, use_global_device_ids=true, to_apply=%region_9.0 | all-reduce | flops 262144 | bytes 1572864 | tf_op jit(solution)/shard_map/psum | solution.py:59
  771.8 5.4 multiply_reduce_fusion.1
  777.2 6.9 multiply_reduce_fusion
  785.3 76.0 %all-reduce = (f32[]{:T(128)}, f32[]{:T(128)}) all-reduce(f32[]{:T(128)S(6)} %add.59, f32[]{:T(128)S(6)} %div.11), channel_id=1, replica_groups=mesh['tgt'=8,'dp'=8,'vocab'=4] {'tgt','dp','vocab'}, use_global_device_ids=true, to_apply=%region_12.0 | all-reduce | flops 2 | bytes 16 | tf_op jit(solution)/shard_map/psum | solution.py:63
  862.0 4.1 multiply_bitcast_fusion
  866.2 3.5 copy.12
  869.7 3.1 broadcast_multiply_fusion
  (14 shorter events, 0.1 us)
Async XLA Ops:
  7.2 146.2 %copy-start = (bf16[3,1024,256]{2,1,0:T(8,128)(2,1)S(1)}, bf16[3,1024,256]{2,1,0:T(8,128)(2,1)}, u32[]{:S(2)}) copy-start(bf16[3,1024,256]{2,1,0:T(8,128)(2,1)} %param.9) | copy-start | bytes 4718596
  7.2 146.2 %all-gather.3.cloned.1.call-start = ((), (), s32[]{:S(2)}) async-start(), calls=%async_computation.2 | async-start | bytes 7077888 | tf_op jit(solution)/shard_map/all_gather | solution.py:14
  7.9 200.1 %copy-start.1 = (bf16[256,2048]{1,0:T(8,128)(2,1)S(1)}, bf16[256,2048]{1,0:T(8,128)(2,1)}, u32[]{:S(2)}) copy-start(bf16[256,2048]{1,0:T(8,128)(2,1)} %param.10) | copy-start | bytes 3145732
  7.9 350.9 %reduce-scatter.3.cloned.1.call-start = ((), (), s32[]{:S(2)}) async-start(), calls=%async_computation.3 | async-start | bytes 10485760 | tf_op jit(solution)/shard_map/reduce_scatter | solution.py:20
  212.5 146.4 %copy-start.3 = (s32[1024]{0:T(1024)S(1)}, s32[1024]{0:T(1024)}, u32[]{:S(2)}) copy-start(s32[1024]{0:T(1024)} %param.14) | copy-start | bytes 12292
  212.5 149.3 %copy-start.4 = (s32[1024]{0:T(1024)S(1)}, s32[1024]{0:T(1024)}, u32[]{:S(2)}) copy-start(s32[1024]{0:T(1024)} %param.15) | copy-start | bytes 12292
  212.5 306.7 %copy-start.2 = (bf16[128,512]{1,0:T(8,128)(2,1)S(1)}, bf16[128,512]{1,0:T(8,128)(2,1)}, u32[]{:S(2)}) copy-start(bf16[128,512]{1,0:T(8,128)(2,1)} %param.11) | copy-start | bytes 393220
  212.5 246.9 %reduce-scatter.5.cloned.1.call-start = ((), (), s32[]{:S(2)}) async-start(), calls=%async_computation.4 | async-start | bytes 2359296 | tf_op jit(solution)/shard_map/reduce_scatter | solution.py:21
  358.9 359.5 %all-gather.5.cloned.1.call-start = ((), (), s32[]{:S(2)}) async-start(), calls=%async_computation.5 | async-start | bytes 4718592 | tf_op jit(solution)/shard_map/all_gather | solution.py:50
Sparse Core Ops, SparseCore 0:
  10.7 142.7 all-gather.2
  212.6 146.1 reduce-scatter.2
  362.9 96.4 reduce-scatter.4
  603.9 114.3 all-gather.4
where the time goes:
time: 882 us; the launch traced here: 879 us
  waiting for transfers between devices  503 us (57%)
  blocking collectives  314 us (36%)
  matrix products  26.7 us (3%)
  between operations  17.2 us (2%)
  other arithmetic  12.8 us (1%)
    reduce_scatter x1, waiting for transfers between devices, per_device(): lax.psum_scatter(whole_term, 'vocab', scatter_dimension=1, tiled=True)  146 us
    all_gather x1, waiting for transfers between devices, per_device(): gathered = lax.all_gather(hidden_rows, 'dp', axis=1, tiled=True)  145 us
    all_gather x1, waiting for transfers between devices, per_device(): shard_piece = lax.all_gather(shard_grads, 'dp', axis=0, tiled=True)  113 us
    reduce_scatter x1, waiting for transfers between devices, per_device(): logits = lax.psum_scatter(split_term, 'dp', scatter_dimension=0, tiled=True)  97 us
    psum x1, blocking collectives, per_device(): squares, loss = lax.psum((squares, loss_part), ('tgt', 'dp', 'vocab'))  76 us
    psum x1, blocking collectives, per_device(): lax.psum((local_total, dotted, prob_mass, picked), ('tgt', 'vocab'))  65 us
    pmax x1, blocking collectives, per_device(): row_peak = lax.pmax(local_max, ('tgt', 'vocab'))  58.7 us
    psum x1, blocking collectives, per_device(): feature_grad = lax.psum(feature_part, 'tgt').astype(jnp.bfloat16)  49 us
  transfers between devices with their start and end apart: 4, of which 4 were waited for; matrix products, arithmetic and copies ran while one was open for 0% of the time, Pallas kernels for 0%

commit v1 on v0

v1 whole, which is shorter than its diff:
```python
import jax
import jax.numpy as jnp
from jax import lax
from jax.sharding import Mesh, PartitionSpec as P

D = 8192
VD = 16384
X, C, Y, ZH, ZL = 4, 2, 4, 2, 4
Z = ZH * ZL
DEPTH = ("zh", "zl")


def spread(value, axes, count):
    return lax.all_to_all(jnp.broadcast_to(value[None], (count,) + value.shape), axes, 0, 0)


def swap(value):
    return lax.ppermute(value, "core", [(0, 1), (1, 0)])


def both_cores(value):
    other = swap(value)
    first = lax.axis_index("core") == 0
    return jnp.stack([jnp.where(first, value, other), jnp.where(first, other, value)])


def pick(value, index, axis):
    return lax.dynamic_index_in_dim(value, index, axis, keepdims=False)


def per_device(
    hidden_rows, fc_weight, head_weight, target_probs, token_ids, vocab_map, segment_ids, loss_mask
):
    x, core, y = lax.axis_index("x"), lax.axis_index("core"), lax.axis_index("y")
    zh, zl = lax.axis_index("zh"), lax.axis_index("zl")
    rows = hidden_rows.shape[1]
    quarter = rows // ZL
    tokens = rows * Y * ZH
    low = tokens // (Y * ZH * X)
    width = fc_weight.shape[2]
    depth = width * Z
    slab = head_weight.shape[1] // Z
    columns = slab * X

    piece = lax.dynamic_slice_in_dim(hidden_rows, zl * quarter, quarter, 1)
    piece = piece.transpose(1, 0, 2).reshape(quarter, -1)
    gathered = lax.all_gather(piece, ("y", "zh", "zl"), axis=0, tiled=True)
    fc_flat = fc_weight.reshape(-1, width)

    head = head_weight.reshape(width, ZL, ZH, slab).transpose(2, 1, 0, 3).reshape(Z, width, slab)
    head = lax.all_to_all(head, DEPTH, 0, 0).reshape(depth, slab)
    head = lax.all_gather(head, "x", axis=1, tiled=True)

    targets = target_probs.reshape(X, low, ZH, slab).transpose(0, 2, 1, 3)
    targets = targets.reshape(X * ZH, low, slab)
    targets = lax.all_to_all(targets, ("x", "zh"), 0, 0).reshape(X, ZH, low, slab)
    targets = targets.transpose(1, 2, 0, 3).reshape(ZH * low, columns).astype(jnp.float32)

    partial = jnp.dot(gathered, fc_flat, preferred_element_type=jnp.float32)
    partial = partial.reshape(Y, ZH, X, low, width)
    partial = pick(partial, core, 1) + swap(pick(partial, 1 - core, 1))
    partial = jnp.sum(lax.all_to_all(partial, "x", 1, 0), axis=0)
    joined_own = partial.reshape(Y * low, width).astype(jnp.bfloat16)
    joined_wide = spread(joined_own, DEPTH, Z).transpose(1, 0, 2).reshape(Y * low, depth)
    joined_pair = both_cores(joined_wide)

    logits = jnp.dot(
        joined_pair.reshape(ZH * Y * low, depth), head, preferred_element_type=jnp.float32
    )
    logits = lax.all_to_all(logits.reshape(ZH, Y, low, columns), "y", 1, 0)
    logits = jnp.sum(logits, axis=0).reshape(ZH * low, columns)

    next_segment = jnp.concatenate([segment_ids[1:], jnp.full((1,), -1, jnp.int32)])
    kept_all = loss_mask * (segment_ids == next_segment).astype(jnp.int32)
    kept_count = jnp.maximum(jnp.sum(kept_all), 1).astype(jnp.float32)

    def own(value):
        value = pick(value.reshape(Y, ZH, X, low), y, 0)
        return pick(value, x, 1).reshape(ZH * low)

    kept_tokens = own(kept_all).astype(jnp.float32)
    labels = vocab_map[own(token_ids)]
    lane = jnp.arange(columns, dtype=jnp.int32)
    vocab_id = (((lane // slab * C + core) * ZL + zl) * ZH + zh) * slab + lane % slab
    onehot = (labels[:, None] == vocab_id[None, :]).astype(jnp.float32)

    local_max = jnp.max(logits, axis=1)
    local_total = jnp.sum(jnp.exp(logits - local_max[:, None]), axis=1)
    picked = jnp.sum(onehot * logits, axis=1)
    dotted = jnp.sum(targets * logits, axis=1)
    prob_mass = jnp.sum(targets, axis=1)
    stats = jnp.stack([local_max, local_total, dotted, prob_mass, picked])
    stats = spread(stats, ("core", "zh", "zl"), C * Z)
    row_peak = jnp.max(stats[:, 0], axis=0)
    exp_total = jnp.sum(stats[:, 1] * jnp.exp(stats[:, 0] - row_peak), axis=0)
    dotted, prob_mass, picked = jnp.sum(stats[:, 2:], axis=0)
    log_total = row_peak + jnp.log(exp_total)
    token_loss = kept_tokens * (log_total * prob_mass - dotted + log_total - picked)
    loss_part = jnp.sum(token_loss) / kept_count / (C * Z)
    draft_probs = jnp.exp(logits - log_total[:, None])
    dlogits = (
        kept_tokens[:, None] * (draft_probs * (prob_mass[:, None] + 1.0) - targets - onehot)
    ).astype(jnp.bfloat16)

    shard = spread(dlogits, "y", Y).reshape(Y, ZH, low, columns)

    def feature(side):
        side = pick(shard, side, 1).reshape(Y * low, columns)
        return lax.dot_general(side, head, (((1,), (1,)), ((), ())), preferred_element_type=jnp.float32)

    theirs = swap(feature(1 - core))
    feature_part = feature(core) + theirs
    feature_part = lax.all_to_all(feature_part.reshape(Y * low, Z, width), DEPTH, 1, 0)
    feature_own = jnp.sum(feature_part, axis=0).astype(jnp.bfloat16)
    feature_all = both_cores(spread(feature_own, "x", X))
    feature_all = feature_all.reshape(ZH, X, Y, low, width).transpose(2, 0, 1, 3, 4)
    feature_all = feature_all.reshape(tokens, width)
    fc_grad = lax.dot_general(
        gathered, feature_all, (((0,), (0,)), ((), ())), preferred_element_type=jnp.float32
    )

    joined_all = both_cores(spread(joined_wide, "x", X)).reshape(tokens, depth)
    dlogits_all = lax.all_to_all(shard.reshape(Y, ZH, low, X, slab), "x", 3, 0)
    dlogits_all = dlogits_all.transpose(2, 0, 1, 3, 4).reshape(tokens, slab)
    head_grad = lax.dot_general(
        joined_all, dlogits_all, (((0,), (0,)), ((), ())), preferred_element_type=jnp.float32
    )
    squares = jnp.sum(head_grad * head_grad) + jnp.sum(fc_grad * fc_grad)
    head_grad = lax.all_to_all(head_grad.reshape(Z, width, slab), DEPTH, 0, 0)
    head_grad = head_grad.reshape(ZH, ZL, width, slab).transpose(2, 1, 0, 3).reshape(width, -1)

    sums = jnp.stack([squares, loss_part])
    sums = jnp.sum(spread(sums, ("x", "core"), X * C), axis=0)
    sums = jnp.sum(spread(sums, ("y", "zh", "zl"), Y * Z), axis=0)
    entries = 3.0 * D * D + 1.0 * D * VD
    scale = lax.rsqrt(sums[0] / entries + 1e-06)
    return ((fc_grad * scale).reshape(fc_weight.shape), head_grad * scale, sums[1])


def solution(mesh):
    fine = Mesh(mesh.devices.reshape(X, C, Y, ZH, ZL), ("x", "core", "y", "zh", "zl"))
    tgt, dp, vocab = ("x", "core"), ("y", "zh"), ("zl",)
    in_specs = (
        P(None, dp, tgt),
        P(None, tgt, dp + vocab),
        P(dp + vocab, tgt),
        P(dp, tgt + vocab),
        P(),
        P(),
        P(),
        P(),
    )
    out_specs = (P(None, tgt, dp + vocab), P(dp + vocab, tgt), P())
    return jax.shard_map(
        per_device, mesh=fine, in_specs=in_specs, out_specs=out_specs, check_vma=False
    )
```

time: 882 us -> 432 us (0.49)
  waiting for transfers between devices: 503 us -> 201 us
  blocking collectives: 314 us -> 97.5 us
  starting transfers between devices: 0.16 us -> 42.1 us
  local copies, waits for them, and re-layouts: 5.6 us -> 23.9 us
    reduce_scatter x2 -> x0, waiting for transfers between devices: 243 us -> none  [the longest x1 146 us: per_device(): lax.psum_scatter(whole_term, 'vocab', scatter_dimension=1, tiled=True)]
    psum x4 -> x0, blocking collectives: 239 us -> none  [the longest x1 76 us: per_device(): squares, loss = lax.psum((squares, loss_part), ('tgt', 'dp', 'vocab'))]
    all_gather x2, waiting for transfers between devices: 259 us -> 67.9 us  [the longest x1 54.8 us: per_device(): gathered = lax.all_gather(piece, ('y', 'zh', 'zl'), axis=0, tiled=True)]
    all_to_all x0 -> x9, waiting for transfers between devices: none -> 129 us  [the longest x1 45.3 us: per_device(): head_grad = lax.all_to_all(head_grad.reshape(Z, width, slab), DEPTH, 0, 0)]
    all_to_all x0 -> x5, blocking collectives: none -> 97.5 us  [the longest x1 42.1 us: per_device(): head = lax.all_to_all(head, DEPTH, 0, 0).reshape(depth, slab)]
    pmax x1 -> x0, blocking collectives: 58.7 us -> none  [per_device(): row_peak = lax.pmax(local_max, ('tgt', 'vocab'))]
    all_to_all x0 -> x9, starting transfers between devices: none -> 41.9 us  [the longest x4 18 us: spread(): lax.all_to_all(jnp.broadcast_to(value[None], (count,) + value.shape), axe...]
    all_gather x1 -> x0, blocking collectives: 16.6 us -> none  [per_device(): shard_grads = lax.all_gather(dlogits, 'vocab', axis=1, tiled=True)]
  transfers between devices with their start and end apart: 4 -> 16, of which waited for: 4 -> 13; matrix products, arithmetic and copies ran while one was open for 0% -> 10% of each run, Pallas kernels for 0% -> 0%
where the time goes in v1:
time: 432 us; the launch traced here: 429 us
  waiting for transfers between devices  201 us (47%)
  blocking collectives  97.5 us (23%)
  starting transfers between devices  42.1 us (10%)
  matrix products  28.8 us (7%)
  local copies, waits for them, and re-layouts  23.9 us (6%)
  other arithmetic  18 us (4%)
  between operations  17.8 us (4%)
    all_gather x1, waiting for transfers between devices, per_device(): gathered = lax.all_gather(piece, ('y', 'zh', 'zl'), axis=0, tiled=True)  54.8 us
    all_to_all x1, waiting for transfers between devices, per_device(): head_grad = lax.all_to_all(head_grad.reshape(Z, width, slab), DEPTH, 0, 0)  45.3 us
    all_to_all x1, blocking collectives, per_device(): head = lax.all_to_all(head, DEPTH, 0, 0).reshape(depth, slab)  42.1 us
    all_to_all x4, waiting for transfers between devices, spread(): lax.all_to_all(jnp.broadcast_to(value[None], (count,) + value.shape), axe...  37.5 us
    all_to_all x3, blocking collectives, spread(): lax.all_to_all(jnp.broadcast_to(value[None], (count,) + value.shape), axe...  37.2 us
    all_to_all x1, waiting for transfers between devices, per_device(): lax.all_to_all(feature_part.reshape(Y * low, Z, width), DEPTH, 1, 0)  22.1 us
    all_to_all x1, blocking collectives, per_device(): partial = jnp.sum(lax.all_to_all(partial, 'x', 1, 0), axis=0)  18.3 us
    all_to_all x4, starting transfers between devices, spread(): lax.all_to_all(jnp.broadcast_to(value[None], (count,) + value.shape), axe...  18 us
  transfers between devices with their start and end apart: 16, of which 13 were waited for; matrix products, arithmetic and copies ran while one was open for 10% of the time, Pallas kernels for 0%

profile of v1, /device:TPU:2, one launch (start us, length us, event | category | flops | bytes accessed | tf_op | source)
XLA Modules:
  0.0 429.2 jit_solution(6362834642913007370)
XLA Ops:
  11.1 42.1 %all_to_all.94 = bf16[8,256,256]{2,1,0:T(8,128)(2,1)} all-to-all(bf16[8,256,256]{2,1,0:T(8,128)(2,1)S(1)} %bitcast.137), channel_id=1, replica_groups=mesh['x'=4,'core'=2,'y'=4,'zh'=2,'zl'=4] {'zh','zl'}, dimensions={0} | all-to-all | bytes 2097152 | tf_op jit(solution)/shard_map/all_to_all | solution.py:51
  53.2 54.8 %all-gather.3.cloned.1.call-done = bf16[1024,3072]{1,0:T(8,128)(2,1)} async-done(((bf16[32,3072]{1,0:T(8,128)(2,1)}), bf16[1024,3072]{1,0:T(8,128)(2,1)}) %all-gather.3.cloned.1.call-update) | async-done | bytes 6291472 | tf_op jit(solution)/shard_map/all_gather | solution.py:47
  108.0 4.6 %fusion.40 = f32[4,2,4,32,256]{4,3,2,1,0:T(8,128)S(1)} fusion(bf16[4,2,4,32,3072]{4,3,2,1,0:T(8,128)(2,1)} %bitcast.161, bf16[3072,256,1,1,1]{1,0,4,3,2:T(8,128)(2,1)S(1)} %bitcast.127), kind=kOutput, calls=%fused_computation.80 | convolution fusion | flops 1610612736 | bytes 8912896 | tf_op jit(solution)/shard_map/dot_general | solution.py:59
  114.8 18.3 %all_to_all.95 = f32[1,4,4,32,256]{4,3,1,0,2:T(8,128)S(1)} all-to-all(f32[1,4,4,32,256]{4,3,1,0,2:T(8,128)S(1)} %copy.124), channel_id=1, replica_groups=mesh['x'=4,'core'=2,'y'=4,'zh'=2,'zl'=4] {'x'}, dimensions={2} | all-to-all | bytes 1048576 | tf_op jit(solution)/shard_map/all_to_all | solution.py:62
  133.1 16.8 %all_to_all.96 = bf16[8,128,256]{2,1,0:T(8,128)(2,1)S(1)} all-to-all(bf16[8,128,256]{2,1,0:T(8,128)(2,1)S(1)} %broadcast_in_dim.17), channel_id=1, replica_groups=mesh['x'=4,'core'=2,'y'=4,'zh'=2,'zl'=4] {'zh','zl'}, dimensions={0} | all-to-all | bytes 1048576 | tf_op jit(solution)/shard_map/all_to_all | solution.py:14
  152.8 13.1 %all-gather.5.cloned.1.call-done = bf16[2048,1024]{1,0:T(8,128)(2,1)} async-done(((bf16[2048,256]{1,0:T(8,128)(2,1)}), bf16[2048,1024]{1,0:T(8,128)(2,1)}) %all-gather.5.cloned.1.call-update) | async-done | bytes 4194320 | tf_op jit(solution)/shard_map/all_gather | solution.py:52
  170.4 3.5 all-to-all-start.3
  175.7 13.0 %all-to-all-done.3 = f32[1,2,4,32,1024]{4,3,1,0,2:T(8,128)S(1)} async-done(((f32[1,2,4,32,1024]{4,3,1,0,2:T(8,128)}), f32[1,2,4,32,1024]{4,3,1,0,2:T(8,128)S(1)}, u32[]{:S(2)}, u32[]{:S(2)}) %all-to-all-start.3) | async-done | bytes 1048608 | tf_op jit(solution)/shard_map/all_to_all | solution.py:70
  188.7 7.6 %all-to-all-start.4 = ((bf16[8,32,256]{2,1,0:T(8,128)(2,1)}), bf16[8,32,256]{2,1,0:T(8,128)(2,1)S(1)}, u32[]{:S(2)}, u32[]{:S(2)}) async-start(bf16[8,32,256]{2,1,0:T(8,128)(2,1)} %bitcast.22), calls=%async_computation.4 | async-start | bytes 262144 | tf_op jit(solution)/shard_map/all_to_all | solution.py:56
  197.3 7.9 %all-to-all-done.4 = bf16[8,32,256]{2,1,0:T(8,128)(2,1)S(1)} async-done(((bf16[8,32,256]{2,1,0:T(8,128)(2,1)}), bf16[8,32,256]{2,1,0:T(8,128)(2,1)S(1)}, u32[]{:S(2)}, u32[]{:S(2)}) %all-to-all-start.4) | async-done | bytes 131104 | tf_op jit(solution)/shard_map/all_to_all | solution.py:56
  206.8 3.6 all-to-all-start.5
  210.7 7.4 %all-to-all-done.5 = f32[16,1,320]{2,1,0:T(1,128)S(1)} async-done(((f32[16,1,320]{2,1,0:T(1,128)}), f32[16,1,320]{2,1,0:T(1,128)S(1)}, u32[]{:S(2)}, u32[]{:S(2)}) %all-to-all-start.5) | async-done | bytes 20512 | tf_op jit(solution)/shard_map/all_to_all | solution.py:14
  224.3 9.4 %all-to-all-done.6 = bf16[4,64,1024]{2,1,0:T(8,128)(2,1)S(1)} async-done(((bf16[4,64,1024]{2,1,0:T(8,128)(2,1)}), bf16[4,64,1024]{2,1,0:T(8,128)(2,1)S(1)}, u32[]{:S(2)}, u32[]{:S(2)}) %all-to-all-start.6) | async-done | bytes 524320 | tf_op jit(solution)/shard_map/all_to_all | solution.py:14
  235.3 6.1 %all-to-all-start.9 = ((bf16[4,128,2048]{2,1,0:T(8,128)(2,1)}), bf16[4,128,2048]{2,1,0:T(8,128)(2,1)}, u32[]{:S(2)}, u32[]{:S(2)}) async-start(bf16[4,128,2048]{2,1,0:T(8,128)(2,1)} %broadcast_in_dim.21), calls=%async_computation.9 | async-start | bytes 4194304 | tf_op jit(solution)/shard_map/all_to_all | solution.py:14
  241.4 4.7 %fusion.41 = f32[128,2048]{1,0:T(8,128)} fusion(bf16[128,1024]{1,0:T(8,128)(2,1)S(1)} %bitcast.148, bf16[2048,1024]{1,0:T(8,128)(2,1)} %all-gather.5.cloned.1.call-done), kind=kOutput, calls=%fused_computation.81 | convolution fusion | flops 536870912 | bytes 5505024 | tf_op jit(solution)/shard_map/dot_general | solution.py:109
  246.1 19.6 %all-to-all-done.9 = bf16[4,128,2048]{2,1,0:T(8,128)(2,1)} async-done(((bf16[4,128,2048]{2,1,0:T(8,128)(2,1)}), bf16[4,128,2048]{2,1,0:T(8,128)(2,1)}, u32[]{:S(2)}, u32[]{:S(2)}) %all-to-all-start.9) | async-done | bytes 2097184 | tf_op jit(solution)/shard_map/all_to_all | solution.py:14
  267.0 4.9 %all-to-all-start.10 = ((bf16[1,4,2,32,4,256]{5,3,2,1,0,4:T(8,128)(2,1)}), bf16[1,4,2,32,4,256]{5,3,2,1,0,4:T(8,128)(2,1)S(1)}, u32[]{:S(2)}, u32[]{:S(2)}) async-start(bf16[1,4,2,32,4,256]{5,3,2,1,0,4:T(8,128)(2,1)} %copy.138), calls=%async_computation.10 | async-start | bytes 1048576 | tf_op jit(solution)/shard_map/all_to_all | solution.py:123
  271.9 3.7 convolution_add_fusion
  277.3 3.6 all-to-all-done.10
  280.9 3.6 all-to-all-start.7
  286.7 4.5 %select_bitcast_fusion.1 = (bf16[1,4,128,2048]{3,2,1,0:T(8,128)(2,1)}, bf16[1,4,128,2048]{3,2,1,0:T(8,128)(2,1)}) fusion(bf16[4,128,2048]{2,1,0:T(8,128)(2,1)} %all-to-all-done.9, bf16[4,128,2048]{2,1,0:T(8,128)(2,1)} %collective-permute-done.4, pred[]{:T(512)S(6)} %eq.36), kind=kLoop, calls=%fused_computation.9 | loop fusion | flops 2097152 | bytes 8388609 | tf_op jit(solution)/shard_map/stack | solution.py:24
  291.2 22.1 %all-to-all-done.7 = f32[1,128,8,256]{3,1,0,2:T(8,128)S(1)} async-done(((f32[1,128,8,256]{3,1,0,2:T(8,128)}), f32[1,128,8,256]{3,1,0,2:T(8,128)S(1)}, u32[]{:S(2)}, u32[]{:S(2)}) %all-to-all-start.7) | async-done | bytes 1048608 | tf_op jit(solution)/shard_map/all_to_all | solution.py:113
  314.1 4.8 %all-to-all-start.8 = ((bf16[4,128,256]{2,1,0:T(8,128)(2,1)}), bf16[4,128,256]{2,1,0:T(8,128)(2,1)S(1)}, u32[]{:S(2)}, u32[]{:S(2)}) async-start(bf16[4,128,256]{2,1,0:T(8,128)(2,1)} %broadcast_in_dim.20), calls=%async_computation.8 | async-start | bytes 524288 | tf_op jit(solution)/shard_map/all_to_all | solution.py:14
  318.9 4.6 %pad_maximum_fusion = bf16[2,4,128,2048]{3,2,1,0:T(8,128)(2,1)} fusion(bf16[1,4,128,2048]{3,2,1,0:T(8,128)(2,1)} %get-tuple-element.13, bf16[1,4,128,2048]{3,2,1,0:T(8,128)(2,1)} %get-tuple-element.12), kind=kLoop, calls=%fused_computation.1 | loop fusion | flops 2097152 | bytes 8388608 | tf_op jit(solution)/shard_map/stack | solution.py:24
  324.6 5.5 %multiply_reduce_fusion.1 = (f32[]{:T(128)}, f32[2048,256]{1,0:T(8,128)}) fusion(bf16[1024,2048]{1,0:T(8,128)(2,1)} %bitcast.135, bf16[1024,256]{1,0:T(8,128)(2,1)S(1)} %bitcast.150), kind=kOutput, calls=%fused_computation.7 | convolution fusion | flops 1074790400 | bytes 6815748 | tf_op jit(solution)/shard_map/dot_general | solution.py:125
  330.2 6.9 %multiply_reduce_fusion = (f32[]{:T(128)}, f32[3072,256]{1,0:T(8,128)}) fusion(bf16[1024,3072]{1,0:T(8,128)(2,1)} %all-gather.3.cloned.1.call-done, bf16[1024,256]{1,0:T(8,128)(2,1)S(1)} %bitcast.153), kind=kOutput, calls=%fused_computation.4 | convolution fusion | flops 1612185600 | bytes 9961476 | tf_op jit(solution)/shard_map/dot_general | solution.py:118
  338.6 7.6 %all_to_all.97 = f32[8,1,2]{2,1,0:T(1,128)S(1)} all-to-all(f32[8,1,2]{2,1,0:T(1,128)S(1)} %broadcast_in_dim.22), channel_id=1, replica_groups=mesh['x'=4,'core'=2,'y'=4,'zh'=2,'zl'=4] {'x','core'}, dimensions={0} | all-to-all | bytes 128 | tf_op jit(solution)/shard_map/all_to_all | solution.py:14
  346.2 12.7 %all_to_all.98 = f32[32,1,2]{2,1,0:T(1,128)S(1)} all-to-all(f32[32,1,2]{2,1,0:T(1,128)S(1)} %broadcast_in_dim.23), channel_id=1, replica_groups=mesh['x'=4,'core'=2,'y'=4,'zh'=2,'zl'=4] {'y','zh','zl'}, dimensions={0} | all-to-all | bytes 512 | tf_op jit(solution)/shard_map/all_to_all | solution.py:14
  359.0 4.3 %all-to-all-start.13 = ((f32[8,256,256]{2,1,0:T(8,128)}), f32[8,256,256]{2,1,0:T(8,128)}, u32[]{:S(2)}, u32[]{:S(2)}) async-start(f32[8,256,256]{2,1,0:T(8,128)} %bitcast.141), calls=%async_computation.13 | async-start | bytes 4194304 | tf_op jit(solution)/shard_map/all_to_all | solution.py:129
  364.6 3.8 broadcast_multiply_fusion
  368.4 45.3 %all-to-all-done.13 = f32[8,256,256]{2,1,0:T(8,128)} async-done(((f32[8,256,256]{2,1,0:T(8,128)}), f32[8,256,256]{2,1,0:T(8,128)}, u32[]{:S(2)}, u32[]{:S(2)}) %all-to-all-start.13) | async-done | bytes 2097184 | tf_op jit(solution)/shard_map/all_to_all | solution.py:129
  418.4 3.9 mul.138
  (112 shorter events, 37.1 us)
Async XLA Ops:
  7.2 100.9 %copy-start = (bf16[3,1024,256]{2,1,0:T(8,128)(2,1)S(1)}, bf16[3,1024,256]{2,1,0:T(8,128)(2,1)}, u32[]{:S(2)}) copy-start(bf16[3,1024,256]{2,1,0:T(8,128)(2,1)} %param.9) | copy-start | bytes 4718596
  7.2 100.8 %all-gather.3.cloned.1.call-start = ((), (), s32[]{:S(2)}) async-start(), calls=%async_computation.14 | async-start | bytes 6488064 | tf_op jit(solution)/shard_map/all_gather | solution.py:47
  9.0 156.9 %all-gather.5.cloned.1.call-start = ((), (), s32[]{:S(2)}) async-start(), calls=%async_computation.15 | async-start | bytes 5242880 | tf_op jit(solution)/shard_map/all_gather | solution.py:52
  112.7 2.0 collective-permute-start
  150.2 2.0 collective-permute-start.1
  169.3 4.6 %copy-start.4 = (s32[1024]{0:T(1024)S(1)}, s32[1024]{0:T(1024)}, u32[]{:S(2)}) copy-start(s32[1024]{0:T(1024)} %param.14) | copy-start | bytes 12292
  169.3 4.7 %copy-start.5 = (s32[1024]{0:T(1024)S(1)}, s32[1024]{0:T(1024)}, u32[]{:S(2)}) copy-start(s32[1024]{0:T(1024)} %param.15) | copy-start | bytes 12292
  169.3 5.5 %copy-start.6 = (s32[1024]{0:T(1024)S(1)}, s32[1024]{0:T(1024)}, u32[]{:S(2)}) copy-start(s32[1024]{0:T(1024)} %param.12) | copy-start | bytes 12292
  169.4 5.7 %copy-start.3 = (bf16[128,512]{1,0:T(8,128)(2,1)S(1)}, bf16[128,512]{1,0:T(8,128)(2,1)}, u32[]{:S(2)}) copy-start(bf16[128,512]{1,0:T(8,128)(2,1)} %param.11) | copy-start | bytes 393220
  169.4 27.0 %copy-start.2 = (s32[128256]{0:T(1024)S(1)}, s32[128256]{0:T(1024)}, u32[]{:S(2)}) copy-start(s32[128256]{0:T(1024)} %param.13) | copy-start | bytes 1539076
  170.4 18.3 %all-to-all-start.3 = ((f32[1,2,4,32,1024]{4,3,1,0,2:T(8,128)}), f32[1,2,4,32,1024]{4,3,1,0,2:T(8,128)S(1)}, u32[]{:S(2)}, u32[]{:S(2)}) async-start(f32[1,2,4,32,1024]{4,3,1,0,2:T(8,128)} %copy.129), calls=%async_computation.3 | async-start | bytes 2097152 | tf_op jit(solution)/shard_map/all_to_all | solution.py:70
  188.7 16.6 %all-to-all-start.4 = ((bf16[8,32,256]{2,1,0:T(8,128)(2,1)}), bf16[8,32,256]{2,1,0:T(8,128)(2,1)S(1)}, u32[]{:S(2)}, u32[]{:S(2)}) async-start(bf16[8,32,256]{2,1,0:T(8,128)(2,1)} %bitcast.22), calls=%async_computation.4 | async-start | bytes 262144 | tf_op jit(solution)/shard_map/all_to_all | solution.py:56
  206.8 11.3 %all-to-all-start.5 = ((f32[16,1,320]{2,1,0:T(1,128)}), f32[16,1,320]{2,1,0:T(1,128)S(1)}, u32[]{:S(2)}, u32[]{:S(2)}) async-start(f32[16,1,320]{2,1,0:T(1,128)} %reshape.436), calls=%async_computation.5 | async-start | bytes 49152 | tf_op jit(solution)/shard_map/all_to_all | solution.py:14
  220.6 13.1 %all-to-all-start.6 = ((bf16[4,64,1024]{2,1,0:T(8,128)(2,1)}), bf16[4,64,1024]{2,1,0:T(8,128)(2,1)S(1)}, u32[]{:S(2)}, u32[]{:S(2)}) async-start(bf16[4,64,1024]{2,1,0:T(8,128)(2,1)} %broadcast_in_dim.19), calls=%async_computation.6 | async-start | bytes 1048576 | tf_op jit(solution)/shard_map/all_to_all | solution.py:14
  235.3 30.4 %all-to-all-start.9 = ((bf16[4,128,2048]{2,1,0:T(8,128)(2,1)}), bf16[4,128,2048]{2,1,0:T(8,128)(2,1)}, u32[]{:S(2)}, u32[]{:S(2)}) async-start(bf16[4,128,2048]{2,1,0:T(8,128)(2,1)} %broadcast_in_dim.21), calls=%async_computation.9 | async-start | bytes 4194304 | tf_op jit(solution)/shard_map/all_to_all | solution.py:14
  246.1 25.8 %collective-permute-start.2 = (f32[128,2048]{1,0:T(8,128)}, f32[128,2048]{1,0:T(8,128)S(1)}, u32[]{:S(2)}, u32[]{:S(2)}) collective-permute-start(f32[128,2048]{1,0:T(8,128)} %fusion.41), channel_id=1, source_target_pairs={{0,32},{32,0},{1,33},{33,1},{2,34},{34,2},{3,35},{35,3},{4,36},{36... | collective-permute-start | bytes 3145736 | tf_op jit(solution)/shard_map/ppermute | solution.py:18
  265.7 21.0 %collective-permute-start.4 = (bf16[4,128,2048]{2,1,0:T(8,128)(2,1)}, bf16[4,128,2048]{2,1,0:T(8,128)(2,1)}, u32[]{:S(2)}, u32[]{:S(2)}) collective-permute-start(bf16[4,128,2048]{2,1,0:T(8,128)(2,1)} %all-to-all-done.9), channel_id=1, source_target_pairs={{0,32},{32,0},{1,33},{33,1},{2,34},{34,2},{3,35},{35,3},{4,36},{36... | collective-permute-start | bytes 6291464 | tf_op jit(solution)/shard_map/ppermute | solution.py:18
  267.0 13.9 %all-to-all-start.10 = ((bf16[1,4,2,32,4,256]{5,3,2,1,0,4:T(8,128)(2,1)}), bf16[1,4,2,32,4,256]{5,3,2,1,0,4:T(8,128)(2,1)S(1)}, u32[]{:S(2)}, u32[]{:S(2)}) async-start(bf16[1,4,2,32,4,256]{5,3,2,1,0,4:T(8,128)(2,1)} %copy.138), calls=%async_computation.10 | async-start | bytes 1048576 | tf_op jit(solution)/shard_map/all_to_all | solution.py:123
  280.9 32.4 %all-to-all-start.7 = ((f32[1,128,8,256]{3,1,0,2:T(8,128)}), f32[1,128,8,256]{3,1,0,2:T(8,128)S(1)}, u32[]{:S(2)}, u32[]{:S(2)}) async-start(f32[1,128,8,256]{3,1,0,2:T(8,128)} %copy.135), calls=%async_computation.7 | async-start | bytes 2097152 | tf_op jit(solution)/shard_map/all_to_all | solution.py:113
  314.1 10.5 %all-to-all-start.8 = ((bf16[4,128,256]{2,1,0:T(8,128)(2,1)}), bf16[4,128,256]{2,1,0:T(8,128)(2,1)S(1)}, u32[]{:S(2)}, u32[]{:S(2)}) async-start(bf16[4,128,256]{2,1,0:T(8,128)(2,1)} %broadcast_in_dim.20), calls=%async_computation.8 | async-start | bytes 524288 | tf_op jit(solution)/shard_map/all_to_all | solution.py:14
  324.6 5.5 %collective-permute-start.3 = (bf16[4,128,256]{2,1,0:T(8,128)(2,1)S(1)}, bf16[4,128,256]{2,1,0:T(8,128)(2,1)S(1)}, u32[]{:S(2)}, u32[]{:S(2)}) collective-permute-start(bf16[4,128,256]{2,1,0:T(8,128)(2,1)S(1)} %all-to-all-done.8), channel_id=1, source_target_pairs={{0,32},{32,0},{1,33},{33,1},{2,34},{34,2},{3,35},{35,3},{4,36},{36... | collective-permute-start | bytes 786440 | tf_op jit(solution)/shard_map/ppermute | solution.py:18
  359.0 54.7 %all-to-all-start.13 = ((f32[8,256,256]{2,1,0:T(8,128)}), f32[8,256,256]{2,1,0:T(8,128)}, u32[]{:S(2)}, u32[]{:S(2)}) async-start(f32[8,256,256]{2,1,0:T(8,128)} %bitcast.141), calls=%async_computation.13 | async-start | bytes 4194304 | tf_op jit(solution)/shard_map/all_to_all | solution.py:129
  415.4 6.9 %copy-start.1 = (bf16[3,1024,256]{2,1,0:T(8,128)(2,1)S(1)}, bf16[3,1024,256]{2,1,0:T(8,128)(2,1)}, u32[]{:S(2)}) copy-start(bf16[3,1024,256]{2,1,0:T(8,128)(2,1)} %param.9) | copy-start | bytes 4718596
Sparse Core Ops, SparseCore 0:
  11.2 96.8 all-gather.2
  109.8 56.0 all-gather.4

commit v2 on v1

v2 whole, which is shorter than its diff:
```python
import jax
import jax.numpy as jnp
from jax import lax
from jax.experimental import pallas as pl
from jax.experimental.pallas import tpu as pltpu
from jax.sharding import Mesh, PartitionSpec as P

D = 8192
VD = 16384
X, C, Y, ZH, ZL = 4, 2, 4, 2, 4
Z = ZH * ZL
DEPTH = ("zh", "zl")


def spread(value, axes, count):
    return lax.all_to_all(jnp.broadcast_to(value[None], (count,) + value.shape), axes, 0, 0)


def swap(value):
    return lax.ppermute(value, "core", [(0, 1), (1, 0)])


def shift(value, axis, by):
    return lax.ppermute(value, axis, [(i, (i + by) % 4) for i in range(4)])


def pick(value, index, axis):
    return lax.dynamic_index_in_dim(value, index, axis, keepdims=False)


def arrange(parts):
    out = jnp.zeros((len(parts),) + parts[0][1].shape, parts[0][1].dtype)
    for index, part in parts:
        out = lax.dynamic_update_index_in_dim(out, part, index, 0)
    return out


def fc_kernel(near_ref, far_ref, feature_ref, out_ref, squares_ref):
    row = 0
    acc = None
    for ref in (near_ref, far_ref):
        rows = ref.shape[0]
        term = lax.dot_general(
            ref[...],
            feature_ref[row : row + rows, :],
            (((0,), (0,)), ((), ())),
            preferred_element_type=jnp.float32,
        )
        acc = term if acc is None else acc + term
        row += rows
    out_ref[...] = acc

    @pl.when(pl.program_id(0) == 0)
    def _():
        squares_ref[...] = jnp.zeros_like(squares_ref)

    squares_ref[...] += jnp.sum(acc * acc, axis=0, keepdims=True)


def fc_product(near, far, feature):
    block = 512
    deep, width = near.shape[1], feature.shape[1]
    out, squares = pl.pallas_call(
        fc_kernel,
        grid=(deep // block,),
        in_specs=[
            pl.BlockSpec((part.shape[0], block), lambda i: (0, i)) for part in (near, far)
        ]
        + [pl.BlockSpec(feature.shape, lambda i: (0, 0))],
        out_specs=[
            pl.BlockSpec((block, width), lambda i: (i, 0)),
            pl.BlockSpec((1, width), lambda i: (0, 0)),
        ],
        out_shape=[
            jax.ShapeDtypeStruct((deep, width), jnp.float32),
            jax.ShapeDtypeStruct((1, width), jnp.float32),
        ],
        compiler_params=pltpu.CompilerParams(
            dimension_semantics=("arbitrary",), vmem_limit_bytes=24 * 1024 * 1024
        ),
        cost_estimate=pl.CostEstimate(
            flops=2 * feature.shape[0] * deep * width, bytes_accessed=10 * 2**20, transcendentals=0
        ),
    )(near, far, feature)
    return out, jnp.sum(squares)


def scale_kernel(scale_ref, value_ref, out_ref):
    out_ref[...] = value_ref[0] * scale_ref[0, 0]


def scaled_columns(value, scale):
    _, width, slab = value.shape
    return pl.pallas_call(
        scale_kernel,
        grid=(Z,),
        in_specs=[
            pl.BlockSpec(memory_space=pltpu.SMEM),
            pl.BlockSpec((1, width, slab), lambda i: ((i % ZH) * ZL + i // ZH, 0, 0)),
        ],
        out_specs=pl.BlockSpec((width, slab), lambda i: (0, i)),
        out_shape=jax.ShapeDtypeStruct((width, Z * slab), jnp.float32),
        cost_estimate=pl.CostEstimate(
            flops=value.size, bytes_accessed=8 * value.size, transcendentals=0
        ),
    )(scale.reshape(1, 1), value)


def total(value):
    value = value + swap(value)
    for axis in ("x", "y"):
        value = (value + shift(value, axis, 2)) + (shift(value, axis, 1) + shift(value, axis, -1))
    for bit in (1, 2, 4):
        value = value + lax.ppermute(value, DEPTH, [(i, i ^ bit) for i in range(Z)])
    return value


def per_device(
    hidden_rows, fc_weight, head_weight, target_probs, token_ids, vocab_map, segment_ids, loss_mask
):
    x, core, y = lax.axis_index("x"), lax.axis_index("core"), lax.axis_index("y")
    zh, zl = lax.axis_index("zh"), lax.axis_index("zl")
    rows = hidden_rows.shape[1]
    tokens = rows * Y * ZH
    low = rows // X
    width = fc_weight.shape[2]
    depth = width * Z
    slab = head_weight.shape[1] // Z
    columns = slab * X
    same_side = core == zh

    flat = hidden_rows.transpose(1, 0, 2).reshape(rows, -1)
    far = lax.ppermute(flat, "zh", [(0, 1), (1, 0)])
    rows_near = lax.all_gather(flat, "y", axis=0, tiled=True)
    rows_far = lax.all_gather(far, "y", axis=0, tiled=True)

    head = head_weight.reshape(width, ZL, ZH, slab).transpose(2, 1, 0, 3).reshape(Z, width, slab)
    head, _ = lax.optimization_barrier((head, far))
    head = lax.all_to_all(head, DEPTH, 0, 0).reshape(depth, slab)

    targets = target_probs.reshape(X, low, ZH, slab).transpose(0, 2, 1, 3)
    targets = targets.reshape(X * ZH, low, slab)
    targets, head = lax.optimization_barrier((targets, head))
    targets = lax.all_to_all(targets, ("x", "zh"), 0, 0).reshape(X, ZH, low, slab)
    targets, rows_near = lax.optimization_barrier((targets, rows_near))

    head = lax.all_gather(head, "x", axis=1, tiled=True)
    targets = targets.transpose(1, 2, 0, 3).reshape(ZH * low, columns).astype(jnp.float32)
    fc_flat = fc_weight.reshape(-1, width)

    part_near = jnp.dot(rows_near, fc_flat, preferred_element_type=jnp.float32)
    part_far = jnp.dot(rows_far, fc_flat, preferred_element_type=jnp.float32)
    theirs = swap(jnp.where(same_side, part_far, part_near))
    partial = jnp.where(same_side, part_near, part_far) + theirs
    partial = partial.reshape(Y, X, low, width)
    joined_own = pick(partial, x, 1)
    for by in (1, -1, 2):
        joined_own = joined_own + shift(pick(partial, (x + by) % X, 1), "x", by)
    joined_own = joined_own.reshape(Y * low, width).astype(jnp.bfloat16)
    joined_wide = spread(joined_own, DEPTH, Z).transpose(1, 0, 2).reshape(Y * low, depth)
    mine, theirs = joined_wide.reshape(Y, low, depth), swap(joined_wide).reshape(Y, low, depth)
    joined_pair = jnp.stack(
        [jnp.where(core == 0, mine, theirs), jnp.where(core == 0, theirs, mine)], axis=1
    )

    partial = jnp.dot(
        joined_pair.reshape(Y * ZH * low, depth), head, preferred_element_type=jnp.float32
    )
    partial = partial.reshape(Y, ZH * low, columns)
    logits = pick(partial, y, 0)
    for by in (1, -1, 2):
        logits = logits + shift(pick(partial, (y + by) % Y, 0), "y", by)

    next_segment = jnp.concatenate([segment_ids[1:], jnp.full((1,), -1, jnp.int32)])
    kept_all = loss_mask * (segment_ids == next_segment).astype(jnp.int32)
    kept_count = jnp.maximum(jnp.sum(kept_all), 1).astype(jnp.float32)

    def own(value):
        value = pick(value.reshape(Y, ZH, X, low), y, 0)
        return pick(value, x, 1).reshape(ZH * low)

    kept_tokens = own(kept_all).astype(jnp.float32)
    labels = vocab_map[own(token_ids)]
    lane = jnp.arange(columns, dtype=jnp.int32)
    vocab_id = (((lane // slab * C + core) * ZL + zl) * ZH + zh) * slab + lane % slab
    onehot = (labels[:, None] == vocab_id[None, :]).astype(jnp.float32)

    local_max = jnp.max(logits, axis=1)
    local_total = jnp.sum(jnp.exp(logits - local_max[:, None]), axis=1)
    picked = jnp.sum(onehot * logits, axis=1)
    dotted = jnp.sum(targets * logits, axis=1)
    prob_mass = jnp.sum(targets, axis=1)
    stats = jnp.stack([local_max, local_total, dotted, prob_mass, picked])
    stats = spread(stats, ("core", "zh", "zl"), C * Z)
    row_peak = jnp.max(stats[:, 0], axis=0)
    exp_total = jnp.sum(stats[:, 1] * jnp.exp(stats[:, 0] - row_peak), axis=0)
    dotted, prob_mass, picked = jnp.sum(stats[:, 2:], axis=0)
    log_total = row_peak + jnp.log(exp_total)
    token_loss = kept_tokens * (log_total * prob_mass - dotted + log_total - picked)
    loss_part = jnp.sum(token_loss) / kept_count / (C * Z)
    draft_probs = jnp.exp(logits - log_total[:, None])
    dlogits = (
        kept_tokens[:, None] * (draft_probs * (prob_mass[:, None] + 1.0) - targets - onehot)
    ).astype(jnp.bfloat16)

    shard = [(y, dlogits)] + [((y - by) % Y, shift(dlogits, "y", by)) for by in (1, -1, 2)]
    shard = arrange(shard).reshape(Y, ZH, low, columns)

    def feature(side):
        side = pick(shard, side, 1).reshape(Y * low, columns)
        return lax.dot_general(side, head, (((1,), (1,)), ((), ())), preferred_element_type=jnp.float32)

    theirs = swap(feature(1 - core))
    feature_part = feature(core) + theirs
    feature_part = lax.all_to_all(feature_part.reshape(Y * low, Z, width), DEPTH, 1, 0)
    feature_own = jnp.sum(feature_part, axis=0).astype(jnp.bfloat16)
    ring = [(x, feature_own)]
    ring += [((x - by) % X, shift(feature_own, "x", by)) for by in (1, -1, 2)]
    ring = arrange(ring).reshape(X, Y, low, width).transpose(1, 0, 2, 3)
    other = swap(ring)
    feature_all = jnp.concatenate([jnp.where(same_side, ring, other), jnp.where(same_side, other, ring)])
    feature_all = feature_all.reshape(tokens, width)
    fc_grad, fc_squares = fc_product(rows_near, rows_far, feature_all)

    joined_all = lax.all_gather(joined_wide, ("x", "core"), axis=0, tiled=True)
    dlogits_all = lax.all_to_all(shard.reshape(Y, ZH, low, X, slab), "x", 3, 0)
    dlogits_all = dlogits_all.transpose(0, 2, 1, 3, 4).reshape(tokens, slab)
    head_grad = lax.dot_general(
        joined_all, dlogits_all, (((0,), (0,)), ((), ())), preferred_element_type=jnp.float32
    )
    squares = jnp.sum(head_grad * head_grad) + fc_squares
    head_grad = lax.all_to_all(head_grad.reshape(Z, width, slab), DEPTH, 0, 0)

    sums = total(jnp.stack([squares, loss_part]))
    entries = 3.0 * D * D + 1.0 * D * VD
    scale = lax.rsqrt(sums[0] / entries + 1e-06)
    return ((fc_grad * scale).reshape(fc_weight.shape), scaled_columns(head_grad, scale), sums[1])


def solution(mesh):
    fine = Mesh(mesh.devices.reshape(X, C, Y, ZH, ZL), ("x", "core", "y", "zh", "zl"))
    tgt, dp, vocab = ("x", "core"), ("y", "zh"), ("zl",)
    in_specs = (
        P(None, dp, tgt),
        P(None, tgt, dp + vocab),
        P(dp + vocab, tgt),
        P(dp, tgt + vocab),
        P(),
        P(),
        P(),
        P(),
    )
    out_specs = (P(None, tgt, dp + vocab), P(dp + vocab, tgt), P())
    return jax.shard_map(
        per_device, mesh=fine, in_specs=in_specs, out_specs=out_specs, check_vma=False
    )
```

time: 432 us -> 340 us (0.79)
  blocking collectives: 97.5 us -> 0 us
  starting transfers between devices: 42.1 us -> 76.2 us
  waiting for transfers between devices: 201 us -> 175 us
  Pallas kernels: 0 us -> 9.48 us
  other arithmetic: 18 us -> 10.1 us
  matrix products: 28.8 us -> 24.2 us
    all_to_all x5 -> x0, blocking collectives: 97.5 us -> none  [the longest x1 42.1 us: per_device(): head = lax.all_to_all(head, DEPTH, 0, 0).reshape(depth, slab)]
    ppermute x0 -> x22, waiting for transfers between devices: none -> 82.5 us  [the longest x18 37.9 us: shift(): return lax.ppermute(value, axis, [(i, (i + by) % 4) for i in range(4)])]
    all_gather x1 -> x3, waiting for transfers between devices: 54.8 us -> 0.02 us  [the longest x1 0.02 us: per_device(): rows_far = lax.all_gather(far, 'y', axis=0, tiled=True)]
    all_to_all x1, waiting for transfers between devices: 45.3 us -> 0.01 us  [per_device(): head_grad = lax.all_to_all(head_grad.reshape(Z, width, slab), DEPTH, 0, 0)]
    ppermute x0 -> x22, starting transfers between devices: none -> 39.6 us  [the longest x18 25.6 us: shift(): return lax.ppermute(value, axis, [(i, (i + by) % 4) for i in range(4)])]
    all_to_all x1, waiting for transfers between devices: 13 us -> 27.1 us  [per_device(): head = lax.all_to_all(head, DEPTH, 0, 0).reshape(depth, slab)]
    all_to_all x4 -> x2, waiting for transfers between devices: 37.5 us -> 23.6 us  [spread(): lax.all_to_all(jnp.broadcast_to(value[None], (count,) + value.shape), axe...]
    pallas_call x0 -> x2, Pallas kernels: none -> 9.48 us  [the longest x1 5.65 us: scaled_columns(): pl.pallas_call(scale_kernel, grid=(Z,), in_specs=[pl.BlockSpec(memory_spa...]
  transfers between devices with their start and end apart: 16 -> 38, of which waited for: 13 -> 27; matrix products, arithmetic and copies ran while one was open for 10% -> 14% of each run, Pallas kernels for 0% -> 1%
where the time goes in v2:
time: 340 us; the launch traced here: 338 us
  waiting for transfers between devices  175 us (51%)
  starting transfers between devices  76.2 us (22%)
  local copies, waits for them, and re-layouts  25.8 us (8%)
  matrix products  24.2 us (7%)
  between operations  17.6 us (5%)
  other arithmetic  10.1 us (3%)
  Pallas kernels  9.48 us (3%)
    ppermute x18, waiting for transfers between devices, shift(): return lax.ppermute(value, axis, [(i, (i + by) % 4) for i in range(4)])  37.9 us
    ppermute x1, waiting for transfers between devices, per_device(): far = lax.ppermute(flat, 'zh', [(0, 1), (1, 0)])  33.4 us
    all_to_all x1, waiting for transfers between devices, per_device(): head = lax.all_to_all(head, DEPTH, 0, 0).reshape(depth, slab)  27.1 us
    ppermute x18, starting transfers between devices, shift(): return lax.ppermute(value, axis, [(i, (i + by) % 4) for i in range(4)])  25.6 us
    all_to_all x2, waiting for transfers between devices, spread(): lax.all_to_all(jnp.broadcast_to(value[None], (count,) + value.shape), axe...  23.6 us
    all_to_all x1, waiting for transfers between devices, per_device(): lax.all_to_all(feature_part.reshape(Y * low, Z, width), DEPTH, 1, 0)  22.1 us
    unnamed x33, local copies, waits for them, and re-layouts  11.3 us
    ppermute x3, waiting for transfers between devices, total(): value = value + lax.ppermute(value, DEPTH, [(i, i ^ bit) for i in range(Z)])  11.2 us
  transfers between devices with their start and end apart: 38, of which 27 were waited for; matrix products, arithmetic and copies ran while one was open for 14% of the time, Pallas kernels for 1%

profile of v2, /device:TPU:2, one launch (start us, length us, event | category | flops | bytes accessed | tf_op | source)
XLA Modules:
  0.0 338.1 jit_solution(11910666770930949944)
XLA Ops:
  10.1 7.3 %collective-permute-start = (bf16[128,3072]{1,0:T(8,128)(2,1)}, bf16[128,3072]{1,0:T(8,128)(2,1)S(1)}, u32[]{:S(2)}, u32[]{:S(2)}) collective-permute-start(bf16[128,3072]{1,0:T(8,128)(2,1)} %copy.118), channel_id=1, source_target_pairs={{0,4},{4,0},{1,5},{5,1},{2,6},{6,2},{3,7},{7,3},{8,12},{12,8},{9,1... | collective-permute-start | bytes 2359304 | tf_op jit(solution)/shard_map/ppermute | solution.py:133
  17.4 33.4 %collective-permute-done = bf16[128,3072]{1,0:T(8,128)(2,1)S(1)} collective-permute-done((bf16[128,3072]{1,0:T(8,128)(2,1)}, bf16[128,3072]{1,0:T(8,128)(2,1)S(1)}, u32[]{:S(2)}, u32[]{:S(2)}) %collective-permute-start) | collective-permute-done | bytes 786464 | tf_op jit(solution)/shard_map/ppermute | solution.py:133
  54.7 7.7 %all-to-all-start = ((bf16[8,256,256]{2,1,0:T(8,128)(2,1)}), bf16[8,256,256]{2,1,0:T(8,128)(2,1)S(1)}, u32[]{:S(2)}, u32[]{:S(2)}) async-start(bf16[8,256,256]{2,1,0:T(8,128)(2,1)} %bitcast.128), calls=%async_computation | async-start | bytes 2097152 | tf_op jit(solution)/shard_map/all_to_all | solution.py:139
  63.2 27.1 %all-to-all-done = bf16[8,256,256]{2,1,0:T(8,128)(2,1)S(1)} async-done(((bf16[8,256,256]{2,1,0:T(8,128)(2,1)}), bf16[8,256,256]{2,1,0:T(8,128)(2,1)S(1)}, u32[]{:S(2)}, u32[]{:S(2)}) %all-to-all-start) | async-done | bytes 1048608 | tf_op jit(solution)/shard_map/all_to_all | solution.py:139
  91.3 4.8 %all-to-all-start.1 = ((bf16[8,32,256]{2,1,0:T(8,128)(2,1)}), bf16[8,32,256]{2,1,0:T(8,128)(2,1)S(1)}, u32[]{:S(2)}, u32[]{:S(2)}) async-start(bf16[8,32,256]{2,1,0:T(8,128)(2,1)} %bitcast.1), calls=%async_computation.1 | async-start | bytes 262144 | tf_op jit(solution)/shard_map/all_to_all | solution.py:144
  96.1 9.1 %all-to-all-done.1 = bf16[8,32,256]{2,1,0:T(8,128)(2,1)S(1)} async-done(((bf16[8,32,256]{2,1,0:T(8,128)(2,1)}), bf16[8,32,256]{2,1,0:T(8,128)(2,1)S(1)}, u32[]{:S(2)}, u32[]{:S(2)}) %all-to-all-start.1) | async-done | bytes 131104 | tf_op jit(solution)/shard_map/all_to_all | solution.py:144
  108.1 3.7 %broadcast_select_fusion.2 = (f32[512,256]{1,0:T(8,128)}, f32[512,256]{1,0:T(8,128)S(1)}) fusion(f32[512,256]{1,0:T(8,128)S(1)} %fusion.36, pred[]{:T(512)S(6)} %eq.38, bf16[512,3072]{1,0:T(8,128)(2,1)} %all-gather.7.cloned.1.call-done.far_ref, bf16[3072,256]{1,0:T(8,128)(2,1)S(1)} %bitcast.122), kind=kOutput, calls=%fused_computation.27 | convolution fusion | flops 805437440 | bytes 6291457 | tf_op jit(solution)/shard_map/dot_general | solution.py:152
  119.5 7.1 %collective-permute-done.4 = f32[4,32,256]{2,1,0:T(8,128)S(1)} collective-permute-done((f32[4,32,256]{2,1,0:T(8,128)S(1)}, f32[4,32,256]{2,1,0:T(8,128)S(1)}, u32[]{:S(2)}, u32[]{:S(2)}) %collective-permute-start.4) | collective-permute-done | bytes 131104 | tf_op jit(solution)/shard_map/ppermute | solution.py:24
  132.1 4.1 %all-to-all-start.2 = ((bf16[8,128,256]{2,1,0:T(8,128)(2,1)}), bf16[8,128,256]{2,1,0:T(8,128)(2,1)S(1)}, u32[]{:S(2)}, u32[]{:S(2)}) async-start(bf16[8,128,256]{2,1,0:T(8,128)(2,1)} %broadcast_in_dim.51), calls=%async_computation.2 | async-start | bytes 1048576 | tf_op jit(solution)/shard_map/all_to_all | solution.py:16
  137.2 16.0 %all-to-all-done.2 = bf16[8,128,256]{2,1,0:T(8,128)(2,1)S(1)} async-done(((bf16[8,128,256]{2,1,0:T(8,128)(2,1)}), bf16[8,128,256]{2,1,0:T(8,128)(2,1)S(1)}, u32[]{:S(2)}, u32[]{:S(2)}) %all-to-all-start.2) | async-done | bytes 524320 | tf_op jit(solution)/shard_map/all_to_all | solution.py:16
  157.4 4.3 %all-gather.9.cloned.1.call-done = bf16[2048,1024]{1,0:T(8,128)(2,1)} async-done(((bf16[2048,256]{1,0:T(8,128)(2,1)}), bf16[2048,1024]{1,0:T(8,128)(2,1)}) %all-gather.9.cloned.1.call-update) | async-done | bytes 4194320 | tf_op jit(solution)/shard_map/all_gather | solution.py:147
  161.7 3.4 %fusion = f32[4,64,1024]{2,1,0:T(8,128)S(1)} fusion(bf16[4,64,2048]{2,1,0:T(8,128)(2,1)S(1)} %bitcast.144, bf16[2048,1024]{1,0:T(8,128)(2,1)} %all-gather.9.cloned.1.call-done), kind=kOutput, calls=%fused_computation.1 | convolution fusion | flops 1073741824 | bytes 6291456 | tf_op jit(solution)/shard_map/dot_general | solution.py:166
  165.2 3.1 collective-permute-start.8
  170.8 5.2 %collective-permute-done.8 = f32[64,1024]{1,0:T(8,128)S(1)} collective-permute-done((f32[64,1024]{1,0:T(8,128)S(1)}, f32[64,1024]{1,0:T(8,128)S(1)}, u32[]{:S(2)}, u32[]{:S(2)}) %collective-permute-start.8) | collective-permute-done | bytes 262176 | tf_op jit(solution)/shard_map/ppermute | solution.py:24
  176.0 3.8 %collective-permute-done.7 = f32[64,1024]{1,0:T(8,128)} collective-permute-done((f32[64,1024]{1,0:T(8,128)S(1)}, f32[64,1024]{1,0:T(8,128)}, u32[]{:S(2)}, u32[]{:S(2)}) %collective-permute-start.7) | collective-permute-done | bytes 262176 | tf_op jit(solution)/shard_map/ppermute | solution.py:24
  182.1 5.5 %all-to-all-start.3 = ((f32[16,1,320]{2,1,0:T(1,128)}), f32[16,1,320]{2,1,0:T(1,128)S(1)}, u32[]{:S(2)}, u32[]{:S(2)}) async-start(f32[16,1,320]{2,1,0:T(1,128)} %reshape.343), calls=%async_computation.3 | async-start | bytes 49152 | tf_op jit(solution)/shard_map/all_to_all | solution.py:16
  187.7 7.6 %all-to-all-done.3 = f32[16,1,320]{2,1,0:T(1,128)S(1)} async-done(((f32[16,1,320]{2,1,0:T(1,128)}), f32[16,1,320]{2,1,0:T(1,128)S(1)}, u32[]{:S(2)}, u32[]{:S(2)}) %all-to-all-start.3) | async-done | bytes 20512 | tf_op jit(solution)/shard_map/all_to_all | solution.py:16
  207.1 4.7 %fusion.37 = f32[128,2048]{1,0:T(8,128)} fusion(bf16[128,1024]{1,0:T(8,128)(2,1)S(1)} %bitcast.148, bf16[2048,1024]{1,0:T(8,128)(2,1)} %all-gather.9.cloned.1.call-done), kind=kOutput, calls=%fused_computation.90 | convolution fusion | flops 536870912 | bytes 5505024 | tf_op jit(solution)/shard_map/dot_general | solution.py:211
  213.1 5.4 %all-to-all-start.5 = ((bf16[1,4,2,32,4,256]{5,3,2,1,0,4:T(8,128)(2,1)}), bf16[1,4,2,32,4,256]{5,3,2,1,0,4:T(8,128)(2,1)S(1)}, u32[]{:S(2)}, u32[]{:S(2)}) async-start(bf16[1,4,2,32,4,256]{5,3,2,1,0,4:T(8,128)(2,1)} %copy.130), calls=%async_computation.5 | async-start | bytes 1048576 | tf_op jit(solution)/shard_map/all_to_all | solution.py:226
  218.5 4.0 %convolution_add_fusion = f32[128,2048]{1,0:T(8,128)S(1)} fusion(f32[128,2048]{1,0:T(8,128)} %collective-permute-done.12, bf16[128,1024]{1,0:T(8,128)(2,1)S(1)} %bitcast.143, bf16[2048,1024]{1,0:T(8,128)(2,1)} %all-gather.9.cloned.1.call-done), kind=kOutput, calls=%fused_computation.3 | convolution fusion | flops 537133056 | bytes 6553600 | tf_op jit(solution)/shard_map/dot_general | solution.py:211
  227.2 3.6 %all-to-all-start.4 = ((f32[1,128,8,256]{3,1,0,2:T(8,128)}), f32[1,128,8,256]{3,1,0,2:T(8,128)S(1)}, u32[]{:S(2)}, u32[]{:S(2)}) async-start(f32[1,128,8,256]{3,1,0,2:T(8,128)} %copy.128), calls=%async_computation.4 | async-start | bytes 2097152 | tf_op jit(solution)/shard_map/all_to_all | solution.py:215
  231.6 5.5 %multiply_reduce_fusion = (f32[]{:T(128)}, f32[2048,256]{1,0:T(8,128)}) fusion(bf16[1024,2048]{0,1:T(8,128)(2,1)} %all-gather.11.cloned.1.call-done, bf16[1024,256]{1,0:T(8,128)(2,1)} %bitcast.149), kind=kOutput, calls=%fused_computation.4 | convolution fusion | flops 1074790400 | bytes 6815748 | tf_op jit(solution)/shard_map/dot_general | solution.py:228
  237.1 22.1 %all-to-all-done.4 = f32[1,128,8,256]{3,1,0,2:T(8,128)S(1)} async-done(((f32[1,128,8,256]{3,1,0,2:T(8,128)}), f32[1,128,8,256]{3,1,0,2:T(8,128)S(1)}, u32[]{:S(2)}, u32[]{:S(2)}) %all-to-all-start.4) | async-done | bytes 1048608 | tf_op jit(solution)/shard_map/all_to_all | solution.py:215
  259.2 4.3 %all-to-all-start.6 = ((f32[8,256,256]{2,1,0:T(8,128)}), f32[8,256,256]{2,1,0:T(8,128)}, u32[]{:S(2)}, u32[]{:S(2)}) async-start(f32[8,256,256]{2,1,0:T(8,128)} %bitcast.138), calls=%async_computation.6 | async-start | bytes 4194304 | tf_op jit(solution)/shard_map/all_to_all | solution.py:232
  277.9 3.8 %shard_map.103 = (f32[3072,256]{1,0:T(8,128)S(1)}, f32[1,256]{1,0:T(1,128)S(1)}) custom-call(bf16[512,3072]{1,0:T(8,128)(2,1)S(1)} %copy-done.3, bf16[512,3072]{1,0:T(8,128)(2,1)S(1)} %copy-done.1, bf16[1024,256]{1,0:T(8,128)(2,1)S(1)} %bitcast.123), custom_call_target="tpu_custom_call" | custom-call | flops 1610612736 | bytes 10485760 | tf_op jit(solution)/shard_map/pallas_call | solution.py:63
  291.5 3.1 collective-permute-done.18
  299.4 3.5 %collective-permute-done.21 = f32[2]{0:T(128)S(1)} collective-permute-done((f32[2]{0:T(128)S(1)}, f32[2]{0:T(128)S(1)}, u32[]{:S(2)}, u32[]{:S(2)}) %collective-permute-start.21) | collective-permute-done | bytes 40 | tf_op jit(solution)/shard_map/ppermute | solution.py:24
  304.8 4.3 %collective-permute-done.24 = f32[2]{0:T(128)S(1)} collective-permute-done((f32[2]{0:T(128)S(1)}, f32[2]{0:T(128)S(1)}, u32[]{:S(2)}, u32[]{:S(2)}) %collective-permute-start.24) | collective-permute-done | bytes 40 | tf_op jit(solution)/shard_map/ppermute | solution.py:114
  309.4 4.0 %collective-permute-done.25 = f32[2]{0:T(128)S(1)} collective-permute-done((f32[2]{0:T(128)S(1)}, f32[2]{0:T(128)S(1)}, u32[]{:S(2)}, u32[]{:S(2)}) %collective-permute-start.25) | collective-permute-done | bytes 40 | tf_op jit(solution)/shard_map/ppermute | solution.py:114
  313.5 4.5 %collective-permute-start.26 = (f32[2]{0:T(128)S(1)}, f32[2]{0:T(128)S(1)}, u32[]{:S(2)}, u32[]{:S(2)}) collective-permute-start(f32[2]{0:T(128)S(1)} %add.341), channel_id=1, source_target_pairs={{0,4},{1,5},{2,6},{3,7},{4,0},{5,1},{6,2},{7,3},{8,12},{9,13},{10,... | collective-permute-start | bytes 32 | tf_op jit(solution)/shard_map/ppermute | solution.py:114
  322.1 3.8 %broadcast_multiply_fusion = f32[3072,256]{1,0:T(8,128)} fusion(f32[3072,256]{1,0:T(8,128)} %copy-done.2, f32[]{:T(128)} %bitcast.58), kind=kLoop, calls=%fused_computation.5 | loop fusion | flops 786432 | bytes 6291460 | tf_op jit(solution)/shard_map/mul | solution.py:237
  325.9 5.7 %shard_map.104 = f32[256,2048]{1,0:T(8,128)} custom-call(f32[1,1]{1,0:T(1,128)} %bitcast.60.scale_ref, f32[8,256,256]{2,1,0:T(8,128)} %all-to-all-done.6.value_ref), custom_call_target="tpu_custom_call" | custom-call | flops 524288 | bytes 4194304 | tf_op jit(solution)/shard_map/pallas_call | solution.py:94
  (168 shorter events, 85.0 us)
Async XLA Ops:
  7.2 98.0 %all-gather.5.cloned.1.call-start = ((), (), s32[]{:S(2)}) async-start(), calls=%async_computation.7 | async-start | bytes 3932160 | tf_op jit(solution)/shard_map/all_gather | solution.py:134
  10.0 98.1 %all-gather.7.cloned.1.call-start = ((), (), s32[]{:S(2)}) async-start(), calls=%async_computation.8 | async-start | bytes 3932160 | tf_op jit(solution)/shard_map/all_gather | solution.py:135
  10.1 40.7 %collective-permute-start = (bf16[128,3072]{1,0:T(8,128)(2,1)}, bf16[128,3072]{1,0:T(8,128)(2,1)S(1)}, u32[]{:S(2)}, u32[]{:S(2)}) collective-permute-start(bf16[128,3072]{1,0:T(8,128)(2,1)} %copy.118), channel_id=1, source_target_pairs={{0,4},{4,0},{1,5},{5,1},{2,6},{6,2},{3,7},{7,3},{8,12},{12,8},{9,1... | collective-permute-start | bytes 2359304 | tf_op jit(solution)/shard_map/ppermute | solution.py:133
  54.7 35.6 %all-to-all-start = ((bf16[8,256,256]{2,1,0:T(8,128)(2,1)}), bf16[8,256,256]{2,1,0:T(8,128)(2,1)S(1)}, u32[]{:S(2)}, u32[]{:S(2)}) async-start(bf16[8,256,256]{2,1,0:T(8,128)(2,1)} %bitcast.128), calls=%async_computation | async-start | bytes 2097152 | tf_op jit(solution)/shard_map/all_to_all | solution.py:139
  62.4 99.3 %all-gather.9.cloned.1.call-start = ((), (), s32[]{:S(2)}) async-start(), calls=%async_computation.9 | async-start | bytes 5242880 | tf_op jit(solution)/shard_map/all_gather | solution.py:147
  91.3 13.9 %all-to-all-start.1 = ((bf16[8,32,256]{2,1,0:T(8,128)(2,1)}), bf16[8,32,256]{2,1,0:T(8,128)(2,1)S(1)}, u32[]{:S(2)}, u32[]{:S(2)}) async-start(bf16[8,32,256]{2,1,0:T(8,128)(2,1)} %bitcast.1), calls=%async_computation.1 | async-start | bytes 262144 | tf_op jit(solution)/shard_map/all_to_all | solution.py:144
  116.0 10.7 %collective-permute-start.4 = (f32[4,32,256]{2,1,0:T(8,128)S(1)}, f32[4,32,256]{2,1,0:T(8,128)S(1)}, u32[]{:S(2)}, u32[]{:S(2)}) collective-permute-start(f32[4,32,256]{2,1,0:T(8,128)S(1)} %get-tuple-element.39), channel_id=1, source_target_pairs={{0,128},{64,192},{128,0},{192,64},{1,129},{65,193},{129,1},{193,65... | collective-permute-start | bytes 393224 | tf_op jit(solution)/shard_map/ppermute | solution.py:24
  117.5 11.9 %collective-permute-start.3 = (f32[4,32,256]{2,1,0:T(8,128)S(1)}, f32[4,32,256]{2,1,0:T(8,128)S(1)}, u32[]{:S(2)}, u32[]{:S(2)}) collective-permute-start(f32[4,32,256]{2,1,0:T(8,128)S(1)} %get-tuple-element.40), channel_id=1, source_target_pairs={{0,192},{64,0},{128,64},{192,128},{1,193},{65,1},{129,65},{193,129... | collective-permute-start | bytes 393224 | tf_op jit(solution)/shard_map/ppermute | solution.py:24
  118.8 12.4 %collective-permute-start.2 = (f32[4,32,256]{2,1,0:T(8,128)S(1)}, f32[4,32,256]{2,1,0:T(8,128)S(1)}, u32[]{:S(2)}, u32[]{:S(2)}) collective-permute-start(f32[4,32,256]{2,1,0:T(8,128)S(1)} %get-tuple-element.38), channel_id=1, source_target_pairs={{0,64},{64,128},{128,192},{192,0},{1,65},{65,129},{129,193},{193,1... | collective-permute-start | bytes 393224 | tf_op jit(solution)/shard_map/ppermute | solution.py:24
  132.1 21.1 %all-to-all-start.2 = ((bf16[8,128,256]{2,1,0:T(8,128)(2,1)}), bf16[8,128,256]{2,1,0:T(8,128)(2,1)S(1)}, u32[]{:S(2)}, u32[]{:S(2)}) async-start(bf16[8,128,256]{2,1,0:T(8,128)(2,1)} %broadcast_in_dim.51), calls=%async_computation.2 | async-start | bytes 1048576 | tf_op jit(solution)/shard_map/all_to_all | solution.py:16
  136.2 95.4 %all-gather.11.cloned.1.call-start = ((), (), s32[]{:S(2)}) async-start(), calls=%async_computation.10 | async-start | bytes 4718592 | tf_op jit(solution)/shard_map/all_gather | solution.py:225
  165.2 10.8 %collective-permute-start.8 = (f32[64,1024]{1,0:T(8,128)S(1)}, f32[64,1024]{1,0:T(8,128)S(1)}, u32[]{:S(2)}, u32[]{:S(2)}) collective-permute-start(f32[64,1024]{1,0:T(8,128)S(1)} %get-tuple-element.30), channel_id=1, source_target_pairs={{0,16},{8,24},{16,0},{24,8},{1,17},{9,25},{17,1},{25,9},{2,18},{10... | collective-permute-start | bytes 786440 | tf_op jit(solution)/shard_map/ppermute | solution.py:24
  168.3 11.5 %collective-permute-start.7 = (f32[64,1024]{1,0:T(8,128)S(1)}, f32[64,1024]{1,0:T(8,128)}, u32[]{:S(2)}, u32[]{:S(2)}) collective-permute-start(f32[64,1024]{1,0:T(8,128)S(1)} %get-tuple-element.31), channel_id=1, source_target_pairs={{0,24},{8,0},{16,8},{24,16},{1,25},{9,1},{17,9},{25,17},{2,26},{10... | collective-permute-start | bytes 786440 | tf_op jit(solution)/shard_map/ppermute | solution.py:24
  169.4 10.4 %collective-permute-start.6 = (f32[64,1024]{1,0:T(8,128)S(1)}, f32[64,1024]{1,0:T(8,128)}, u32[]{:S(2)}, u32[]{:S(2)}) collective-permute-start(f32[64,1024]{1,0:T(8,128)S(1)} %get-tuple-element.29), channel_id=1, source_target_pairs={{0,8},{8,16},{16,24},{24,0},{1,9},{9,17},{17,25},{25,1},{2,10},{10... | collective-permute-start | bytes 786440 | tf_op jit(solution)/shard_map/ppermute | solution.py:24
  182.1 13.2 %all-to-all-start.3 = ((f32[16,1,320]{2,1,0:T(1,128)}), f32[16,1,320]{2,1,0:T(1,128)S(1)}, u32[]{:S(2)}, u32[]{:S(2)}) async-start(f32[16,1,320]{2,1,0:T(1,128)} %reshape.343), calls=%async_computation.3 | async-start | bytes 49152 | tf_op jit(solution)/shard_map/all_to_all | solution.py:16
  196.9 6.5 %collective-permute-start.9 = (bf16[64,1024]{1,0:T(8,128)(2,1)S(1)}, bf16[64,1024]{1,0:T(8,128)(2,1)S(1)}, u32[]{:S(2)}, u32[]{:S(2)}) collective-permute-start(bf16[64,1024]{1,0:T(8,128)(2,1)S(1)} %get-tuple-element.26), channel_id=1, source_target_pairs={{0,8},{8,16},{16,24},{24,0},{1,9},{9,17},{17,25},{25,1},{2,10},{10... | collective-permute-start | bytes 393224 | tf_op jit(solution)/shard_map/ppermute | solution.py:24
  198.4 7.2 %collective-permute-start.10 = (bf16[64,1024]{1,0:T(8,128)(2,1)S(1)}, bf16[64,1024]{1,0:T(8,128)(2,1)S(1)}, u32[]{:S(2)}, u32[]{:S(2)}) collective-permute-start(bf16[64,1024]{1,0:T(8,128)(2,1)S(1)} %get-tuple-element.26), channel_id=1, source_target_pairs={{0,24},{8,0},{16,8},{24,16},{1,25},{9,1},{17,9},{25,17},{2,26},{10... | collective-permute-start | bytes 393224 | tf_op jit(solution)/shard_map/ppermute | solution.py:24
  200.3 6.8 %collective-permute-start.11 = (bf16[64,1024]{1,0:T(8,128)(2,1)S(1)}, bf16[64,1024]{1,0:T(8,128)(2,1)S(1)}, u32[]{:S(2)}, u32[]{:S(2)}) collective-permute-start(bf16[64,1024]{1,0:T(8,128)(2,1)S(1)} %get-tuple-element.26), channel_id=1, source_target_pairs={{0,16},{8,24},{16,0},{24,8},{1,17},{9,25},{17,1},{25,9},{2,18},{10... | collective-permute-start | bytes 393224 | tf_op jit(solution)/shard_map/ppermute | solution.py:24
  211.8 6.7 %collective-permute-start.12 = (f32[128,2048]{1,0:T(8,128)}, f32[128,2048]{1,0:T(8,128)}, u32[]{:S(2)}, u32[]{:S(2)}) collective-permute-start(f32[128,2048]{1,0:T(8,128)} %fusion.37), channel_id=1, source_target_pairs={{0,32},{32,0},{1,33},{33,1},{2,34},{34,2},{3,35},{35,3},{4,36},{36... | collective-permute-start | bytes 3145736 | tf_op jit(solution)/shard_map/ppermute | solution.py:20
  213.1 14.1 %all-to-all-start.5 = ((bf16[1,4,2,32,4,256]{5,3,2,1,0,4:T(8,128)(2,1)}), bf16[1,4,2,32,4,256]{5,3,2,1,0,4:T(8,128)(2,1)S(1)}, u32[]{:S(2)}, u32[]{:S(2)}) async-start(bf16[1,4,2,32,4,256]{5,3,2,1,0,4:T(8,128)(2,1)} %copy.130), calls=%async_computation.5 | async-start | bytes 1048576 | tf_op jit(solution)/shard_map/all_to_all | solution.py:226
  227.2 32.1 %all-to-all-start.4 = ((f32[1,128,8,256]{3,1,0,2:T(8,128)}), f32[1,128,8,256]{3,1,0,2:T(8,128)S(1)}, u32[]{:S(2)}, u32[]{:S(2)}) async-start(f32[1,128,8,256]{3,1,0,2:T(8,128)} %copy.128), calls=%async_computation.4 | async-start | bytes 2097152 | tf_op jit(solution)/shard_map/all_to_all | solution.py:215
  259.2 66.6 %all-to-all-start.6 = ((f32[8,256,256]{2,1,0:T(8,128)}), f32[8,256,256]{2,1,0:T(8,128)}, u32[]{:S(2)}, u32[]{:S(2)}) async-start(f32[8,256,256]{2,1,0:T(8,128)} %bitcast.138), calls=%async_computation.6 | async-start | bytes 4194304 | tf_op jit(solution)/shard_map/all_to_all | solution.py:232
  263.7 4.3 %collective-permute-start.13 = (bf16[128,256]{1,0:T(8,128)(2,1)S(1)}, bf16[128,256]{1,0:T(8,128)(2,1)S(1)}, u32[]{:S(2)}, u32[]{:S(2)}) collective-permute-start(bf16[128,256]{1,0:T(8,128)(2,1)S(1)} %reduce_sum.105), channel_id=1, source_target_pairs={{0,64},{64,128},{128,192},{192,0},{1,65},{65,129},{129,193},{193,1... | collective-permute-start | bytes 196616 | tf_op jit(solution)/shard_map/ppermute | solution.py:24
  263.8 4.8 %collective-permute-start.14 = (bf16[128,256]{1,0:T(8,128)(2,1)S(1)}, bf16[128,256]{1,0:T(8,128)(2,1)S(1)}, u32[]{:S(2)}, u32[]{:S(2)}) collective-permute-start(bf16[128,256]{1,0:T(8,128)(2,1)S(1)} %reduce_sum.105), channel_id=1, source_target_pairs={{0,192},{64,0},{128,64},{192,128},{1,193},{65,1},{129,65},{193,129... | collective-permute-start | bytes 196616 | tf_op jit(solution)/shard_map/ppermute | solution.py:24
  265.8 5.8 %collective-permute-start.15 = (bf16[128,256]{1,0:T(8,128)(2,1)S(1)}, bf16[128,256]{1,0:T(8,128)(2,1)S(1)}, u32[]{:S(2)}, u32[]{:S(2)}) collective-permute-start(bf16[128,256]{1,0:T(8,128)(2,1)S(1)} %reduce_sum.105), channel_id=1, source_target_pairs={{0,128},{64,192},{128,0},{192,64},{1,129},{65,193},{129,1},{193,65... | collective-permute-start | bytes 196616 | tf_op jit(solution)/shard_map/ppermute | solution.py:24
  286.8 4.8 %collective-permute-start.19 = (f32[2]{0:T(128)S(1)}, f32[2]{0:T(128)S(1)}, u32[]{:S(2)}, u32[]{:S(2)}) collective-permute-start(f32[2]{0:T(128)S(1)} %fusion.49), channel_id=1, source_target_pairs={{0,64},{64,128},{128,192},{192,0},{1,65},{65,129},{129,193},{193,1... | collective-permute-start | bytes 32 | tf_op jit(solution)/shard_map/ppermute | solution.py:24
  289.6 5.0 %collective-permute-start.18 = (f32[2]{0:T(128)S(1)}, f32[2]{0:T(128)S(1)}, u32[]{:S(2)}, u32[]{:S(2)}) collective-permute-start(f32[2]{0:T(128)S(1)} %fusion.49), channel_id=1, source_target_pairs={{0,128},{64,192},{128,0},{192,64},{1,129},{65,193},{129,1},{193,65... | collective-permute-start | bytes 32 | tf_op jit(solution)/shard_map/ppermute | solution.py:24
  294.6 4.8 %collective-permute-start.22 = (f32[2]{0:T(128)S(1)}, f32[2]{0:T(128)S(1)}, u32[]{:S(2)}, u32[]{:S(2)}) collective-permute-start(f32[2]{0:T(128)S(1)} %add_add_fusion.1), channel_id=1, source_target_pairs={{0,8},{8,16},{16,24},{24,0},{1,9},{9,17},{17,25},{25,1},{2,10},{10... | collective-permute-start | bytes 32 | tf_op jit(solution)/shard_map/ppermute | solution.py:24
  297.8 5.0 %collective-permute-start.21 = (f32[2]{0:T(128)S(1)}, f32[2]{0:T(128)S(1)}, u32[]{:S(2)}, u32[]{:S(2)}) collective-permute-start(f32[2]{0:T(128)S(1)} %add_add_fusion.1), channel_id=1, source_target_pairs={{0,16},{8,24},{16,0},{24,8},{1,17},{9,25},{17,1},{25,9},{2,18},{10... | collective-permute-start | bytes 32 | tf_op jit(solution)/shard_map/ppermute | solution.py:24
  302.9 6.1 %collective-permute-start.24 = (f32[2]{0:T(128)S(1)}, f32[2]{0:T(128)S(1)}, u32[]{:S(2)}, u32[]{:S(2)}) collective-permute-start(f32[2]{0:T(128)S(1)} %add_add_fusion), channel_id=1, source_target_pairs={{0,1},{1,0},{2,3},{3,2},{4,5},{5,4},{6,7},{7,6},{8,9},{9,8},{10,11... | collective-permute-start | bytes 32 | tf_op jit(solution)/shard_map/ppermute | solution.py:114
  309.0 4.4 %collective-permute-start.25 = (f32[2]{0:T(128)S(1)}, f32[2]{0:T(128)S(1)}, u32[]{:S(2)}, u32[]{:S(2)}) collective-permute-start(f32[2]{0:T(128)S(1)} %add.340), channel_id=1, source_target_pairs={{0,2},{1,3},{2,0},{3,1},{4,6},{5,7},{6,4},{7,5},{8,10},{9,11},{10,... | collective-permute-start | bytes 32 | tf_op jit(solution)/shard_map/ppermute | solution.py:114
  313.5 7.4 %collective-permute-start.26 = (f32[2]{0:T(128)S(1)}, f32[2]{0:T(128)S(1)}, u32[]{:S(2)}, u32[]{:S(2)}) collective-permute-start(f32[2]{0:T(128)S(1)} %add.341), channel_id=1, source_target_pairs={{0,4},{1,5},{2,6},{3,7},{4,0},{5,1},{6,2},{7,3},{8,12},{9,13},{10,... | collective-permute-start | bytes 32 | tf_op jit(solution)/shard_map/ppermute | solution.py:114
  (20 other events, 252.2 us)
Sparse Core Ops, SparseCore 0:
  10.4 45.0 all-gather.4
  57.3 42.3 all-gather.6
  102.0 59.5 all-gather.8
  163.4 38.2 all-gather.10

commit v3 on v2

--- a/solution.py
+++ b/solution.py
@@ -35,10 +35,20 @@
     return out
 
 
-def fc_kernel(near_ref, far_ref, feature_ref, out_ref, squares_ref):
+VMEM_BYTES = 56 * 1024 * 1024
+
+
+def kernel_params():
+    return pltpu.CompilerParams(
+        dimension_semantics=("arbitrary",), vmem_limit_bytes=VMEM_BYTES
+    )
+
+
+def fc_kernel(*refs):
+    row_refs, (feature_ref, out_ref, squares_ref) = refs[:-3], refs[-3:]
     row = 0
     acc = None
-    for ref in (near_ref, far_ref):
+    for ref in row_refs:
         rows = ref.shape[0]
         term = lax.dot_general(
             ref[...],
@@ -57,15 +67,13 @@
     squares_ref[...] += jnp.sum(acc * acc, axis=0, keepdims=True)
 
 
-def fc_product(near, far, feature):
+def fc_product(groups, feature):
     block = 512
-    deep, width = near.shape[1], feature.shape[1]
+    deep, width = groups[0].shape[1], feature.shape[1]
     out, squares = pl.pallas_call(
         fc_kernel,
         grid=(deep // block,),
-        in_specs=[
-            pl.BlockSpec((part.shape[0], block), lambda i: (0, i)) for part in (near, far)
-        ]
+        in_specs=[pl.BlockSpec((part.shape[0], block), lambda i: (0, i)) for part in groups]
         + [pl.BlockSpec(feature.shape, lambda i: (0, 0))],
         out_specs=[
             pl.BlockSpec((block, width), lambda i: (i, 0)),
@@ -75,35 +83,90 @@
             jax.ShapeDtypeStruct((deep, width), jnp.float32),
             jax.ShapeDtypeStruct((1, width), jnp.float32),
         ],
-        compiler_params=pltpu.CompilerParams(
-            dimension_semantics=("arbitrary",), vmem_limit_bytes=24 * 1024 * 1024
-        ),
+        compiler_params=kernel_params(),
         cost_estimate=pl.CostEstimate(
             flops=2 * feature.shape[0] * deep * width, bytes_accessed=10 * 2**20, transcendentals=0
         ),
-    )(near, far, feature)
+    )(*groups, feature)
     return out, jnp.sum(squares)
 
 
-def scale_kernel(scale_ref, value_ref, out_ref):
-    out_ref[...] = value_ref[0] * scale_ref[0, 0]
-
-
-def scaled_columns(value, scale):
-    _, width, slab = value.shape
+def head_kernel(joined_ref, value_ref, out_ref, squares_ref):
+    acc = lax.dot_general(
+        joined_ref[...],
+        value_ref[...],
+        (((0,), (0,)), ((), ())),
+        preferred_element_type=jnp.float32,
+    )
+    out_ref[0] = acc
+
+    @pl.when(pl.program_id(0) == 0)
+    def _():
+        squares_ref[...] = jnp.zeros_like(squares_ref)
+
+    squares_ref[...] += jnp.sum(acc * acc, axis=0, keepdims=True)
+
+
+def head_product(joined, value):
+    rows, depth = joined.shape
+    width, slab = depth // Z, value.shape[1]
+    out, squares = pl.pallas_call(
+        head_kernel,
+        grid=(Z,),
+        in_specs=[
+            pl.BlockSpec((rows, width), lambda i: (0, i)),
+            pl.BlockSpec(value.shape, lambda i: (0, 0)),
+        ],
+        out_specs=[
+            pl.BlockSpec((1, width, slab), lambda i: (i, 0, 0)),
+            pl.BlockSpec((1, slab), lambda i: (0, 0)),
+        ],
+        out_shape=[
+            jax.ShapeDtypeStruct((Z, width, slab), jnp.float32),
+            jax.ShapeDtypeStruct((1, slab), jnp.float32),
+        ],
+        compiler_params=kernel_params(),
+        cost_estimate=pl.CostEstimate(
+            flops=2 * rows * depth * slab, bytes_accessed=7 * 2**20, transcendentals=0
+        ),
+    )(joined, value)
+    return out, jnp.sum(squares)
+
+
+def scale_kernel(scale_ref, fc_ref, head_ref, fc_out_ref, head_out_ref):
+    scale = scale_ref[0, 0]
+    slab = head_ref.shape[3]
+    fc_out_ref[...] = fc_ref[...] * scale
+    for side in range(ZH):
+        head_out_ref[:, side * slab : (side + 1) * slab] = head_ref[side, 0] * scale
+
+
+def scaled(fc_grad, head_grad, scale):
+    deep, width = fc_grad.shape
+    _, _, rows, slab = head_grad.shape
     return pl.pallas_call(
         scale_kernel,
-        grid=(Z,),
+        grid=(ZL,),
         in_specs=[
             pl.BlockSpec(memory_space=pltpu.SMEM),
-            pl.BlockSpec((1, width, slab), lambda i: ((i % ZH) * ZL + i // ZH, 0, 0)),
-        ],
-        out_specs=pl.BlockSpec((width, slab), lambda i: (0, i)),
-        out_shape=jax.ShapeDtypeStruct((width, Z * slab), jnp.float32),
+            pl.BlockSpec((deep // ZL, width), lambda i: (i, 0)),
+            pl.BlockSpec((ZH, 1, rows, slab), lambda i: (0, i, 0, 0)),
+        ],
+        out_specs=[
+            pl.BlockSpec((deep // ZL, width), lambda i: (i, 0)),
+            pl.BlockSpec((rows, ZH * slab), lambda i: (0, i)),
+        ],
+        out_shape=[
+            jax.ShapeDtypeStruct(fc_grad.shape, jnp.float32),
+            jax.ShapeDtypeStruct((rows, Z * slab), jnp.float32),
+        ],
+        compiler_params=kernel_params(),
         cost_estimate=pl.CostEstimate(
-            flops=value.size, bytes_accessed=8 * value.size, transcendentals=0
+            flops=fc_grad.size + head_grad.size,
+            bytes_accessed=8 * (fc_grad.size + head_grad.size),
+            transcendentals=0,
         ),
-    )(scale.reshape(1, 1), value)
+    )(scale.reshape(1, 1), fc_grad, head_grad)
 
 
 def total(value):
@@ -159,6 +222,7 @@
     joined_own = joined_own.reshape(Y * low, width).astype(jnp.bfloat16)
     joined_wide = spread(joined_own, DEPTH, Z).transpose(1, 0, 2).reshape(Y * low, depth)
     mine, theirs = joined_wide.reshape(Y, low, depth), swap(joined_wide).reshape(Y, low, depth)
+    joined_all = lax.all_gather(joined_wide, ("x", "core"), axis=0, tiled=True)
     joined_pair = jnp.stack(
         [jnp.where(core == 0, mine, theirs), jnp.where(core == 0, theirs, mine)], axis=1
     )
@@ -205,6 +269,7 @@
 
     shard = [(y, dlogits)] + [((y - by) % Y, shift(dlogits, "y", by)) for by in (1, -1, 2)]
     shard = arrange(shard).reshape(Y, ZH, low, columns)
+    shard, joined_all = lax.optimization_barrier((shard, joined_all))
 
     def feature(side):
         side = pick(shard, side, 1).reshape(Y * low, columns)
@@ -213,28 +278,28 @@
     theirs = swap(feature(1 - core))
     feature_part = feature(core) + theirs
     feature_part = lax.all_to_all(feature_part.reshape(Y * low, Z, width), DEPTH, 1, 0)
+
+    dlogits_all = lax.all_gather(shard.reshape(-1, columns), "x", axis=0, tiled=True)
+    dlogits_all = lax.dynamic_slice_in_dim(dlogits_all, x * slab, slab, 1)
+    dlogits_all = dlogits_all.reshape(X, Y, ZH, low, slab).transpose(0, 2, 1, 3, 4)
+    head_grad, head_squares = head_product(joined_all, dlogits_all.reshape(tokens, slab))
+    feature_part, head_grad = lax.optimization_barrier((feature_part, head_grad))
+    head_grad = lax.all_to_all(head_grad, DEPTH, 0, 0)
+
     feature_own = jnp.sum(feature_part, axis=0).astype(jnp.bfloat16)
+
     ring = [(x, feature_own)]
     ring += [((x - by) % X, shift(feature_own, "x", by)) for by in (1, -1, 2)]
     ring = arrange(ring).reshape(X, Y, low, width).transpose(1, 0, 2, 3)
     other = swap(ring)
-    feature_all = jnp.concatenate([jnp.where(same_side, ring, other), jnp.where(same_side, other, ring)])
-    feature_all = feature_all.reshape(tokens, width)
-    fc_grad, fc_squares = fc_product(rows_near, rows_far, feature_all)
-
-    joined_all = lax.all_gather(joined_wide, ("x", "core"), axis=0, tiled=True)
-    dlogits_all = lax.all_to_all(shard.reshape(Y, ZH, low, X, slab), "x", 3, 0)
-    dlogits_all = dlogits_all.transpose(0, 2, 1, 3, 4).reshape(tokens, slab)
-    head_grad = lax.dot_general(
-        joined_all, dlogits_all, (((0,), (0,)), ((), ())), preferred_element_type=jnp.float32
-    )
-    squares = jnp.sum(head_grad * head_grad) + fc_squares
-    head_grad = lax.all_to_all(head_grad.reshape(Z, width, slab), DEPTH, 0, 0)
-
-    sums = total(jnp.stack([squares, loss_part]))
+    feature_all = jnp.stack([jnp.where(same_side, ring, other), jnp.where(same_side, other, ring)])
+    fc_grad, fc_squares = fc_product([rows_near, rows_far], feature_all.reshape(tokens, width))
+
+    sums = total(jnp.stack([head_squares + fc_squares, loss_part]))
     entries = 3.0 * D * D + 1.0 * D * VD
     scale = lax.rsqrt(sums[0] / entries + 1e-06)
-    return ((fc_grad * scale).reshape(fc_weight.shape), scaled_columns(head_grad, scale), sums[1])
+    fc_step, head_step = scaled(fc_grad, head_grad.reshape(ZH, ZL, width, slab), scale)
+    return (fc_step.reshape(fc_weight.shape), head_step, sums[1])
 
 
 def solution(mesh):

time: 340 us -> 331 us (0.974)
  blocking collectives: 0 us -> 20.7 us
  waiting for transfers between devices: 175 us -> 163 us
  starting transfers between devices: 76.2 us -> 64.3 us
  Pallas kernels: 9.48 us -> 20.1 us
  matrix products: 24.2 us -> 15.4 us
  local copies, waits for them, and re-layouts: 25.8 us -> 21.1 us
    all_to_all x0 -> x1, blocking collectives: none -> 20.7 us  [spread(): lax.all_to_all(jnp.broadcast_to(value[None], (count,) + value.shape), axe...]
    all_to_all x2 -> x1, waiting for transfers between devices: 23.6 us -> 7.52 us  [spread(): lax.all_to_all(jnp.broadcast_to(value[None], (count,) + value.shape), axe...]
    all_to_all x1, waiting for transfers between devices: 22.1 us -> 6.5 us  [per_device(): lax.all_to_all(feature_part.reshape(Y * low, Z, width), DEPTH, 1, 0)]
    all_gather x0 -> x1, waiting for transfers between devices: none -> 13.4 us  [per_device(): lax.all_gather(shard.reshape(-1, columns), 'x', axis=0, tiled=True)]
    pallas_call x1 -> x2, Pallas kernels: 5.65 us -> 12.7 us  [the longest x1 7.47 us: head_product(): pl.pallas_call(head_kernel, grid=(Z,), in_specs=[pl.BlockSpec((rows, widt...]
    dot_general x1 -> x0, matrix products: 5.54 us -> none  [per_device(): lax.dot_general(joined_all, dlogits_all, (((0,), (0,)), ((), ())), prefer...]
    all_to_all x2 -> x1, starting transfers between devices: 9.78 us -> 4.36 us  [per_device(): head_grad = lax.all_to_all(head_grad, DEPTH, 0, 0)]
    unnamed x33 -> x31, local copies, waits for them, and re-layouts: 11.3 us -> 6.24 us
  transfers between devices with their start and end apart: 38 -> 37, of which waited for: 27 -> 31; matrix products, arithmetic and copies ran while one was open for 14% -> 11% of each run, Pallas kernels for 1% -> 4%
where the time goes in v3:
time: 331 us; the launch traced here: 330 us
  waiting for transfers between devices  163 us (49%)
  starting transfers between devices  64.3 us (19%)
  local copies, waits for them, and re-layouts  21.1 us (6%)
  blocking collectives  20.7 us (6%)
  Pallas kernels  20.1 us (6%)
  between operations  17.6 us (5%)
  matrix products  15.4 us (5%)
  other arithmetic  7.68 us (2%)
    ppermute x18, waiting for transfers between devices, shift(): return lax.ppermute(value, axis, [(i, (i + by) % 4) for i in range(4)])  39.7 us
    ppermute x1, waiting for transfers between devices, per_device(): far = lax.ppermute(flat, 'zh', [(0, 1), (1, 0)])  33.4 us
    all_to_all x1, waiting for transfers between devices, per_device(): head = lax.all_to_all(head, DEPTH, 0, 0).reshape(depth, slab)  27.1 us
    ppermute x18, starting transfers between devices, shift(): return lax.ppermute(value, axis, [(i, (i + by) % 4) for i in range(4)])  22.2 us
    all_to_all x1, blocking collectives, spread(): lax.all_to_all(jnp.broadcast_to(value[None], (count,) + value.shape), axe...  20.7 us
    ppermute x3, waiting for transfers between devices, total(): value = value + lax.ppermute(value, DEPTH, [(i, i ^ bit) for i in range(Z)])  15.7 us
    all_gather x1, waiting for transfers between devices, per_device(): lax.all_gather(shard.reshape(-1, columns), 'x', axis=0, tiled=True)  13.4 us
    all_to_all x1, waiting for transfers between devices, per_device(): lax.all_to_all(targets, ('x', 'zh'), 0, 0).reshape(X, ZH, low, slab)  9.07 us
  transfers between devices with their start and end apart: 37, of which 31 were waited for; matrix products, arithmetic and copies ran while one was open for 11% of the time, Pallas kernels for 4%

profile of v3, /device:TPU:2, one launch (start us, length us, event | category | flops | bytes accessed | tf_op | source)
XLA Modules:
  0.0 330.1 jit_solution(8079198628638940599)
XLA Ops:
  10.1 7.3 %collective-permute-start = (bf16[128,3072]{1,0:T(8,128)(2,1)}, bf16[128,3072]{1,0:T(8,128)(2,1)S(1)}, u32[]{:S(2)}, u32[]{:S(2)}) collective-permute-start(bf16[128,3072]{1,0:T(8,128)(2,1)} %copy.118), channel_id=1, source_target_pairs={{0,4},{4,0},{1,5},{5,1},{2,6},{6,2},{3,7},{7,3},{8,12},{12,8},{9,1... | collective-permute-start | bytes 2359304 | tf_op jit(solution)/shard_map/ppermute | solution.py:196
  17.4 33.4 %collective-permute-done = bf16[128,3072]{1,0:T(8,128)(2,1)S(1)} collective-permute-done((bf16[128,3072]{1,0:T(8,128)(2,1)}, bf16[128,3072]{1,0:T(8,128)(2,1)S(1)}, u32[]{:S(2)}, u32[]{:S(2)}) %collective-permute-start) | collective-permute-done | bytes 786464 | tf_op jit(solution)/shard_map/ppermute | solution.py:196
  54.7 7.7 %all-to-all-start = ((bf16[8,256,256]{2,1,0:T(8,128)(2,1)}), bf16[8,256,256]{2,1,0:T(8,128)(2,1)S(1)}, u32[]{:S(2)}, u32[]{:S(2)}) async-start(bf16[8,256,256]{2,1,0:T(8,128)(2,1)} %bitcast.131), calls=%async_computation | async-start | bytes 2097152 | tf_op jit(solution)/shard_map/all_to_all | solution.py:202
  63.2 27.1 %all-to-all-done = bf16[8,256,256]{2,1,0:T(8,128)(2,1)S(1)} async-done(((bf16[8,256,256]{2,1,0:T(8,128)(2,1)}), bf16[8,256,256]{2,1,0:T(8,128)(2,1)S(1)}, u32[]{:S(2)}, u32[]{:S(2)}) %all-to-all-start) | async-done | bytes 1048608 | tf_op jit(solution)/shard_map/all_to_all | solution.py:202
  91.3 4.8 %all-to-all-start.1 = ((bf16[8,32,256]{2,1,0:T(8,128)(2,1)}), bf16[8,32,256]{2,1,0:T(8,128)(2,1)S(1)}, u32[]{:S(2)}, u32[]{:S(2)}) async-start(bf16[8,32,256]{2,1,0:T(8,128)(2,1)} %bitcast.1), calls=%async_computation.1 | async-start | bytes 262144 | tf_op jit(solution)/shard_map/all_to_all | solution.py:207
  96.1 9.1 %all-to-all-done.1 = bf16[8,32,256]{2,1,0:T(8,128)(2,1)S(1)} async-done(((bf16[8,32,256]{2,1,0:T(8,128)(2,1)}), bf16[8,32,256]{2,1,0:T(8,128)(2,1)S(1)}, u32[]{:S(2)}, u32[]{:S(2)}) %all-to-all-start.1) | async-done | bytes 131104 | tf_op jit(solution)/shard_map/all_to_all | solution.py:207
  105.2 2.9 fusion.36
  108.1 3.7 %broadcast_select_fusion.2 = (f32[512,256]{1,0:T(8,128)}, f32[512,256]{1,0:T(8,128)S(1)}) fusion(f32[512,256]{1,0:T(8,128)S(1)} %fusion.36, pred[]{:T(512)S(6)} %eq.40, bf16[512,3072]{1,0:T(8,128)(2,1)} %all-gather.8.cloned.1.call-done.refs_1_, bf16[3072,256]{1,0:T(8,128)(2,1)S(1)} %bitcast.123), kind=kOutput, calls=%fused_computation.27 | convolution fusion | flops 805437440 | bytes 6291457 | tf_op jit(solution)/shard_map/dot_general | solution.py:215
  119.7 5.5 %collective-permute-done.2 = f32[4,32,256]{2,1,0:T(8,128)S(1)} collective-permute-done((f32[4,32,256]{2,1,0:T(8,128)S(1)}, f32[4,32,256]{2,1,0:T(8,128)S(1)}, u32[]{:S(2)}, u32[]{:S(2)}) %collective-permute-start.2) | collective-permute-done | bytes 131104 | tf_op jit(solution)/shard_map/ppermute | solution.py:24
  125.5 6.7 %collective-permute-done.4 = f32[4,32,256]{2,1,0:T(8,128)S(1)} collective-permute-done((f32[4,32,256]{2,1,0:T(8,128)S(1)}, f32[4,32,256]{2,1,0:T(8,128)S(1)}, u32[]{:S(2)}, u32[]{:S(2)}) %collective-permute-start.4) | collective-permute-done | bytes 131104 | tf_op jit(solution)/shard_map/ppermute | solution.py:24
  132.2 20.7 %all_to_all.40 = bf16[8,128,256]{2,1,0:T(8,128)(2,1)S(1)} all-to-all(bf16[8,128,256]{2,1,0:T(8,128)(2,1)S(1)} %broadcast_in_dim.50), channel_id=1, replica_groups=mesh['x'=4,'core'=2,'y'=4,'zh'=2,'zl'=4] {'zh','zl'}, dimensions={0} | all-to-all | bytes 1048576 | tf_op jit(solution)/shard_map/all_to_all | solution.py:16
  157.2 4.5 %all-gather.10.cloned.1.call-done = bf16[2048,1024]{1,0:T(8,128)(2,1)} async-done(((bf16[2048,256]{1,0:T(8,128)(2,1)}), bf16[2048,1024]{1,0:T(8,128)(2,1)}) %all-gather.10.cloned.1.call-update) | async-done | bytes 4194320 | tf_op jit(solution)/shard_map/all_gather | solution.py:210
  161.7 3.4 %fusion = f32[4,64,1024]{2,1,0:T(8,128)S(1)} fusion(bf16[4,64,2048]{2,1,0:T(8,128)(2,1)S(1)} %bitcast.147, bf16[2048,1024]{1,0:T(8,128)(2,1)} %all-gather.10.cloned.1.call-done), kind=kOutput, calls=%fused_computation.1 | convolution fusion | flops 1073741824 | bytes 6291456 | tf_op jit(solution)/shard_map/dot_general | solution.py:230
  170.8 4.0 %collective-permute-done.6 = f32[64,1024]{1,0:T(8,128)S(1)} collective-permute-done((f32[64,1024]{1,0:T(8,128)S(1)}, f32[64,1024]{1,0:T(8,128)S(1)}, u32[]{:S(2)}, u32[]{:S(2)}) %collective-permute-start.6) | collective-permute-done | bytes 262176 | tf_op jit(solution)/shard_map/ppermute | solution.py:24
  174.8 3.8 %collective-permute-done.7 = f32[64,1024]{1,0:T(8,128)} collective-permute-done((f32[64,1024]{1,0:T(8,128)S(1)}, f32[64,1024]{1,0:T(8,128)}, u32[]{:S(2)}, u32[]{:S(2)}) %collective-permute-start.7) | collective-permute-done | bytes 262176 | tf_op jit(solution)/shard_map/ppermute | solution.py:24
  182.6 6.6 %all-to-all-start.3 = ((f32[16,1,320]{2,1,0:T(1,128)}), f32[16,1,320]{2,1,0:T(1,128)S(1)}, u32[]{:S(2)}, u32[]{:S(2)}) async-start(f32[16,1,320]{2,1,0:T(1,128)} %reshape.350), calls=%async_computation.3 | async-start | bytes 49152 | tf_op jit(solution)/shard_map/all_to_all | solution.py:16
  189.4 7.5 %all-to-all-done.3 = f32[16,1,320]{2,1,0:T(1,128)S(1)} async-done(((f32[16,1,320]{2,1,0:T(1,128)}), f32[16,1,320]{2,1,0:T(1,128)S(1)}, u32[]{:S(2)}, u32[]{:S(2)}) %all-to-all-start.3) | async-done | bytes 20512 | tf_op jit(solution)/shard_map/all_to_all | solution.py:16
  202.0 3.1 collective-permute-done.9
  210.4 3.9 %fusion.37 = f32[128,2048]{1,0:T(8,128)S(1)} fusion(bf16[128,1024]{1,0:T(8,128)(2,1)S(1)} %bitcast.151, bf16[2048,1024]{1,0:T(8,128)(2,1)} %all-gather.10.cloned.1.call-done), kind=kOutput, calls=%fused_computation.89 | convolution fusion | flops 536870912 | bytes 5505024 | tf_op jit(solution)/shard_map/dot_general | solution.py:276
  214.4 2.6 collective-permute-done.12
  220.3 3.6 %all-to-all-start.4 = ((f32[1,128,8,256]{3,1,0,2:T(8,128)}), f32[1,128,8,256]{3,1,0,2:T(8,128)S(1)}, u32[]{:S(2)}, u32[]{:S(2)}) async-start(f32[1,128,8,256]{3,1,0,2:T(8,128)} %copy.127), calls=%async_computation.4 | async-start | bytes 2097152 | tf_op jit(solution)/shard_map/all_to_all | solution.py:280
  223.8 13.4 %all-gather.14.cloned.1.call-done = bf16[1024,1024]{1,0:T(8,128)(2,1)} async-done(((bf16[256,1024]{1,0:T(8,128)(2,1)}), bf16[1024,1024]{1,0:T(8,128)(2,1)}) %all-gather.14.cloned.1.call-update) | async-done | bytes 2097168 | tf_op jit(solution)/shard_map/all_gather | solution.py:282
  239.2 7.5 %shard_map.103 = (f32[8,256,256]{2,1,0:T(8,128)}, f32[1,256]{1,0:T(1,128)}) custom-call(bf16[1024,2048]{1,0:T(8,128)(2,1)} %all-gather.12.cloned.1.call-done.joined_ref, bf16[1024,256]{1,0:T(8,128)(2,1)} %bitcast.137), custom_call_target="tpu_custom_call" | custom-call | flops 1073741824 | bytes 7340032 | tf_op jit(solution)/shard_map/pallas_call | solution.py:113
  246.7 6.5 %all-to-all-done.4 = f32[1,128,8,256]{3,1,0,2:T(8,128)S(1)} async-done(((f32[1,128,8,256]{3,1,0,2:T(8,128)}), f32[1,128,8,256]{3,1,0,2:T(8,128)S(1)}, u32[]{:S(2)}, u32[]{:S(2)}) %all-to-all-start.4) | async-done | bytes 1048608 | tf_op jit(solution)/shard_map/all_to_all | solution.py:280
  253.1 4.4 %all-to-all-start.5 = ((f32[8,256,256]{2,1,0:T(8,128)}), f32[8,256,256]{2,1,0:T(8,128)}, u32[]{:S(2)}, u32[]{:S(2)}) async-start(f32[8,256,256]{2,1,0:T(8,128)} %get-tuple-element.30), calls=%async_computation.5 | async-start | bytes 4194304 | tf_op jit(solution)/shard_map/all_to_all | solution.py:287
  262.7 2.8 collective-permute-done.15
  269.4 7.4 %shard_map.104 = (f32[3072,256]{1,0:T(8,128)}, f32[1,256]{1,0:T(1,128)}) custom-call(bf16[512,3072]{1,0:T(8,128)(2,1)} %all-gather.6.cloned.1.call-done.refs_0_, bf16[512,3072]{1,0:T(8,128)(2,1)} %all-gather.8.cloned.1.call-done.refs_1_, bf16[1024,256]{1,0:T(8,128)(2,1)} %bitcast.143), custom_call_target="tpu_custom_call" | custom-call | flops 1610612736 | bytes 10485760 | tf_op jit(solution)/shard_map/pallas_call | solution.py:73
  296.3 8.8 %collective-permute-done.24 = f32[2]{0:T(128)S(1)} collective-permute-done((f32[2]{0:T(128)S(1)}, f32[2]{0:T(128)S(1)}, u32[]{:S(2)}, u32[]{:S(2)}) %collective-permute-start.24) | collective-permute-done | bytes 40 | tf_op jit(solution)/shard_map/ppermute | solution.py:177
  305.6 4.0 %collective-permute-done.25 = f32[2]{0:T(128)S(1)} collective-permute-done((f32[2]{0:T(128)S(1)}, f32[2]{0:T(128)S(1)}, u32[]{:S(2)}, u32[]{:S(2)}) %collective-permute-start.25) | collective-permute-done | bytes 40 | tf_op jit(solution)/shard_map/ppermute | solution.py:177
  309.6 4.5 %collective-permute-start.26 = (f32[2]{0:T(128)S(1)}, f32[2]{0:T(128)S(1)}, u32[]{:S(2)}, u32[]{:S(2)}) collective-permute-start(f32[2]{0:T(128)S(1)} %add.345), channel_id=1, source_target_pairs={{0,4},{1,5},{2,6},{3,7},{4,0},{5,1},{6,2},{7,3},{8,12},{9,13},{10,... | collective-permute-start | bytes 32 | tf_op jit(solution)/shard_map/ppermute | solution.py:177
  314.1 2.9 collective-permute-done.26
  318.3 5.3 %shard_map.105 = (f32[3072,256]{1,0:T(8,128)}, f32[256,2048]{1,0:T(8,128)}) custom-call(f32[1,1]{1,0:T(1,128)} %bitcast.59.scale_ref, f32[3072,256]{1,0:T(8,128)} %get-tuple-element.29.fc_ref, f32[2,4,256,256]{3,2,1,0:T(8,128)} %bitcast.60.head_ref), custom_call_target="tpu_custom_call" | custom-call | flops 1310720 | bytes 10485760 | tf_op jit(solution)/shard_map/pallas_call | solution.py:147
  (164 shorter events, 73.4 us)
Async XLA Ops:
  7.2 98.0 %all-gather.6.cloned.1.call-start = ((), (), s32[]{:S(2)}) async-start(), calls=%async_computation.6 | async-start | bytes 3932160 | tf_op jit(solution)/shard_map/all_gather | solution.py:197
  10.0 98.1 %all-gather.8.cloned.1.call-start = ((), (), s32[]{:S(2)}) async-start(), calls=%async_computation.7 | async-start | bytes 3932160 | tf_op jit(solution)/shard_map/all_gather | solution.py:198
  10.1 40.7 %collective-permute-start = (bf16[128,3072]{1,0:T(8,128)(2,1)}, bf16[128,3072]{1,0:T(8,128)(2,1)S(1)}, u32[]{:S(2)}, u32[]{:S(2)}) collective-permute-start(bf16[128,3072]{1,0:T(8,128)(2,1)} %copy.118), channel_id=1, source_target_pairs={{0,4},{4,0},{1,5},{5,1},{2,6},{6,2},{3,7},{7,3},{8,12},{12,8},{9,1... | collective-permute-start | bytes 2359304 | tf_op jit(solution)/shard_map/ppermute | solution.py:196
  54.7 35.6 %all-to-all-start = ((bf16[8,256,256]{2,1,0:T(8,128)(2,1)}), bf16[8,256,256]{2,1,0:T(8,128)(2,1)S(1)}, u32[]{:S(2)}, u32[]{:S(2)}) async-start(bf16[8,256,256]{2,1,0:T(8,128)(2,1)} %bitcast.131), calls=%async_computation | async-start | bytes 2097152 | tf_op jit(solution)/shard_map/all_to_all | solution.py:202
  62.4 99.3 %all-gather.10.cloned.1.call-start = ((), (), s32[]{:S(2)}) async-start(), calls=%async_computation.8 | async-start | bytes 5242880 | tf_op jit(solution)/shard_map/all_gather | solution.py:210
  91.3 13.9 %all-to-all-start.1 = ((bf16[8,32,256]{2,1,0:T(8,128)(2,1)}), bf16[8,32,256]{2,1,0:T(8,128)(2,1)S(1)}, u32[]{:S(2)}, u32[]{:S(2)}) async-start(bf16[8,32,256]{2,1,0:T(8,128)(2,1)} %bitcast.1), calls=%async_computation.1 | async-start | bytes 262144 | tf_op jit(solution)/shard_map/all_to_all | solution.py:207
  96.1 112.3 %all-gather.12.cloned.1.call-start = ((), (), s32[]{:S(2)}) async-start(), calls=%async_computation.9 | async-start | bytes 4718592 | tf_op jit(solution)/shard_map/all_gather | solution.py:225
  116.0 9.2 %collective-permute-start.2 = (f32[4,32,256]{2,1,0:T(8,128)S(1)}, f32[4,32,256]{2,1,0:T(8,128)S(1)}, u32[]{:S(2)}, u32[]{:S(2)}) collective-permute-start(f32[4,32,256]{2,1,0:T(8,128)S(1)} %get-tuple-element.54), channel_id=1, source_target_pairs={{0,64},{64,128},{128,192},{192,0},{1,65},{65,129},{129,193},{193,1... | collective-permute-start | bytes 393224 | tf_op jit(solution)/shard_map/ppermute | solution.py:24
  116.8 8.7 %collective-permute-start.3 = (f32[4,32,256]{2,1,0:T(8,128)S(1)}, f32[4,32,256]{2,1,0:T(8,128)S(1)}, u32[]{:S(2)}, u32[]{:S(2)}) collective-permute-start(f32[4,32,256]{2,1,0:T(8,128)S(1)} %get-tuple-element.56), channel_id=1, source_target_pairs={{0,192},{64,0},{128,64},{192,128},{1,193},{65,1},{129,65},{193,129... | collective-permute-start | bytes 393224 | tf_op jit(solution)/shard_map/ppermute | solution.py:24
  118.1 14.0 %collective-permute-start.4 = (f32[4,32,256]{2,1,0:T(8,128)S(1)}, f32[4,32,256]{2,1,0:T(8,128)S(1)}, u32[]{:S(2)}, u32[]{:S(2)}) collective-permute-start(f32[4,32,256]{2,1,0:T(8,128)S(1)} %get-tuple-element.55), channel_id=1, source_target_pairs={{0,128},{64,192},{128,0},{192,64},{1,129},{65,193},{129,1},{193,65... | collective-permute-start | bytes 393224 | tf_op jit(solution)/shard_map/ppermute | solution.py:24
  165.2 9.6 %collective-permute-start.6 = (f32[64,1024]{1,0:T(8,128)S(1)}, f32[64,1024]{1,0:T(8,128)S(1)}, u32[]{:S(2)}, u32[]{:S(2)}) collective-permute-start(f32[64,1024]{1,0:T(8,128)S(1)} %get-tuple-element.45), channel_id=1, source_target_pairs={{0,8},{8,16},{16,24},{24,0},{1,9},{9,17},{17,25},{25,1},{2,10},{10... | collective-permute-start | bytes 786440 | tf_op jit(solution)/shard_map/ppermute | solution.py:24
  166.8 11.8 %collective-permute-start.7 = (f32[64,1024]{1,0:T(8,128)S(1)}, f32[64,1024]{1,0:T(8,128)}, u32[]{:S(2)}, u32[]{:S(2)}) collective-permute-start(f32[64,1024]{1,0:T(8,128)S(1)} %get-tuple-element.47), channel_id=1, source_target_pairs={{0,24},{8,0},{16,8},{24,16},{1,25},{9,1},{17,9},{25,17},{2,26},{10... | collective-permute-start | bytes 786440 | tf_op jit(solution)/shard_map/ppermute | solution.py:24
  168.5 11.8 %collective-permute-start.8 = (f32[64,1024]{1,0:T(8,128)S(1)}, f32[64,1024]{1,0:T(8,128)}, u32[]{:S(2)}, u32[]{:S(2)}) collective-permute-start(f32[64,1024]{1,0:T(8,128)S(1)} %get-tuple-element.46), channel_id=1, source_target_pairs={{0,16},{8,24},{16,0},{24,8},{1,17},{9,25},{17,1},{25,9},{2,18},{10... | collective-permute-start | bytes 786440 | tf_op jit(solution)/shard_map/ppermute | solution.py:24
  182.6 14.3 %all-to-all-start.3 = ((f32[16,1,320]{2,1,0:T(1,128)}), f32[16,1,320]{2,1,0:T(1,128)S(1)}, u32[]{:S(2)}, u32[]{:S(2)}) async-start(f32[16,1,320]{2,1,0:T(1,128)} %reshape.350), calls=%async_computation.3 | async-start | bytes 49152 | tf_op jit(solution)/shard_map/all_to_all | solution.py:16
  189.3 48.0 %all-gather.14.cloned.1.call-start = ((), (), s32[]{:S(2)}) async-start(), calls=%async_computation.10 | async-start | bytes 2621440 | tf_op jit(solution)/shard_map/all_gather | solution.py:282
  198.6 6.5 %collective-permute-start.9 = (bf16[64,1024]{1,0:T(8,128)(2,1)S(1)}, bf16[64,1024]{1,0:T(8,128)(2,1)S(1)}, u32[]{:S(2)}, u32[]{:S(2)}) collective-permute-start(bf16[64,1024]{1,0:T(8,128)(2,1)S(1)} %get-tuple-element.40), channel_id=1, source_target_pairs={{0,8},{8,16},{16,24},{24,0},{1,9},{9,17},{17,25},{25,1},{2,10},{10... | collective-permute-start | bytes 393224 | tf_op jit(solution)/shard_map/ppermute | solution.py:24
  199.8 7.4 %collective-permute-start.10 = (bf16[64,1024]{1,0:T(8,128)(2,1)S(1)}, bf16[64,1024]{1,0:T(8,128)(2,1)S(1)}, u32[]{:S(2)}, u32[]{:S(2)}) collective-permute-start(bf16[64,1024]{1,0:T(8,128)(2,1)S(1)} %get-tuple-element.40), channel_id=1, source_target_pairs={{0,24},{8,0},{16,8},{24,16},{1,25},{9,1},{17,9},{25,17},{2,26},{10... | collective-permute-start | bytes 393224 | tf_op jit(solution)/shard_map/ppermute | solution.py:24
  201.9 6.5 %collective-permute-start.11 = (bf16[64,1024]{1,0:T(8,128)(2,1)S(1)}, bf16[64,1024]{1,0:T(8,128)(2,1)S(1)}, u32[]{:S(2)}, u32[]{:S(2)}) collective-permute-start(bf16[64,1024]{1,0:T(8,128)(2,1)S(1)} %get-tuple-element.40), channel_id=1, source_target_pairs={{0,16},{8,24},{16,0},{24,8},{1,17},{9,25},{17,1},{25,9},{2,18},{10... | collective-permute-start | bytes 393224 | tf_op jit(solution)/shard_map/ppermute | solution.py:24
  220.3 32.9 %all-to-all-start.4 = ((f32[1,128,8,256]{3,1,0,2:T(8,128)}), f32[1,128,8,256]{3,1,0,2:T(8,128)S(1)}, u32[]{:S(2)}, u32[]{:S(2)}) async-start(f32[1,128,8,256]{3,1,0,2:T(8,128)} %copy.127), calls=%async_computation.4 | async-start | bytes 2097152 | tf_op jit(solution)/shard_map/all_to_all | solution.py:280
  253.1 65.2 %all-to-all-start.5 = ((f32[8,256,256]{2,1,0:T(8,128)}), f32[8,256,256]{2,1,0:T(8,128)}, u32[]{:S(2)}, u32[]{:S(2)}) async-start(f32[8,256,256]{2,1,0:T(8,128)} %get-tuple-element.30), calls=%async_computation.5 | async-start | bytes 4194304 | tf_op jit(solution)/shard_map/all_to_all | solution.py:287
  257.6 4.3 %collective-permute-start.13 = (bf16[128,256]{1,0:T(8,128)(2,1)S(1)}, bf16[128,256]{1,0:T(8,128)(2,1)S(1)}, u32[]{:S(2)}, u32[]{:S(2)}) collective-permute-start(bf16[128,256]{1,0:T(8,128)(2,1)S(1)} %reduce_sum.106), channel_id=1, source_target_pairs={{0,64},{64,128},{128,192},{192,0},{1,65},{65,129},{129,193},{193,1... | collective-permute-start | bytes 196616 | tf_op jit(solution)/shard_map/ppermute | solution.py:24
  258.4 4.3 %collective-permute-start.14 = (bf16[128,256]{1,0:T(8,128)(2,1)S(1)}, bf16[128,256]{1,0:T(8,128)(2,1)S(1)}, u32[]{:S(2)}, u32[]{:S(2)}) collective-permute-start(bf16[128,256]{1,0:T(8,128)(2,1)S(1)} %reduce_sum.106), channel_id=1, source_target_pairs={{0,192},{64,0},{128,64},{192,128},{1,193},{65,1},{129,65},{193,129... | collective-permute-start | bytes 196616 | tf_op jit(solution)/shard_map/ppermute | solution.py:24
  259.7 5.8 %collective-permute-start.15 = (bf16[128,256]{1,0:T(8,128)(2,1)S(1)}, bf16[128,256]{1,0:T(8,128)(2,1)S(1)}, u32[]{:S(2)}, u32[]{:S(2)}) collective-permute-start(bf16[128,256]{1,0:T(8,128)(2,1)S(1)} %reduce_sum.106), channel_id=1, source_target_pairs={{0,128},{64,192},{128,0},{192,64},{1,129},{65,193},{129,1},{193,65... | collective-permute-start | bytes 196616 | tf_op jit(solution)/shard_map/ppermute | solution.py:24
  280.8 5.3 %collective-permute-start.18 = (f32[2]{0:T(128)S(1)}, f32[2]{0:T(128)S(1)}, u32[]{:S(2)}, u32[]{:S(2)}) collective-permute-start(f32[2]{0:T(128)S(1)} %fusion.47), channel_id=1, source_target_pairs={{0,128},{64,192},{128,0},{192,64},{1,129},{65,193},{129,1},{193,65... | collective-permute-start | bytes 32 | tf_op jit(solution)/shard_map/ppermute | solution.py:24
  282.0 4.1 %collective-permute-start.19 = (f32[2]{0:T(128)S(1)}, f32[2]{0:T(128)S(1)}, u32[]{:S(2)}, u32[]{:S(2)}) collective-permute-start(f32[2]{0:T(128)S(1)} %fusion.47), channel_id=1, source_target_pairs={{0,64},{64,128},{128,192},{192,0},{1,65},{65,129},{129,193},{193,1... | collective-permute-start | bytes 32 | tf_op jit(solution)/shard_map/ppermute | solution.py:24
  284.0 3.5 %collective-permute-start.20 = (f32[2]{0:T(128)S(1)}, f32[2]{0:T(128)S(1)}, u32[]{:S(2)}, u32[]{:S(2)}) collective-permute-start(f32[2]{0:T(128)S(1)} %fusion.47), channel_id=1, source_target_pairs={{0,192},{64,0},{128,64},{192,128},{1,193},{65,1},{129,65},{193,129... | collective-permute-start | bytes 32 | tf_op jit(solution)/shard_map/ppermute | solution.py:24
  287.6 5.0 %collective-permute-start.21 = (f32[2]{0:T(128)S(1)}, f32[2]{0:T(128)S(1)}, u32[]{:S(2)}, u32[]{:S(2)}) collective-permute-start(f32[2]{0:T(128)S(1)} %add_add_fusion.1), channel_id=1, source_target_pairs={{0,16},{8,24},{16,0},{24,8},{1,17},{9,25},{17,1},{25,9},{2,18},{10... | collective-permute-start | bytes 32 | tf_op jit(solution)/shard_map/ppermute | solution.py:24
  288.4 4.8 %collective-permute-start.22 = (f32[2]{0:T(128)S(1)}, f32[2]{0:T(128)S(1)}, u32[]{:S(2)}, u32[]{:S(2)}) collective-permute-start(f32[2]{0:T(128)S(1)} %add_add_fusion.1), channel_id=1, source_target_pairs={{0,8},{8,16},{16,24},{24,0},{1,9},{9,17},{17,25},{25,1},{2,10},{10... | collective-permute-start | bytes 32 | tf_op jit(solution)/shard_map/ppermute | solution.py:24
  290.9 3.5 %collective-permute-start.23 = (f32[2]{0:T(128)S(1)}, f32[2]{0:T(128)S(1)}, u32[]{:S(2)}, u32[]{:S(2)}) collective-permute-start(f32[2]{0:T(128)S(1)} %add_add_fusion.1), channel_id=1, source_target_pairs={{0,24},{8,0},{16,8},{24,16},{1,25},{9,1},{17,9},{25,17},{2,26},{10... | collective-permute-start | bytes 32 | tf_op jit(solution)/shard_map/ppermute | solution.py:24
  294.4 10.7 %collective-permute-start.24 = (f32[2]{0:T(128)S(1)}, f32[2]{0:T(128)S(1)}, u32[]{:S(2)}, u32[]{:S(2)}) collective-permute-start(f32[2]{0:T(128)S(1)} %add_add_fusion), channel_id=1, source_target_pairs={{0,1},{1,0},{2,3},{3,2},{4,5},{5,4},{6,7},{7,6},{8,9},{9,8},{10,11... | collective-permute-start | bytes 32 | tf_op jit(solution)/shard_map/ppermute | solution.py:177
  305.1 4.4 %collective-permute-start.25 = (f32[2]{0:T(128)S(1)}, f32[2]{0:T(128)S(1)}, u32[]{:S(2)}, u32[]{:S(2)}) collective-permute-start(f32[2]{0:T(128)S(1)} %add.344), channel_id=1, source_target_pairs={{0,2},{1,3},{2,0},{3,1},{4,6},{5,7},{6,4},{7,5},{8,10},{9,11},{10,... | collective-permute-start | bytes 32 | tf_op jit(solution)/shard_map/ppermute | solution.py:177
  309.6 7.4 %collective-permute-start.26 = (f32[2]{0:T(128)S(1)}, f32[2]{0:T(128)S(1)}, u32[]{:S(2)}, u32[]{:S(2)}) collective-permute-start(f32[2]{0:T(128)S(1)} %add.345), channel_id=1, source_target_pairs={{0,4},{1,5},{2,6},{3,7},{4,0},{5,1},{6,2},{7,3},{8,12},{9,13},{10,... | collective-permute-start | bytes 32 | tf_op jit(solution)/shard_map/ppermute | solution.py:177
  (18 other events, 315.5 us)
Sparse Core Ops, SparseCore 0:
  10.4 45.0 all-gather.5
  57.3 42.3 all-gather.7
  102.0 59.5 all-gather.9
  164.0 33.3 all-gather.11
  209.3 27.8 all-gather.13

commit v4 on v3

--- a/solution.py
+++ b/solution.py
@@ -73,7 +73,11 @@
     out, squares = pl.pallas_call(
         fc_kernel,
         grid=(deep // block,),
-        in_specs=[pl.BlockSpec((part.shape[0], block), lambda i: (0, i)) for part in groups]
+        in_specs=[
+            pl.BlockSpec((part.shape[0] // 2, block), lambda i, half=half: (half, i))
+            for part in groups
+            for half in range(2)
+        ]
         + [pl.BlockSpec(feature.shape, lambda i: (0, 0))],
         out_specs=[
             pl.BlockSpec((block, width), lambda i: (i, 0)),
@@ -87,8 +91,8 @@
         cost_estimate=pl.CostEstimate(
             flops=2 * feature.shape[0] * deep * width, bytes_accessed=10 * 2**20, transcendentals=0
         ),
-    )(*groups, feature)
-    return out, jnp.sum(squares)
+    )(*[part for part in groups for _ in range(2)], feature)
+    return out, squares
 
 
 def head_kernel(joined_ref, value_ref, out_ref, squares_ref):
@@ -130,7 +134,7 @@
             flops=2 * rows * depth * slab, bytes_accessed=7 * 2**20, transcendentals=0
         ),
     )(joined, value)
-    return out, jnp.sum(squares)
+    return out, squares
 
 
 def scale_kernel(scale_ref, fc_ref, head_ref, fc_out_ref, head_out_ref):
@@ -173,9 +177,12 @@
     value = value + swap(value)
     for axis in ("x", "y"):
         value = (value + shift(value, axis, 2)) + (shift(value, axis, 1) + shift(value, axis, -1))
-    for bit in (1, 2, 4):
-        value = value + lax.ppermute(value, DEPTH, [(i, i ^ bit) for i in range(Z)])
-    return value
+    parts = [value]
+    for by in range(1, Z):
+        parts.append(lax.ppermute(value, DEPTH, [(i, i ^ by) for i in range(Z)]))
+    while len(parts) > 1:
+        parts = [first + second for first, second in zip(parts[::2], parts[1::2])]
+    return parts[0]
 
 
 def per_device(
@@ -205,13 +212,12 @@
     targets = targets.reshape(X * ZH, low, slab)
     targets, head = lax.optimization_barrier((targets, head))
     targets = lax.all_to_all(targets, ("x", "zh"), 0, 0).reshape(X, ZH, low, slab)
-    targets, rows_near = lax.optimization_barrier((targets, rows_near))
 
     head = lax.all_gather(head, "x", axis=1, tiled=True)
-    targets = targets.transpose(1, 2, 0, 3).reshape(ZH * low, columns).astype(jnp.float32)
     fc_flat = fc_weight.reshape(-1, width)
 
     part_near = jnp.dot(rows_near, fc_flat, preferred_element_type=jnp.float32)
+    part_near, targets = lax.optimization_barrier((part_near, targets))
     part_far = jnp.dot(rows_far, fc_flat, preferred_element_type=jnp.float32)
     theirs = swap(jnp.where(same_side, part_far, part_near))
     partial = jnp.where(same_side, part_near, part_far) + theirs
@@ -249,6 +255,7 @@
     vocab_id = (((lane // slab * C + core) * ZL + zl) * ZH + zh) * slab + lane % slab
     onehot = (labels[:, None] == vocab_id[None, :]).astype(jnp.float32)
 
+    targets = targets.transpose(1, 2, 0, 3).reshape(ZH * low, columns).astype(jnp.float32)
     local_max = jnp.max(logits, axis=1)
     local_total = jnp.sum(jnp.exp(logits - local_max[:, None]), axis=1)
     picked = jnp.sum(onehot * logits, axis=1)
@@ -295,7 +302,9 @@
     feature_all = jnp.stack([jnp.where(same_side, ring, other), jnp.where(same_side, other, ring)])
     fc_grad, fc_squares = fc_product([rows_near, rows_far], feature_all.reshape(tokens, width))
 
-    sums = total(jnp.stack([head_squares + fc_squares, loss_part]))
+    loss_lane = jnp.where(jnp.arange(width) == 0, loss_part, 0.0)[None, :]
+    sums = total(jnp.concatenate([head_squares + fc_squares, loss_lane]))
+    sums = jnp.sum(sums, axis=1)
     entries = 3.0 * D * D + 1.0 * D * VD
     scale = lax.rsqrt(sums[0] / entries + 1e-06)
     fc_step, head_step = scaled(fc_grad, head_grad.reshape(ZH, ZL, width, slab), scale)

time: 331 us -> 327 us (0.988)
  waiting for transfers between devices: 163 us -> 153 us
  starting transfers between devices: 64.3 us -> 71.2 us
    ppermute x3 -> x7, waiting for transfers between devices: 15.7 us -> 6.49 us  [total(): parts.append(lax.ppermute(value, DEPTH, [(i, i ^ by) for i in range(Z)]))]
    ppermute x3 -> x7, starting transfers between devices: 6.85 us -> 12.9 us  [total(): parts.append(lax.ppermute(value, DEPTH, [(i, i ^ by) for i in range(Z)]))]
    all_gather x1, waiting for transfers between devices: 4.46 us -> 8.24 us  [per_device(): head = lax.all_gather(head, 'x', axis=1, tiled=True)]
  transfers between devices with their start and end apart: 37 -> 41, of which waited for: 31 -> 31; matrix products, arithmetic and copies ran while one was open for 11% -> 11% of each run, Pallas kernels for 4% -> 5%
where the time goes in v4:
time: 327 us; the launch traced here: 323 us
  waiting for transfers between devices  153 us (47%)
  starting transfers between devices  71.2 us (22%)
  local copies, waits for them, and re-layouts  21.1 us (6%)
  Pallas kernels  20.1 us (6%)
  blocking collectives  19.4 us (6%)
  between operations  16.3 us (5%)
  matrix products  15.4 us (5%)
  other arithmetic  6.35 us (2%)
    ppermute x18, waiting for transfers between devices, shift(): return lax.ppermute(value, axis, [(i, (i + by) % 4) for i in range(4)])  38.3 us
    ppermute x1, waiting for transfers between devices, per_device(): far = lax.ppermute(flat, 'zh', [(0, 1), (1, 0)])  33.4 us
    all_to_all x1, waiting for transfers between devices, per_device(): head = lax.all_to_all(head, DEPTH, 0, 0).reshape(depth, slab)  27.1 us
    ppermute x18, starting transfers between devices, shift(): return lax.ppermute(value, axis, [(i, (i + by) % 4) for i in range(4)])  24.7 us
    all_to_all x1, blocking collectives, spread(): lax.all_to_all(jnp.broadcast_to(value[None], (count,) + value.shape), axe...  19.4 us
    all_gather x1, waiting for transfers between devices, per_device(): lax.all_gather(shard.reshape(-1, columns), 'x', axis=0, tiled=True)  14.1 us
    ppermute x7, starting transfers between devices, total(): parts.append(lax.ppermute(value, DEPTH, [(i, i ^ by) for i in range(Z)]))  12.9 us
    all_gather x1, waiting for transfers between devices, per_device(): head = lax.all_gather(head, 'x', axis=1, tiled=True)  8.24 us
  transfers between devices with their start and end apart: 41, of which 31 were waited for; matrix products, arithmetic and copies ran while one was open for 11% of the time, Pallas kernels for 5%

profile of v4, /device:TPU:2, one launch (start us, length us, event | category | flops | bytes accessed | tf_op | source)
XLA Modules:
  0.0 323.3 jit_solution(2311444624964461397)
XLA Ops:
  10.1 7.3 %collective-permute-start = (bf16[128,3072]{1,0:T(8,128)(2,1)}, bf16[128,3072]{1,0:T(8,128)(2,1)S(1)}, u32[]{:S(2)}, u32[]{:S(2)}) collective-permute-start(bf16[128,3072]{1,0:T(8,128)(2,1)} %copy.116), channel_id=1, source_target_pairs={{0,4},{4,0},{1,5},{5,1},{2,6},{6,2},{3,7},{7,3},{8,12},{12,8},{9,1... | collective-permute-start | bytes 2359304 | tf_op jit(solution)/shard_map/ppermute | solution.py:203
  17.4 33.4 %collective-permute-done = bf16[128,3072]{1,0:T(8,128)(2,1)S(1)} collective-permute-done((bf16[128,3072]{1,0:T(8,128)(2,1)}, bf16[128,3072]{1,0:T(8,128)(2,1)S(1)}, u32[]{:S(2)}, u32[]{:S(2)}) %collective-permute-start) | collective-permute-done | bytes 786464 | tf_op jit(solution)/shard_map/ppermute | solution.py:203
  54.7 7.7 %all-to-all-start = ((bf16[8,256,256]{2,1,0:T(8,128)(2,1)}), bf16[8,256,256]{2,1,0:T(8,128)(2,1)S(1)}, u32[]{:S(2)}, u32[]{:S(2)}) async-start(bf16[8,256,256]{2,1,0:T(8,128)(2,1)} %bitcast.129), calls=%async_computation | async-start | bytes 2097152 | tf_op jit(solution)/shard_map/all_to_all | solution.py:209
  63.2 27.1 %all-to-all-done = bf16[8,256,256]{2,1,0:T(8,128)(2,1)S(1)} async-done(((bf16[8,256,256]{2,1,0:T(8,128)(2,1)}), bf16[8,256,256]{2,1,0:T(8,128)(2,1)S(1)}, u32[]{:S(2)}, u32[]{:S(2)}) %all-to-all-start) | async-done | bytes 1048608 | tf_op jit(solution)/shard_map/all_to_all | solution.py:209
  91.3 4.8 %all-to-all-start.1 = ((bf16[8,32,256]{2,1,0:T(8,128)(2,1)}), bf16[8,32,256]{2,1,0:T(8,128)(2,1)S(1)}, u32[]{:S(2)}, u32[]{:S(2)}) async-start(bf16[8,32,256]{2,1,0:T(8,128)(2,1)} %bitcast.4), calls=%async_computation.1 | async-start | bytes 262144 | tf_op jit(solution)/shard_map/all_to_all | solution.py:214
  96.1 2.9 fusion.37
  99.0 6.2 %all-to-all-done.1 = bf16[8,32,256]{2,1,0:T(8,128)(2,1)S(1)} async-done(((bf16[8,32,256]{2,1,0:T(8,128)(2,1)}), bf16[8,32,256]{2,1,0:T(8,128)(2,1)S(1)}, u32[]{:S(2)}, u32[]{:S(2)}) %all-to-all-start.1) | async-done | bytes 131104 | tf_op jit(solution)/shard_map/all_to_all | solution.py:214
  105.2 3.7 %broadcast_select_fusion.2 = (f32[512,256]{1,0:T(8,128)}, f32[512,256]{1,0:T(8,128)S(1)}) fusion(f32[512,256]{1,0:T(8,128)S(1)} %fusion.37, pred[]{:T(512)S(6)} %eq.53, bf16[512,3072]{1,0:T(8,128)(2,1)} %all-gather.8.cloned.1.call-done.refs_2_.refs_3_, bf16[3072,256]{1,0:T(8,128)(2,1)S(1)} %bitcast.121), kind=kOutput, calls=%fused_computation.27 | convolution fusion | flops 805437440 | bytes 6291457 | tf_op jit(solution)/shard_map/dot_general | solution.py:221
  116.9 5.1 %collective-permute-done.2 = f32[4,32,256]{2,1,0:T(8,128)S(1)} collective-permute-done((f32[4,32,256]{2,1,0:T(8,128)S(1)}, f32[4,32,256]{2,1,0:T(8,128)S(1)}, u32[]{:S(2)}, u32[]{:S(2)}) %collective-permute-start.2) | collective-permute-done | bytes 131104 | tf_op jit(solution)/shard_map/ppermute | solution.py:24
  122.0 6.3 %collective-permute-done.4 = f32[4,32,256]{2,1,0:T(8,128)S(1)} collective-permute-done((f32[4,32,256]{2,1,0:T(8,128)S(1)}, f32[4,32,256]{2,1,0:T(8,128)S(1)}, u32[]{:S(2)}, u32[]{:S(2)}) %collective-permute-start.4) | collective-permute-done | bytes 131104 | tf_op jit(solution)/shard_map/ppermute | solution.py:24
  128.3 19.4 %all_to_all.40 = bf16[8,128,256]{2,1,0:T(8,128)(2,1)S(1)} all-to-all(bf16[8,128,256]{2,1,0:T(8,128)(2,1)S(1)} %broadcast_in_dim.59), channel_id=1, replica_groups=mesh['x'=4,'core'=2,'y'=4,'zh'=2,'zl'=4] {'zh','zl'}, dimensions={0} | all-to-all | bytes 1048576 | tf_op jit(solution)/shard_map/all_to_all | solution.py:16
  152.0 8.2 %all-gather.10.cloned.1.call-done = bf16[2048,1024]{1,0:T(8,128)(2,1)} async-done(((bf16[2048,256]{1,0:T(8,128)(2,1)}), bf16[2048,1024]{1,0:T(8,128)(2,1)}) %all-gather.10.cloned.1.call-update) | async-done | bytes 4194320 | tf_op jit(solution)/shard_map/all_gather | solution.py:216
  160.2 3.4 %fusion = f32[4,64,1024]{2,1,0:T(8,128)S(1)} fusion(bf16[4,64,2048]{2,1,0:T(8,128)(2,1)S(1)} %bitcast.145, bf16[2048,1024]{1,0:T(8,128)(2,1)} %all-gather.10.cloned.1.call-done), kind=kOutput, calls=%fused_computation.1 | convolution fusion | flops 1073741824 | bytes 6291456 | tf_op jit(solution)/shard_map/dot_general | solution.py:236
  163.8 2.8 collective-permute-start.6
  170.6 3.6 %collective-permute-done.6 = f32[64,1024]{1,0:T(8,128)S(1)} collective-permute-done((f32[64,1024]{1,0:T(8,128)S(1)}, f32[64,1024]{1,0:T(8,128)S(1)}, u32[]{:S(2)}, u32[]{:S(2)}) %collective-permute-start.6) | collective-permute-done | bytes 262176 | tf_op jit(solution)/shard_map/ppermute | solution.py:24
  175.9 4.2 %collective-permute-done.8 = f32[64,1024]{1,0:T(8,128)} collective-permute-done((f32[64,1024]{1,0:T(8,128)S(1)}, f32[64,1024]{1,0:T(8,128)}, u32[]{:S(2)}, u32[]{:S(2)}) %collective-permute-start.8) | collective-permute-done | bytes 262176 | tf_op jit(solution)/shard_map/ppermute | solution.py:24
  182.5 4.9 %all-to-all-start.3 = ((f32[16,1,320]{2,1,0:T(1,128)}), f32[16,1,320]{2,1,0:T(1,128)S(1)}, u32[]{:S(2)}, u32[]{:S(2)}) async-start(f32[16,1,320]{2,1,0:T(1,128)} %reshape.360), calls=%async_computation.3 | async-start | bytes 49152 | tf_op jit(solution)/shard_map/all_to_all | solution.py:16
  187.5 7.5 %all-to-all-done.3 = f32[16,1,320]{2,1,0:T(1,128)S(1)} async-done(((f32[16,1,320]{2,1,0:T(1,128)}), f32[16,1,320]{2,1,0:T(1,128)S(1)}, u32[]{:S(2)}, u32[]{:S(2)}) %all-to-all-start.3) | async-done | bytes 20512 | tf_op jit(solution)/shard_map/all_to_all | solution.py:16
  200.1 3.0 collective-permute-done.9
  208.6 3.9 %fusion.38 = f32[128,2048]{1,0:T(8,128)S(1)} fusion(bf16[128,1024]{1,0:T(8,128)(2,1)S(1)} %bitcast.149, bf16[2048,1024]{1,0:T(8,128)(2,1)} %all-gather.10.cloned.1.call-done), kind=kOutput, calls=%fused_computation.92 | convolution fusion | flops 536870912 | bytes 5505024 | tf_op jit(solution)/shard_map/dot_general | solution.py:283
  212.6 2.6 collective-permute-done.12
  218.4 3.6 %all-to-all-start.4 = ((f32[1,128,8,256]{3,1,0,2:T(8,128)}), f32[1,128,8,256]{3,1,0,2:T(8,128)S(1)}, u32[]{:S(2)}, u32[]{:S(2)}) async-start(f32[1,128,8,256]{3,1,0,2:T(8,128)} %copy.127), calls=%async_computation.4 | async-start | bytes 2097152 | tf_op jit(solution)/shard_map/all_to_all | solution.py:287
  221.9 14.1 %all-gather.14.cloned.1.call-done = bf16[1024,1024]{1,0:T(8,128)(2,1)} async-done(((bf16[256,1024]{1,0:T(8,128)(2,1)}), bf16[1024,1024]{1,0:T(8,128)(2,1)}) %all-gather.14.cloned.1.call-update) | async-done | bytes 2097168 | tf_op jit(solution)/shard_map/all_gather | solution.py:289
  238.0 7.5 %shard_map.103 = (f32[8,256,256]{2,1,0:T(8,128)}, f32[1,256]{1,0:T(1,128)}) custom-call(bf16[1024,2048]{1,0:T(8,128)(2,1)} %all-gather.12.cloned.1.call-done.joined_ref, bf16[1024,256]{1,0:T(8,128)(2,1)} %bitcast.136), custom_call_target="tpu_custom_call" | custom-call | flops 1073741824 | bytes 7340032 | tf_op jit(solution)/shard_map/pallas_call | solution.py:117
  245.5 5.8 %all-to-all-done.4 = f32[1,128,8,256]{3,1,0,2:T(8,128)S(1)} async-done(((f32[1,128,8,256]{3,1,0,2:T(8,128)}), f32[1,128,8,256]{3,1,0,2:T(8,128)S(1)}, u32[]{:S(2)}, u32[]{:S(2)}) %all-to-all-start.4) | async-done | bytes 1048608 | tf_op jit(solution)/shard_map/all_to_all | solution.py:287
  251.3 4.3 %all-to-all-start.5 = ((f32[8,256,256]{2,1,0:T(8,128)}), f32[8,256,256]{2,1,0:T(8,128)}, u32[]{:S(2)}, u32[]{:S(2)}) async-start(f32[8,256,256]{2,1,0:T(8,128)} %get-tuple-element.30), calls=%async_computation.5 | async-start | bytes 4194304 | tf_op jit(solution)/shard_map/all_to_all | solution.py:294
  266.9 7.3 %shard_map.104 = (f32[3072,256]{1,0:T(8,128)}, f32[1,256]{1,0:T(1,128)}) custom-call(bf16[512,3072]{1,0:T(8,128)(2,1)} %all-gather.6.cloned.1.call-done.refs_0_.refs_1_, bf16[512,3072]{1,0:T(8,128)(2,1)} %all-gather.6.cloned.1.call-done.refs_0_.refs_1_, bf16[512,3072]{1,0:T(8,128)(2,1)} %all-gather.8.cloned.1.call-done.refs_2_.refs_3_, ...), custom_call_target="tpu_custom_call" | custom-call | flops 1610612736 | bytes 10485760 | tf_op jit(solution)/shard_map/pallas_call | solution.py:73
  284.7 2.4 collective-permute-start.22
  292.5 2.4 collective-permute-start.25
  295.0 5.8 %collective-permute-start.27 = (f32[2,256]{1,0:T(2,128)S(1)}, f32[2,256]{1,0:T(2,128)S(1)}, u32[]{:S(2)}, u32[]{:S(2)}) collective-permute-start(f32[2,256]{1,0:T(2,128)S(1)} %add_add_fusion), channel_id=1, source_target_pairs={{0,4},{1,5},{2,6},{3,7},{4,0},{5,1},{6,2},{7,3},{8,12},{9,13},{10,... | collective-permute-start | bytes 6152 | tf_op jit(solution)/shard_map/ppermute | solution.py:182
  300.8 2.6 collective-permute-done.24
  311.5 5.3 %shard_map.105 = (f32[3072,256]{1,0:T(8,128)}, f32[256,2048]{1,0:T(8,128)}) custom-call(f32[1,1]{1,0:T(1,128)} %bitcast.57.scale_ref, f32[3072,256]{1,0:T(8,128)} %get-tuple-element.29.fc_ref, f32[2,4,256,256]{3,2,1,0:T(8,128)} %bitcast.58.head_ref), custom_call_target="tpu_custom_call" | custom-call | flops 1310720 | bytes 10485760 | tf_op jit(solution)/shard_map/pallas_call | solution.py:151
  (170 shorter events, 77.9 us)
Async XLA Ops:
  7.2 88.9 %all-gather.6.cloned.1.call-start = ((), (), s32[]{:S(2)}) async-start(), calls=%async_computation.6 | async-start | bytes 3932160 | tf_op jit(solution)/shard_map/all_gather | solution.py:204
  10.0 95.2 %all-gather.8.cloned.1.call-start = ((), (), s32[]{:S(2)}) async-start(), calls=%async_computation.7 | async-start | bytes 3932160 | tf_op jit(solution)/shard_map/all_gather | solution.py:205
  10.1 40.7 %collective-permute-start = (bf16[128,3072]{1,0:T(8,128)(2,1)}, bf16[128,3072]{1,0:T(8,128)(2,1)S(1)}, u32[]{:S(2)}, u32[]{:S(2)}) collective-permute-start(bf16[128,3072]{1,0:T(8,128)(2,1)} %copy.116), channel_id=1, source_target_pairs={{0,4},{4,0},{1,5},{5,1},{2,6},{6,2},{3,7},{7,3},{8,12},{12,8},{9,1... | collective-permute-start | bytes 2359304 | tf_op jit(solution)/shard_map/ppermute | solution.py:203
  54.7 35.6 %all-to-all-start = ((bf16[8,256,256]{2,1,0:T(8,128)(2,1)}), bf16[8,256,256]{2,1,0:T(8,128)(2,1)S(1)}, u32[]{:S(2)}, u32[]{:S(2)}) async-start(bf16[8,256,256]{2,1,0:T(8,128)(2,1)} %bitcast.129), calls=%async_computation | async-start | bytes 2097152 | tf_op jit(solution)/shard_map/all_to_all | solution.py:209
  62.4 97.8 %all-gather.10.cloned.1.call-start = ((), (), s32[]{:S(2)}) async-start(), calls=%async_computation.8 | async-start | bytes 5242880 | tf_op jit(solution)/shard_map/all_gather | solution.py:216
  91.3 13.9 %all-to-all-start.1 = ((bf16[8,32,256]{2,1,0:T(8,128)(2,1)}), bf16[8,32,256]{2,1,0:T(8,128)(2,1)S(1)}, u32[]{:S(2)}, u32[]{:S(2)}) async-start(bf16[8,32,256]{2,1,0:T(8,128)(2,1)} %bitcast.4), calls=%async_computation.1 | async-start | bytes 262144 | tf_op jit(solution)/shard_map/all_to_all | solution.py:214
  96.1 110.4 %all-gather.12.cloned.1.call-start = ((), (), s32[]{:S(2)}) async-start(), calls=%async_computation.9 | async-start | bytes 4718592 | tf_op jit(solution)/shard_map/all_gather | solution.py:231
  113.0 8.9 %collective-permute-start.2 = (f32[4,32,256]{2,1,0:T(8,128)S(1)}, f32[4,32,256]{2,1,0:T(8,128)S(1)}, u32[]{:S(2)}, u32[]{:S(2)}) collective-permute-start(f32[4,32,256]{2,1,0:T(8,128)S(1)} %get-tuple-element.54), channel_id=1, source_target_pairs={{0,64},{64,128},{128,192},{192,0},{1,65},{65,129},{129,193},{193,1... | collective-permute-start | bytes 393224 | tf_op jit(solution)/shard_map/ppermute | solution.py:24
  113.8 8.1 %collective-permute-start.3 = (f32[4,32,256]{2,1,0:T(8,128)S(1)}, f32[4,32,256]{2,1,0:T(8,128)S(1)}, u32[]{:S(2)}, u32[]{:S(2)}) collective-permute-start(f32[4,32,256]{2,1,0:T(8,128)S(1)} %get-tuple-element.56), channel_id=1, source_target_pairs={{0,192},{64,0},{128,64},{192,128},{1,193},{65,1},{129,65},{193,129... | collective-permute-start | bytes 393224 | tf_op jit(solution)/shard_map/ppermute | solution.py:24
  115.1 13.1 %collective-permute-start.4 = (f32[4,32,256]{2,1,0:T(8,128)S(1)}, f32[4,32,256]{2,1,0:T(8,128)S(1)}, u32[]{:S(2)}, u32[]{:S(2)}) collective-permute-start(f32[4,32,256]{2,1,0:T(8,128)S(1)} %get-tuple-element.55), channel_id=1, source_target_pairs={{0,128},{64,192},{128,0},{192,64},{1,129},{65,193},{129,1},{193,65... | collective-permute-start | bytes 393224 | tf_op jit(solution)/shard_map/ppermute | solution.py:24
  163.8 10.4 %collective-permute-start.6 = (f32[64,1024]{1,0:T(8,128)S(1)}, f32[64,1024]{1,0:T(8,128)S(1)}, u32[]{:S(2)}, u32[]{:S(2)}) collective-permute-start(f32[64,1024]{1,0:T(8,128)S(1)} %get-tuple-element.45), channel_id=1, source_target_pairs={{0,8},{8,16},{16,24},{24,0},{1,9},{9,17},{17,25},{25,1},{2,10},{10... | collective-permute-start | bytes 786440 | tf_op jit(solution)/shard_map/ppermute | solution.py:24
  166.6 9.4 %collective-permute-start.7 = (f32[64,1024]{1,0:T(8,128)S(1)}, f32[64,1024]{1,0:T(8,128)}, u32[]{:S(2)}, u32[]{:S(2)}) collective-permute-start(f32[64,1024]{1,0:T(8,128)S(1)} %get-tuple-element.47), channel_id=1, source_target_pairs={{0,24},{8,0},{16,8},{24,16},{1,25},{9,1},{17,9},{25,17},{2,26},{10... | collective-permute-start | bytes 786440 | tf_op jit(solution)/shard_map/ppermute | solution.py:24
  167.9 12.2 %collective-permute-start.8 = (f32[64,1024]{1,0:T(8,128)S(1)}, f32[64,1024]{1,0:T(8,128)}, u32[]{:S(2)}, u32[]{:S(2)}) collective-permute-start(f32[64,1024]{1,0:T(8,128)S(1)} %get-tuple-element.46), channel_id=1, source_target_pairs={{0,16},{8,24},{16,0},{24,8},{1,17},{9,25},{17,1},{25,9},{2,18},{10... | collective-permute-start | bytes 786440 | tf_op jit(solution)/shard_map/ppermute | solution.py:24
  182.5 12.6 %all-to-all-start.3 = ((f32[16,1,320]{2,1,0:T(1,128)}), f32[16,1,320]{2,1,0:T(1,128)S(1)}, u32[]{:S(2)}, u32[]{:S(2)}) async-start(f32[16,1,320]{2,1,0:T(1,128)} %reshape.360), calls=%async_computation.3 | async-start | bytes 49152 | tf_op jit(solution)/shard_map/all_to_all | solution.py:16
  187.4 48.7 %all-gather.14.cloned.1.call-start = ((), (), s32[]{:S(2)}) async-start(), calls=%async_computation.10 | async-start | bytes 2621440 | tf_op jit(solution)/shard_map/all_gather | solution.py:289
  196.7 6.5 %collective-permute-start.9 = (bf16[64,1024]{1,0:T(8,128)(2,1)S(1)}, bf16[64,1024]{1,0:T(8,128)(2,1)S(1)}, u32[]{:S(2)}, u32[]{:S(2)}) collective-permute-start(bf16[64,1024]{1,0:T(8,128)(2,1)S(1)} %get-tuple-element.40), channel_id=1, source_target_pairs={{0,8},{8,16},{16,24},{24,0},{1,9},{9,17},{17,25},{25,1},{2,10},{10... | collective-permute-start | bytes 393224 | tf_op jit(solution)/shard_map/ppermute | solution.py:24
  197.9 7.3 %collective-permute-start.10 = (bf16[64,1024]{1,0:T(8,128)(2,1)S(1)}, bf16[64,1024]{1,0:T(8,128)(2,1)S(1)}, u32[]{:S(2)}, u32[]{:S(2)}) collective-permute-start(bf16[64,1024]{1,0:T(8,128)(2,1)S(1)} %get-tuple-element.40), channel_id=1, source_target_pairs={{0,24},{8,0},{16,8},{24,16},{1,25},{9,1},{17,9},{25,17},{2,26},{10... | collective-permute-start | bytes 393224 | tf_op jit(solution)/shard_map/ppermute | solution.py:24
  200.0 6.5 %collective-permute-start.11 = (bf16[64,1024]{1,0:T(8,128)(2,1)S(1)}, bf16[64,1024]{1,0:T(8,128)(2,1)S(1)}, u32[]{:S(2)}, u32[]{:S(2)}) collective-permute-start(bf16[64,1024]{1,0:T(8,128)(2,1)S(1)} %get-tuple-element.40), channel_id=1, source_target_pairs={{0,16},{8,24},{16,0},{24,8},{1,17},{9,25},{17,1},{25,9},{2,18},{10... | collective-permute-start | bytes 393224 | tf_op jit(solution)/shard_map/ppermute | solution.py:24
  218.4 32.9 %all-to-all-start.4 = ((f32[1,128,8,256]{3,1,0,2:T(8,128)}), f32[1,128,8,256]{3,1,0,2:T(8,128)S(1)}, u32[]{:S(2)}, u32[]{:S(2)}) async-start(f32[1,128,8,256]{3,1,0,2:T(8,128)} %copy.127), calls=%async_computation.4 | async-start | bytes 2097152 | tf_op jit(solution)/shard_map/all_to_all | solution.py:287
  251.3 60.2 %all-to-all-start.5 = ((f32[8,256,256]{2,1,0:T(8,128)}), f32[8,256,256]{2,1,0:T(8,128)}, u32[]{:S(2)}, u32[]{:S(2)}) async-start(f32[8,256,256]{2,1,0:T(8,128)} %get-tuple-element.30), calls=%async_computation.5 | async-start | bytes 4194304 | tf_op jit(solution)/shard_map/all_to_all | solution.py:294
  255.7 4.3 %collective-permute-start.13 = (bf16[128,256]{1,0:T(8,128)(2,1)S(1)}, bf16[128,256]{1,0:T(8,128)(2,1)S(1)}, u32[]{:S(2)}, u32[]{:S(2)}) collective-permute-start(bf16[128,256]{1,0:T(8,128)(2,1)S(1)} %reduce_sum.96), channel_id=1, source_target_pairs={{0,64},{64,128},{128,192},{192,0},{1,65},{65,129},{129,193},{193,1... | collective-permute-start | bytes 196616 | tf_op jit(solution)/shard_map/ppermute | solution.py:24
  257.8 5.8 %collective-permute-start.15 = (bf16[128,256]{1,0:T(8,128)(2,1)S(1)}, bf16[128,256]{1,0:T(8,128)(2,1)S(1)}, u32[]{:S(2)}, u32[]{:S(2)}) collective-permute-start(bf16[128,256]{1,0:T(8,128)(2,1)S(1)} %reduce_sum.96), channel_id=1, source_target_pairs={{0,128},{64,192},{128,0},{192,64},{1,129},{65,193},{129,1},{193,65... | collective-permute-start | bytes 196616 | tf_op jit(solution)/shard_map/ppermute | solution.py:24
  276.3 5.4 %collective-permute-start.18 = (f32[2,256]{1,0:T(2,128)S(1)}, f32[2,256]{1,0:T(2,128)S(1)}, u32[]{:S(2)}, u32[]{:S(2)}) collective-permute-start(f32[2,256]{1,0:T(2,128)S(1)} %fusion.29), channel_id=1, source_target_pairs={{0,128},{64,192},{128,0},{192,64},{1,129},{65,193},{129,1},{193,65... | collective-permute-start | bytes 6152 | tf_op jit(solution)/shard_map/ppermute | solution.py:24
  283.6 5.2 %collective-permute-start.21 = (f32[2,256]{1,0:T(2,128)S(1)}, f32[2,256]{1,0:T(2,128)S(1)}, u32[]{:S(2)}, u32[]{:S(2)}) collective-permute-start(f32[2,256]{1,0:T(2,128)S(1)} %add_add_fusion.1), channel_id=1, source_target_pairs={{0,16},{8,24},{16,0},{24,8},{1,17},{9,25},{17,1},{25,9},{2,18},{10... | collective-permute-start | bytes 6152 | tf_op jit(solution)/shard_map/ppermute | solution.py:24
  284.7 4.8 %collective-permute-start.22 = (f32[2,256]{1,0:T(2,128)S(1)}, f32[2,256]{1,0:T(2,128)S(1)}, u32[]{:S(2)}, u32[]{:S(2)}) collective-permute-start(f32[2,256]{1,0:T(2,128)S(1)} %add_add_fusion.1), channel_id=1, source_target_pairs={{0,8},{8,16},{16,24},{24,0},{1,9},{9,17},{17,25},{25,1},{2,10},{10... | collective-permute-start | bytes 6152 | tf_op jit(solution)/shard_map/ppermute | solution.py:24
  290.7 12.8 %collective-permute-start.24 = (f32[2,256]{1,0:T(2,128)S(1)}, f32[2,256]{1,0:T(2,128)S(1)}, u32[]{:S(2)}, u32[]{:S(2)}) collective-permute-start(f32[2,256]{1,0:T(2,128)S(1)} %add_add_fusion), channel_id=1, source_target_pairs={{0,1},{1,0},{2,3},{3,2},{4,5},{5,4},{6,7},{7,6},{8,9},{9,8},{10,11... | collective-permute-start | bytes 6152 | tf_op jit(solution)/shard_map/ppermute | solution.py:182
  292.5 12.8 %collective-permute-start.25 = (f32[2,256]{1,0:T(2,128)S(1)}, f32[2,256]{1,0:T(2,128)S(1)}, u32[]{:S(2)}, u32[]{:S(2)}) collective-permute-start(f32[2,256]{1,0:T(2,128)S(1)} %add_add_fusion), channel_id=1, source_target_pairs={{0,2},{1,3},{2,0},{3,1},{4,6},{5,7},{6,4},{7,5},{8,10},{9,11},{10,... | collective-permute-start | bytes 6152 | tf_op jit(solution)/shard_map/ppermute | solution.py:182
  294.9 11.3 %collective-permute-start.26 = (f32[2,256]{1,0:T(2,128)S(1)}, f32[2,256]{1,0:T(2,128)S(1)}, u32[]{:S(2)}, u32[]{:S(2)}) collective-permute-start(f32[2,256]{1,0:T(2,128)S(1)} %add_add_fusion), channel_id=1, source_target_pairs={{0,3},{1,2},{2,1},{3,0},{4,7},{5,6},{6,5},{7,4},{8,11},{9,10},{10,... | collective-permute-start | bytes 6152 | tf_op jit(solution)/shard_map/ppermute | solution.py:182
  295.0 12.5 %collective-permute-start.27 = (f32[2,256]{1,0:T(2,128)S(1)}, f32[2,256]{1,0:T(2,128)S(1)}, u32[]{:S(2)}, u32[]{:S(2)}) collective-permute-start(f32[2,256]{1,0:T(2,128)S(1)} %add_add_fusion), channel_id=1, source_target_pairs={{0,4},{1,5},{2,6},{3,7},{4,0},{5,1},{6,2},{7,3},{8,12},{9,13},{10,... | collective-permute-start | bytes 6152 | tf_op jit(solution)/shard_map/ppermute | solution.py:182
  300.8 6.7 %collective-permute-start.28 = (f32[2,256]{1,0:T(2,128)S(1)}, f32[2,256]{1,0:T(2,128)S(1)}, u32[]{:S(2)}, u32[]{:S(2)}) collective-permute-start(f32[2,256]{1,0:T(2,128)S(1)} %add_add_fusion), channel_id=1, source_target_pairs={{0,5},{1,4},{2,7},{3,6},{4,1},{5,0},{6,3},{7,2},{8,13},{9,12},{10,... | collective-permute-start | bytes 6152 | tf_op jit(solution)/shard_map/ppermute | solution.py:182
  303.5 5.7 %collective-permute-start.29 = (f32[2,256]{1,0:T(2,128)S(1)}, f32[2,256]{1,0:T(2,128)S(1)}, u32[]{:S(2)}, u32[]{:S(2)}) collective-permute-start(f32[2,256]{1,0:T(2,128)S(1)} %add_add_fusion), channel_id=1, source_target_pairs={{0,6},{1,7},{2,4},{3,5},{4,2},{5,3},{6,0},{7,1},{8,14},{9,15},{10,... | collective-permute-start | bytes 6152 | tf_op jit(solution)/shard_map/ppermute | solution.py:182
  305.3 4.8 %collective-permute-start.30 = (f32[2,256]{1,0:T(2,128)S(1)}, f32[2,256]{1,0:T(2,128)S(1)}, u32[]{:S(2)}, u32[]{:S(2)}) collective-permute-start(f32[2,256]{1,0:T(2,128)S(1)} %add_add_fusion), channel_id=1, source_target_pairs={{0,7},{1,6},{2,5},{3,4},{4,3},{5,2},{6,1},{7,0},{8,15},{9,14},{10,... | collective-permute-start | bytes 6152 | tf_op jit(solution)/shard_map/ppermute | solution.py:182
  (22 other events, 299.1 us)
Sparse Core Ops, SparseCore 0:
  10.4 45.0 all-gather.5
  57.3 42.3 all-gather.7
  102.0 58.1 all-gather.9
  162.5 33.4 all-gather.11
  207.4 28.5 all-gather.13

commit v5 on v4

--- a/solution.py
+++ b/solution.py
@@ -177,12 +177,9 @@
     value = value + swap(value)
     for axis in ("x", "y"):
         value = (value + shift(value, axis, 2)) + (shift(value, axis, 1) + shift(value, axis, -1))
-    parts = [value]
-    for by in range(1, Z):
-        parts.append(lax.ppermute(value, DEPTH, [(i, i ^ by) for i in range(Z)]))
-    while len(parts) > 1:
-        parts = [first + second for first, second in zip(parts[::2], parts[1::2])]
-    return parts[0]
+    at = [lax.ppermute(value, DEPTH, [(i, i ^ by) for i in range(Z)]) for by in (1, 2, 3)]
+    value = (value + at[0]) + (at[1] + at[2])
+    return value + lax.ppermute(value, DEPTH, [(i, i ^ ZL) for i in range(Z)])
 
 
 def per_device(

time: 327 us -> 325 us (level)
  waiting for transfers between devices: 153 us -> 158 us
  starting transfers between devices: 71.2 us -> 67.2 us
    ppermute x7 -> x4, waiting for transfers between devices: 6.49 us -> 11.3 us  [the longest x3 8.3 us: total(): lax.ppermute(value, DEPTH, [(i, i ^ by) for i in range(Z)])]
    ppermute x7 -> x4, starting transfers between devices: 12.9 us -> 8.97 us  [the longest x1 4.59 us: total(): return value + lax.ppermute(value, DEPTH, [(i, i ^ ZL) for i in range(Z)])]
  transfers between devices with their start and end apart: 41 -> 38, of which waited for: 31 -> 29; matrix products, arithmetic and copies ran while one was open for 11% -> 11% of each run, Pallas kernels for 5% -> 5%
where the time goes in v5:
time: 325 us; the launch traced here: 324 us
  waiting for transfers between devices  158 us (49%)
  starting transfers between devices  67.2 us (21%)
  local copies, waits for them, and re-layouts  21.1 us (6%)
  Pallas kernels  20.1 us (6%)
  blocking collectives  19.4 us (6%)
  between operations  16.3 us (5%)
  matrix products  15.4 us (5%)
  other arithmetic  6.38 us (2%)
    ppermute x18, waiting for transfers between devices, shift(): return lax.ppermute(value, axis, [(i, (i + by) % 4) for i in range(4)])  38.3 us
    ppermute x1, waiting for transfers between devices, per_device(): far = lax.ppermute(flat, 'zh', [(0, 1), (1, 0)])  33.4 us
    all_to_all x1, waiting for transfers between devices, per_device(): head = lax.all_to_all(head, DEPTH, 0, 0).reshape(depth, slab)  27.1 us
    ppermute x18, starting transfers between devices, shift(): return lax.ppermute(value, axis, [(i, (i + by) % 4) for i in range(4)])  24.7 us
    all_to_all x1, blocking collectives, spread(): lax.all_to_all(jnp.broadcast_to(value[None], (count,) + value.shape), axe...  19.4 us
    all_gather x1, waiting for transfers between devices, per_device(): lax.all_gather(shard.reshape(-1, columns), 'x', axis=0, tiled=True)  14.1 us
    ppermute x3, waiting for transfers between devices, total(): lax.ppermute(value, DEPTH, [(i, i ^ by) for i in range(Z)])  8.3 us
    all_gather x1, waiting for transfers between devices, per_device(): head = lax.all_gather(head, 'x', axis=1, tiled=True)  8.25 us
  transfers between devices with their start and end apart: 38, of which 29 were waited for; matrix products, arithmetic and copies ran while one was open for 11% of the time, Pallas kernels for 5%

profile of v5, /device:TPU:2, one launch (start us, length us, event | category | flops | bytes accessed | tf_op | source)
XLA Modules:
  0.0 324.2 jit_solution(2526026498646105386)
XLA Ops:
  10.1 7.3 %collective-permute-start = (bf16[128,3072]{1,0:T(8,128)(2,1)}, bf16[128,3072]{1,0:T(8,128)(2,1)S(1)}, u32[]{:S(2)}, u32[]{:S(2)}) collective-permute-start(bf16[128,3072]{1,0:T(8,128)(2,1)} %copy.116), channel_id=1, source_target_pairs={{0,4},{4,0},{1,5},{5,1},{2,6},{6,2},{3,7},{7,3},{8,12},{12,8},{9,1... | collective-permute-start | bytes 2359304 | tf_op jit(solution)/shard_map/ppermute | solution.py:200
  17.4 33.4 %collective-permute-done = bf16[128,3072]{1,0:T(8,128)(2,1)S(1)} collective-permute-done((bf16[128,3072]{1,0:T(8,128)(2,1)}, bf16[128,3072]{1,0:T(8,128)(2,1)S(1)}, u32[]{:S(2)}, u32[]{:S(2)}) %collective-permute-start) | collective-permute-done | bytes 786464 | tf_op jit(solution)/shard_map/ppermute | solution.py:200
  54.7 7.7 %all-to-all-start = ((bf16[8,256,256]{2,1,0:T(8,128)(2,1)}), bf16[8,256,256]{2,1,0:T(8,128)(2,1)S(1)}, u32[]{:S(2)}, u32[]{:S(2)}) async-start(bf16[8,256,256]{2,1,0:T(8,128)(2,1)} %bitcast.129), calls=%async_computation | async-start | bytes 2097152 | tf_op jit(solution)/shard_map/all_to_all | solution.py:206
  63.2 27.1 %all-to-all-done = bf16[8,256,256]{2,1,0:T(8,128)(2,1)S(1)} async-done(((bf16[8,256,256]{2,1,0:T(8,128)(2,1)}), bf16[8,256,256]{2,1,0:T(8,128)(2,1)S(1)}, u32[]{:S(2)}, u32[]{:S(2)}) %all-to-all-start) | async-done | bytes 1048608 | tf_op jit(solution)/shard_map/all_to_all | solution.py:206
  91.3 4.8 %all-to-all-start.1 = ((bf16[8,32,256]{2,1,0:T(8,128)(2,1)}), bf16[8,32,256]{2,1,0:T(8,128)(2,1)S(1)}, u32[]{:S(2)}, u32[]{:S(2)}) async-start(bf16[8,32,256]{2,1,0:T(8,128)(2,1)} %bitcast.4), calls=%async_computation.1 | async-start | bytes 262144 | tf_op jit(solution)/shard_map/all_to_all | solution.py:211
  96.1 2.9 fusion.37
  99.0 6.2 %all-to-all-done.1 = bf16[8,32,256]{2,1,0:T(8,128)(2,1)S(1)} async-done(((bf16[8,32,256]{2,1,0:T(8,128)(2,1)}), bf16[8,32,256]{2,1,0:T(8,128)(2,1)S(1)}, u32[]{:S(2)}, u32[]{:S(2)}) %all-to-all-start.1) | async-done | bytes 131104 | tf_op jit(solution)/shard_map/all_to_all | solution.py:211
  105.2 3.7 %broadcast_select_fusion.2 = (f32[512,256]{1,0:T(8,128)}, f32[512,256]{1,0:T(8,128)S(1)}) fusion(f32[512,256]{1,0:T(8,128)S(1)} %fusion.37, pred[]{:T(512)S(6)} %eq.53, bf16[512,3072]{1,0:T(8,128)(2,1)} %all-gather.8.cloned.1.call-done.refs_2_.refs_3_, bf16[3072,256]{1,0:T(8,128)(2,1)S(1)} %bitcast.121), kind=kOutput, calls=%fused_computation.27 | convolution fusion | flops 805437440 | bytes 6291457 | tf_op jit(solution)/shard_map/dot_general | solution.py:218
  116.9 5.1 %collective-permute-done.2 = f32[4,32,256]{2,1,0:T(8,128)S(1)} collective-permute-done((f32[4,32,256]{2,1,0:T(8,128)S(1)}, f32[4,32,256]{2,1,0:T(8,128)S(1)}, u32[]{:S(2)}, u32[]{:S(2)}) %collective-permute-start.2) | collective-permute-done | bytes 131104 | tf_op jit(solution)/shard_map/ppermute | solution.py:24
  122.0 6.3 %collective-permute-done.4 = f32[4,32,256]{2,1,0:T(8,128)S(1)} collective-permute-done((f32[4,32,256]{2,1,0:T(8,128)S(1)}, f32[4,32,256]{2,1,0:T(8,128)S(1)}, u32[]{:S(2)}, u32[]{:S(2)}) %collective-permute-start.4) | collective-permute-done | bytes 131104 | tf_op jit(solution)/shard_map/ppermute | solution.py:24
  128.3 19.4 %all_to_all.40 = bf16[8,128,256]{2,1,0:T(8,128)(2,1)S(1)} all-to-all(bf16[8,128,256]{2,1,0:T(8,128)(2,1)S(1)} %broadcast_in_dim.59), channel_id=1, replica_groups=mesh['x'=4,'core'=2,'y'=4,'zh'=2,'zl'=4] {'zh','zl'}, dimensions={0} | all-to-all | bytes 1048576 | tf_op jit(solution)/shard_map/all_to_all | solution.py:16
  152.0 8.2 %all-gather.10.cloned.1.call-done = bf16[2048,1024]{1,0:T(8,128)(2,1)} async-done(((bf16[2048,256]{1,0:T(8,128)(2,1)}), bf16[2048,1024]{1,0:T(8,128)(2,1)}) %all-gather.10.cloned.1.call-update) | async-done | bytes 4194320 | tf_op jit(solution)/shard_map/all_gather | solution.py:213
  160.3 3.4 %fusion = f32[4,64,1024]{2,1,0:T(8,128)S(1)} fusion(bf16[4,64,2048]{2,1,0:T(8,128)(2,1)S(1)} %bitcast.145, bf16[2048,1024]{1,0:T(8,128)(2,1)} %all-gather.10.cloned.1.call-done), kind=kOutput, calls=%fused_computation.1 | convolution fusion | flops 1073741824 | bytes 6291456 | tf_op jit(solution)/shard_map/dot_general | solution.py:233
  163.8 2.8 collective-permute-start.6
  170.6 3.6 %collective-permute-done.6 = f32[64,1024]{1,0:T(8,128)S(1)} collective-permute-done((f32[64,1024]{1,0:T(8,128)S(1)}, f32[64,1024]{1,0:T(8,128)S(1)}, u32[]{:S(2)}, u32[]{:S(2)}) %collective-permute-start.6) | collective-permute-done | bytes 262176 | tf_op jit(solution)/shard_map/ppermute | solution.py:24
  175.9 4.2 %collective-permute-done.8 = f32[64,1024]{1,0:T(8,128)} collective-permute-done((f32[64,1024]{1,0:T(8,128)S(1)}, f32[64,1024]{1,0:T(8,128)}, u32[]{:S(2)}, u32[]{:S(2)}) %collective-permute-start.8) | collective-permute-done | bytes 262176 | tf_op jit(solution)/shard_map/ppermute | solution.py:24
  182.5 4.9 %all-to-all-start.3 = ((f32[16,1,320]{2,1,0:T(1,128)}), f32[16,1,320]{2,1,0:T(1,128)S(1)}, u32[]{:S(2)}, u32[]{:S(2)}) async-start(f32[16,1,320]{2,1,0:T(1,128)} %reshape.360), calls=%async_computation.3 | async-start | bytes 49152 | tf_op jit(solution)/shard_map/all_to_all | solution.py:16
  187.5 7.5 %all-to-all-done.3 = f32[16,1,320]{2,1,0:T(1,128)S(1)} async-done(((f32[16,1,320]{2,1,0:T(1,128)}), f32[16,1,320]{2,1,0:T(1,128)S(1)}, u32[]{:S(2)}, u32[]{:S(2)}) %all-to-all-start.3) | async-done | bytes 20512 | tf_op jit(solution)/shard_map/all_to_all | solution.py:16
  200.1 3.0 collective-permute-done.9
  208.6 3.9 %fusion.38 = f32[128,2048]{1,0:T(8,128)S(1)} fusion(bf16[128,1024]{1,0:T(8,128)(2,1)S(1)} %bitcast.149, bf16[2048,1024]{1,0:T(8,128)(2,1)} %all-gather.10.cloned.1.call-done), kind=kOutput, calls=%fused_computation.93 | convolution fusion | flops 536870912 | bytes 5505024 | tf_op jit(solution)/shard_map/dot_general | solution.py:280
  212.6 2.6 collective-permute-done.12
  218.4 3.6 %all-to-all-start.4 = ((f32[1,128,8,256]{3,1,0,2:T(8,128)}), f32[1,128,8,256]{3,1,0,2:T(8,128)S(1)}, u32[]{:S(2)}, u32[]{:S(2)}) async-start(f32[1,128,8,256]{3,1,0,2:T(8,128)} %copy.127), calls=%async_computation.4 | async-start | bytes 2097152 | tf_op jit(solution)/shard_map/all_to_all | solution.py:284
  222.0 14.1 %all-gather.14.cloned.1.call-done = bf16[1024,1024]{1,0:T(8,128)(2,1)} async-done(((bf16[256,1024]{1,0:T(8,128)(2,1)}), bf16[1024,1024]{1,0:T(8,128)(2,1)}) %all-gather.14.cloned.1.call-update) | async-done | bytes 2097168 | tf_op jit(solution)/shard_map/all_gather | solution.py:286
  238.0 7.5 %shard_map.103 = (f32[8,256,256]{2,1,0:T(8,128)}, f32[1,256]{1,0:T(1,128)}) custom-call(bf16[1024,2048]{1,0:T(8,128)(2,1)} %all-gather.12.cloned.1.call-done.joined_ref, bf16[1024,256]{1,0:T(8,128)(2,1)} %bitcast.136), custom_call_target="tpu_custom_call" | custom-call | flops 1073741824 | bytes 7340032 | tf_op jit(solution)/shard_map/pallas_call | solution.py:117
  245.4 5.8 %all-to-all-done.4 = f32[1,128,8,256]{3,1,0,2:T(8,128)S(1)} async-done(((f32[1,128,8,256]{3,1,0,2:T(8,128)}), f32[1,128,8,256]{3,1,0,2:T(8,128)S(1)}, u32[]{:S(2)}, u32[]{:S(2)}) %all-to-all-start.4) | async-done | bytes 1048608 | tf_op jit(solution)/shard_map/all_to_all | solution.py:284
  251.3 4.3 %all-to-all-start.5 = ((f32[8,256,256]{2,1,0:T(8,128)}), f32[8,256,256]{2,1,0:T(8,128)}, u32[]{:S(2)}, u32[]{:S(2)}) async-start(f32[8,256,256]{2,1,0:T(8,128)} %get-tuple-element.30), calls=%async_computation.5 | async-start | bytes 4194304 | tf_op jit(solution)/shard_map/all_to_all | solution.py:291
  266.9 7.3 %shard_map.104 = (f32[3072,256]{1,0:T(8,128)}, f32[1,256]{1,0:T(1,128)}) custom-call(bf16[512,3072]{1,0:T(8,128)(2,1)} %all-gather.6.cloned.1.call-done.refs_0_.refs_1_, bf16[512,3072]{1,0:T(8,128)(2,1)} %all-gather.6.cloned.1.call-done.refs_0_.refs_1_, bf16[512,3072]{1,0:T(8,128)(2,1)} %all-gather.8.cloned.1.call-done.refs_2_.refs_3_, ...), custom_call_target="tpu_custom_call" | custom-call | flops 1610612736 | bytes 10485760 | tf_op jit(solution)/shard_map/pallas_call | solution.py:73
  284.7 2.4 collective-permute-start.22
  295.1 8.3 %collective-permute-done.24 = f32[2,256]{1,0:T(2,128)S(1)} collective-permute-done((f32[2,256]{1,0:T(2,128)S(1)}, f32[2,256]{1,0:T(2,128)S(1)}, u32[]{:S(2)}, u32[]{:S(2)}) %collective-permute-start.24) | collective-permute-done | bytes 2080 | tf_op jit(solution)/shard_map/ppermute | solution.py:180
  303.4 4.6 %collective-permute-start.27 = (f32[2,256]{1,0:T(2,128)S(1)}, f32[2,256]{1,0:T(2,128)S(1)}, u32[]{:S(2)}, u32[]{:S(2)}) collective-permute-start(f32[2,256]{1,0:T(2,128)S(1)} %add_add_fusion), channel_id=1, source_target_pairs={{0,4},{1,5},{2,6},{3,7},{4,0},{5,1},{6,2},{7,3},{8,12},{9,13},{10,... | collective-permute-start | bytes 6152 | tf_op jit(solution)/shard_map/ppermute | solution.py:182
  308.0 3.0 collective-permute-done.27
  312.4 5.3 %shard_map.105 = (f32[3072,256]{1,0:T(8,128)}, f32[256,2048]{1,0:T(8,128)}) custom-call(f32[1,1]{1,0:T(1,128)} %bitcast.57.scale_ref, f32[3072,256]{1,0:T(8,128)} %get-tuple-element.29.fc_ref, f32[2,4,256,256]{3,2,1,0:T(8,128)} %bitcast.58.head_ref), custom_call_target="tpu_custom_call" | custom-call | flops 1310720 | bytes 10485760 | tf_op jit(solution)/shard_map/pallas_call | solution.py:151
  (165 shorter events, 73.7 us)
Async XLA Ops:
  7.2 89.0 %all-gather.6.cloned.1.call-start = ((), (), s32[]{:S(2)}) async-start(), calls=%async_computation.6 | async-start | bytes 3932160 | tf_op jit(solution)/shard_map/all_gather | solution.py:201
  10.0 95.2 %all-gather.8.cloned.1.call-start = ((), (), s32[]{:S(2)}) async-start(), calls=%async_computation.7 | async-start | bytes 3932160 | tf_op jit(solution)/shard_map/all_gather | solution.py:202
  10.1 40.7 %collective-permute-start = (bf16[128,3072]{1,0:T(8,128)(2,1)}, bf16[128,3072]{1,0:T(8,128)(2,1)S(1)}, u32[]{:S(2)}, u32[]{:S(2)}) collective-permute-start(bf16[128,3072]{1,0:T(8,128)(2,1)} %copy.116), channel_id=1, source_target_pairs={{0,4},{4,0},{1,5},{5,1},{2,6},{6,2},{3,7},{7,3},{8,12},{12,8},{9,1... | collective-permute-start | bytes 2359304 | tf_op jit(solution)/shard_map/ppermute | solution.py:200
  54.7 35.6 %all-to-all-start = ((bf16[8,256,256]{2,1,0:T(8,128)(2,1)}), bf16[8,256,256]{2,1,0:T(8,128)(2,1)S(1)}, u32[]{:S(2)}, u32[]{:S(2)}) async-start(bf16[8,256,256]{2,1,0:T(8,128)(2,1)} %bitcast.129), calls=%async_computation | async-start | bytes 2097152 | tf_op jit(solution)/shard_map/all_to_all | solution.py:206
  62.4 97.8 %all-gather.10.cloned.1.call-start = ((), (), s32[]{:S(2)}) async-start(), calls=%async_computation.8 | async-start | bytes 5242880 | tf_op jit(solution)/shard_map/all_gather | solution.py:213
  91.3 13.9 %all-to-all-start.1 = ((bf16[8,32,256]{2,1,0:T(8,128)(2,1)}), bf16[8,32,256]{2,1,0:T(8,128)(2,1)S(1)}, u32[]{:S(2)}, u32[]{:S(2)}) async-start(bf16[8,32,256]{2,1,0:T(8,128)(2,1)} %bitcast.4), calls=%async_computation.1 | async-start | bytes 262144 | tf_op jit(solution)/shard_map/all_to_all | solution.py:211
  96.1 110.4 %all-gather.12.cloned.1.call-start = ((), (), s32[]{:S(2)}) async-start(), calls=%async_computation.9 | async-start | bytes 4718592 | tf_op jit(solution)/shard_map/all_gather | solution.py:228
  113.0 8.9 %collective-permute-start.2 = (f32[4,32,256]{2,1,0:T(8,128)S(1)}, f32[4,32,256]{2,1,0:T(8,128)S(1)}, u32[]{:S(2)}, u32[]{:S(2)}) collective-permute-start(f32[4,32,256]{2,1,0:T(8,128)S(1)} %get-tuple-element.54), channel_id=1, source_target_pairs={{0,64},{64,128},{128,192},{192,0},{1,65},{65,129},{129,193},{193,1... | collective-permute-start | bytes 393224 | tf_op jit(solution)/shard_map/ppermute | solution.py:24
  113.9 8.1 %collective-permute-start.3 = (f32[4,32,256]{2,1,0:T(8,128)S(1)}, f32[4,32,256]{2,1,0:T(8,128)S(1)}, u32[]{:S(2)}, u32[]{:S(2)}) collective-permute-start(f32[4,32,256]{2,1,0:T(8,128)S(1)} %get-tuple-element.56), channel_id=1, source_target_pairs={{0,192},{64,0},{128,64},{192,128},{1,193},{65,1},{129,65},{193,129... | collective-permute-start | bytes 393224 | tf_op jit(solution)/shard_map/ppermute | solution.py:24
  115.1 13.1 %collective-permute-start.4 = (f32[4,32,256]{2,1,0:T(8,128)S(1)}, f32[4,32,256]{2,1,0:T(8,128)S(1)}, u32[]{:S(2)}, u32[]{:S(2)}) collective-permute-start(f32[4,32,256]{2,1,0:T(8,128)S(1)} %get-tuple-element.55), channel_id=1, source_target_pairs={{0,128},{64,192},{128,0},{192,64},{1,129},{65,193},{129,1},{193,65... | collective-permute-start | bytes 393224 | tf_op jit(solution)/shard_map/ppermute | solution.py:24
  163.8 10.4 %collective-permute-start.6 = (f32[64,1024]{1,0:T(8,128)S(1)}, f32[64,1024]{1,0:T(8,128)S(1)}, u32[]{:S(2)}, u32[]{:S(2)}) collective-permute-start(f32[64,1024]{1,0:T(8,128)S(1)} %get-tuple-element.45), channel_id=1, source_target_pairs={{0,8},{8,16},{16,24},{24,0},{1,9},{9,17},{17,25},{25,1},{2,10},{10... | collective-permute-start | bytes 786440 | tf_op jit(solution)/shard_map/ppermute | solution.py:24
  166.6 9.3 %collective-permute-start.7 = (f32[64,1024]{1,0:T(8,128)S(1)}, f32[64,1024]{1,0:T(8,128)}, u32[]{:S(2)}, u32[]{:S(2)}) collective-permute-start(f32[64,1024]{1,0:T(8,128)S(1)} %get-tuple-element.47), channel_id=1, source_target_pairs={{0,24},{8,0},{16,8},{24,16},{1,25},{9,1},{17,9},{25,17},{2,26},{10... | collective-permute-start | bytes 786440 | tf_op jit(solution)/shard_map/ppermute | solution.py:24
  167.9 12.2 %collective-permute-start.8 = (f32[64,1024]{1,0:T(8,128)S(1)}, f32[64,1024]{1,0:T(8,128)}, u32[]{:S(2)}, u32[]{:S(2)}) collective-permute-start(f32[64,1024]{1,0:T(8,128)S(1)} %get-tuple-element.46), channel_id=1, source_target_pairs={{0,16},{8,24},{16,0},{24,8},{1,17},{9,25},{17,1},{25,9},{2,18},{10... | collective-permute-start | bytes 786440 | tf_op jit(solution)/shard_map/ppermute | solution.py:24
  182.5 12.6 %all-to-all-start.3 = ((f32[16,1,320]{2,1,0:T(1,128)}), f32[16,1,320]{2,1,0:T(1,128)S(1)}, u32[]{:S(2)}, u32[]{:S(2)}) async-start(f32[16,1,320]{2,1,0:T(1,128)} %reshape.360), calls=%async_computation.3 | async-start | bytes 49152 | tf_op jit(solution)/shard_map/all_to_all | solution.py:16
  187.4 48.7 %all-gather.14.cloned.1.call-start = ((), (), s32[]{:S(2)}) async-start(), calls=%async_computation.10 | async-start | bytes 2621440 | tf_op jit(solution)/shard_map/all_gather | solution.py:286
  196.7 6.5 %collective-permute-start.9 = (bf16[64,1024]{1,0:T(8,128)(2,1)S(1)}, bf16[64,1024]{1,0:T(8,128)(2,1)S(1)}, u32[]{:S(2)}, u32[]{:S(2)}) collective-permute-start(bf16[64,1024]{1,0:T(8,128)(2,1)S(1)} %get-tuple-element.40), channel_id=1, source_target_pairs={{0,8},{8,16},{16,24},{24,0},{1,9},{9,17},{17,25},{25,1},{2,10},{10... | collective-permute-start | bytes 393224 | tf_op jit(solution)/shard_map/ppermute | solution.py:24
  198.0 7.3 %collective-permute-start.10 = (bf16[64,1024]{1,0:T(8,128)(2,1)S(1)}, bf16[64,1024]{1,0:T(8,128)(2,1)S(1)}, u32[]{:S(2)}, u32[]{:S(2)}) collective-permute-start(bf16[64,1024]{1,0:T(8,128)(2,1)S(1)} %get-tuple-element.40), channel_id=1, source_target_pairs={{0,24},{8,0},{16,8},{24,16},{1,25},{9,1},{17,9},{25,17},{2,26},{10... | collective-permute-start | bytes 393224 | tf_op jit(solution)/shard_map/ppermute | solution.py:24
  200.0 6.5 %collective-permute-start.11 = (bf16[64,1024]{1,0:T(8,128)(2,1)S(1)}, bf16[64,1024]{1,0:T(8,128)(2,1)S(1)}, u32[]{:S(2)}, u32[]{:S(2)}) collective-permute-start(bf16[64,1024]{1,0:T(8,128)(2,1)S(1)} %get-tuple-element.40), channel_id=1, source_target_pairs={{0,16},{8,24},{16,0},{24,8},{1,17},{9,25},{17,1},{25,9},{2,18},{10... | collective-permute-start | bytes 393224 | tf_op jit(solution)/shard_map/ppermute | solution.py:24
  218.4 32.9 %all-to-all-start.4 = ((f32[1,128,8,256]{3,1,0,2:T(8,128)}), f32[1,128,8,256]{3,1,0,2:T(8,128)S(1)}, u32[]{:S(2)}, u32[]{:S(2)}) async-start(f32[1,128,8,256]{3,1,0,2:T(8,128)} %copy.127), calls=%async_computation.4 | async-start | bytes 2097152 | tf_op jit(solution)/shard_map/all_to_all | solution.py:284
  251.3 61.1 %all-to-all-start.5 = ((f32[8,256,256]{2,1,0:T(8,128)}), f32[8,256,256]{2,1,0:T(8,128)}, u32[]{:S(2)}, u32[]{:S(2)}) async-start(f32[8,256,256]{2,1,0:T(8,128)} %get-tuple-element.30), calls=%async_computation.5 | async-start | bytes 4194304 | tf_op jit(solution)/shard_map/all_to_all | solution.py:291
  255.7 4.3 %collective-permute-start.13 = (bf16[128,256]{1,0:T(8,128)(2,1)S(1)}, bf16[128,256]{1,0:T(8,128)(2,1)S(1)}, u32[]{:S(2)}, u32[]{:S(2)}) collective-permute-start(bf16[128,256]{1,0:T(8,128)(2,1)S(1)} %reduce_sum.96), channel_id=1, source_target_pairs={{0,64},{64,128},{128,192},{192,0},{1,65},{65,129},{129,193},{193,1... | collective-permute-start | bytes 196616 | tf_op jit(solution)/shard_map/ppermute | solution.py:24
  257.2 4.3 %collective-permute-start.14 = (bf16[128,256]{1,0:T(8,128)(2,1)S(1)}, bf16[128,256]{1,0:T(8,128)(2,1)S(1)}, u32[]{:S(2)}, u32[]{:S(2)}) collective-permute-start(bf16[128,256]{1,0:T(8,128)(2,1)S(1)} %reduce_sum.96), channel_id=1, source_target_pairs={{0,192},{64,0},{128,64},{192,128},{1,193},{65,1},{129,65},{193,129... | collective-permute-start | bytes 196616 | tf_op jit(solution)/shard_map/ppermute | solution.py:24
  257.8 5.8 %collective-permute-start.15 = (bf16[128,256]{1,0:T(8,128)(2,1)S(1)}, bf16[128,256]{1,0:T(8,128)(2,1)S(1)}, u32[]{:S(2)}, u32[]{:S(2)}) collective-permute-start(bf16[128,256]{1,0:T(8,128)(2,1)S(1)} %reduce_sum.96), channel_id=1, source_target_pairs={{0,128},{64,192},{128,0},{192,64},{1,129},{65,193},{129,1},{193,65... | collective-permute-start | bytes 196616 | tf_op jit(solution)/shard_map/ppermute | solution.py:24
  276.3 5.4 %collective-permute-start.18 = (f32[2,256]{1,0:T(2,128)S(1)}, f32[2,256]{1,0:T(2,128)S(1)}, u32[]{:S(2)}, u32[]{:S(2)}) collective-permute-start(f32[2,256]{1,0:T(2,128)S(1)} %fusion.29), channel_id=1, source_target_pairs={{0,128},{64,192},{128,0},{192,64},{1,129},{65,193},{129,1},{193,65... | collective-permute-start | bytes 6152 | tf_op jit(solution)/shard_map/ppermute | solution.py:24
  278.1 3.6 %collective-permute-start.19 = (f32[2,256]{1,0:T(2,128)S(1)}, f32[2,256]{1,0:T(2,128)S(1)}, u32[]{:S(2)}, u32[]{:S(2)}) collective-permute-start(f32[2,256]{1,0:T(2,128)S(1)} %fusion.29), channel_id=1, source_target_pairs={{0,64},{64,128},{128,192},{192,0},{1,65},{65,129},{129,193},{193,1... | collective-permute-start | bytes 6152 | tf_op jit(solution)/shard_map/ppermute | solution.py:24
  280.1 3.6 %collective-permute-start.20 = (f32[2,256]{1,0:T(2,128)S(1)}, f32[2,256]{1,0:T(2,128)S(1)}, u32[]{:S(2)}, u32[]{:S(2)}) collective-permute-start(f32[2,256]{1,0:T(2,128)S(1)} %fusion.29), channel_id=1, source_target_pairs={{0,192},{64,0},{128,64},{192,128},{1,193},{65,1},{129,65},{193,129... | collective-permute-start | bytes 6152 | tf_op jit(solution)/shard_map/ppermute | solution.py:24
  283.7 5.2 %collective-permute-start.21 = (f32[2,256]{1,0:T(2,128)S(1)}, f32[2,256]{1,0:T(2,128)S(1)}, u32[]{:S(2)}, u32[]{:S(2)}) collective-permute-start(f32[2,256]{1,0:T(2,128)S(1)} %add_add_fusion.2), channel_id=1, source_target_pairs={{0,16},{8,24},{16,0},{24,8},{1,17},{9,25},{17,1},{25,9},{2,18},{10... | collective-permute-start | bytes 6152 | tf_op jit(solution)/shard_map/ppermute | solution.py:24
  284.7 4.8 %collective-permute-start.22 = (f32[2,256]{1,0:T(2,128)S(1)}, f32[2,256]{1,0:T(2,128)S(1)}, u32[]{:S(2)}, u32[]{:S(2)}) collective-permute-start(f32[2,256]{1,0:T(2,128)S(1)} %add_add_fusion.2), channel_id=1, source_target_pairs={{0,8},{8,16},{16,24},{24,0},{1,9},{9,17},{17,25},{25,1},{2,10},{10... | collective-permute-start | bytes 6152 | tf_op jit(solution)/shard_map/ppermute | solution.py:24
  290.7 12.7 %collective-permute-start.24 = (f32[2,256]{1,0:T(2,128)S(1)}, f32[2,256]{1,0:T(2,128)S(1)}, u32[]{:S(2)}, u32[]{:S(2)}) collective-permute-start(f32[2,256]{1,0:T(2,128)S(1)} %add_add_fusion.1), channel_id=1, source_target_pairs={{0,1},{1,0},{2,3},{3,2},{4,5},{5,4},{6,7},{7,6},{8,9},{9,8},{10,11... | collective-permute-start | bytes 6152 | tf_op jit(solution)/shard_map/ppermute | solution.py:180
  292.6 10.8 %collective-permute-start.25 = (f32[2,256]{1,0:T(2,128)S(1)}, f32[2,256]{1,0:T(2,128)S(1)}, u32[]{:S(2)}, u32[]{:S(2)}) collective-permute-start(f32[2,256]{1,0:T(2,128)S(1)} %add_add_fusion.1), channel_id=1, source_target_pairs={{0,2},{1,3},{2,0},{3,1},{4,6},{5,7},{6,4},{7,5},{8,10},{9,11},{10,... | collective-permute-start | bytes 6152 | tf_op jit(solution)/shard_map/ppermute | solution.py:180
  294.9 8.5 %collective-permute-start.26 = (f32[2,256]{1,0:T(2,128)S(1)}, f32[2,256]{1,0:T(2,128)S(1)}, u32[]{:S(2)}, u32[]{:S(2)}) collective-permute-start(f32[2,256]{1,0:T(2,128)S(1)} %add_add_fusion.1), channel_id=1, source_target_pairs={{0,3},{1,2},{2,1},{3,0},{4,7},{5,6},{6,5},{7,4},{8,11},{9,10},{10,... | collective-permute-start | bytes 6152 | tf_op jit(solution)/shard_map/ppermute | solution.py:180
  303.4 7.6 %collective-permute-start.27 = (f32[2,256]{1,0:T(2,128)S(1)}, f32[2,256]{1,0:T(2,128)S(1)}, u32[]{:S(2)}, u32[]{:S(2)}) collective-permute-start(f32[2,256]{1,0:T(2,128)S(1)} %add_add_fusion), channel_id=1, source_target_pairs={{0,4},{1,5},{2,6},{3,7},{4,0},{5,1},{6,2},{7,3},{8,12},{9,13},{10,... | collective-permute-start | bytes 6152 | tf_op jit(solution)/shard_map/ppermute | solution.py:182
  (19 other events, 287.7 us)
Sparse Core Ops, SparseCore 0:
  10.4 45.0 all-gather.5
  57.3 42.3 all-gather.7
  102.0 58.1 all-gather.9
  162.5 33.4 all-gather.11
  207.5 28.5 all-gather.13

commit v6 on v5

--- a/solution.py
+++ b/solution.py
@@ -38,9 +38,9 @@
 VMEM_BYTES = 56 * 1024 * 1024
 
 
-def kernel_params():
+def kernel_params(vmem_bytes=VMEM_BYTES):
     return pltpu.CompilerParams(
-        dimension_semantics=("arbitrary",), vmem_limit_bytes=VMEM_BYTES
+        dimension_semantics=("arbitrary",), vmem_limit_bytes=vmem_bytes
     )
 
 
@@ -87,7 +87,7 @@
             jax.ShapeDtypeStruct((deep, width), jnp.float32),
             jax.ShapeDtypeStruct((1, width), jnp.float32),
         ],
-        compiler_params=kernel_params(),
+        compiler_params=kernel_params(24 * 1024 * 1024),
         cost_estimate=pl.CostEstimate(
             flops=2 * feature.shape[0] * deep * width, bytes_accessed=10 * 2**20, transcendentals=0
         ),

time: 325 us -> 325 us (level)
  local copies, waits for them, and re-layouts: 21.1 us -> 25.5 us
  Pallas kernels: 20.1 us -> 16.6 us
    unnamed x31 -> x37, local copies, waits for them, and re-layouts: 6.24 us -> 11.5 us
    pallas_call x1, Pallas kernels: 7.34 us -> 3.86 us  [fc_product(): pl.pallas_call(fc_kernel, grid=(deep // block,), in_specs=[pl.BlockSpec((...]
  transfers between devices with their start and end apart: 38 -> 38, of which waited for: 29 -> 29; matrix products, arithmetic and copies ran while one was open for 11% -> 11% of each run, Pallas kernels for 5% -> 3%
where the time goes in v6:
time: 325 us; the launch traced here: 324 us
  waiting for transfers between devices  158 us (49%)
  starting transfers between devices  67.3 us (21%)
  local copies, waits for them, and re-layouts  25.5 us (8%)
  blocking collectives  19.4 us (6%)
  Pallas kernels  16.6 us (5%)
  between operations  16.4 us (5%)
  matrix products  15.4 us (5%)
  other arithmetic  5.72 us (2%)
    ppermute x18, waiting for transfers between devices, shift(): return lax.ppermute(value, axis, [(i, (i + by) % 4) for i in range(4)])  38.3 us
    ppermute x1, waiting for transfers between devices, per_device(): far = lax.ppermute(flat, 'zh', [(0, 1), (1, 0)])  33.4 us
    all_to_all x1, waiting for transfers between devices, per_device(): head = lax.all_to_all(head, DEPTH, 0, 0).reshape(depth, slab)  27.1 us
    ppermute x18, starting transfers between devices, shift(): return lax.ppermute(value, axis, [(i, (i + by) % 4) for i in range(4)])  24.7 us
    all_to_all x1, blocking collectives, spread(): lax.all_to_all(jnp.broadcast_to(value[None], (count,) + value.shape), axe...  19.4 us
    all_gather x1, waiting for transfers between devices, per_device(): lax.all_gather(shard.reshape(-1, columns), 'x', axis=0, tiled=True)  14.1 us
    unnamed x37, local copies, waits for them, and re-layouts  11.5 us
    all_gather x1, waiting for transfers between devices, per_device(): head = lax.all_gather(head, 'x', axis=1, tiled=True)  8.24 us
  transfers between devices with their start and end apart: 38, of which 29 were waited for; matrix products, arithmetic and copies ran while one was open for 11% of the time, Pallas kernels for 3%

profile of v6, /device:TPU:2, one launch (start us, length us, event | category | flops | bytes accessed | tf_op | source)
XLA Modules:
  0.0 324.2 jit_solution(14580867740164069008)
XLA Ops:
  10.1 7.3 %collective-permute-start = (bf16[128,3072]{1,0:T(8,128)(2,1)}, bf16[128,3072]{1,0:T(8,128)(2,1)S(1)}, u32[]{:S(2)}, u32[]{:S(2)}) collective-permute-start(bf16[128,3072]{1,0:T(8,128)(2,1)} %copy.116), channel_id=1, source_target_pairs={{0,4},{4,0},{1,5},{5,1},{2,6},{6,2},{3,7},{7,3},{8,12},{12,8},{9,1... | collective-permute-start | bytes 2359304 | tf_op jit(solution)/shard_map/ppermute | solution.py:200
  17.4 33.4 %collective-permute-done = bf16[128,3072]{1,0:T(8,128)(2,1)S(1)} collective-permute-done((bf16[128,3072]{1,0:T(8,128)(2,1)}, bf16[128,3072]{1,0:T(8,128)(2,1)S(1)}, u32[]{:S(2)}, u32[]{:S(2)}) %collective-permute-start) | collective-permute-done | bytes 786464 | tf_op jit(solution)/shard_map/ppermute | solution.py:200
  54.7 7.7 %all-to-all-start = ((bf16[8,256,256]{2,1,0:T(8,128)(2,1)}), bf16[8,256,256]{2,1,0:T(8,128)(2,1)S(1)}, u32[]{:S(2)}, u32[]{:S(2)}) async-start(bf16[8,256,256]{2,1,0:T(8,128)(2,1)} %bitcast.130), calls=%async_computation | async-start | bytes 2097152 | tf_op jit(solution)/shard_map/all_to_all | solution.py:206
  63.2 27.1 %all-to-all-done = bf16[8,256,256]{2,1,0:T(8,128)(2,1)S(1)} async-done(((bf16[8,256,256]{2,1,0:T(8,128)(2,1)}), bf16[8,256,256]{2,1,0:T(8,128)(2,1)S(1)}, u32[]{:S(2)}, u32[]{:S(2)}) %all-to-all-start) | async-done | bytes 1048608 | tf_op jit(solution)/shard_map/all_to_all | solution.py:206
  91.3 4.8 %all-to-all-start.1 = ((bf16[8,32,256]{2,1,0:T(8,128)(2,1)}), bf16[8,32,256]{2,1,0:T(8,128)(2,1)S(1)}, u32[]{:S(2)}, u32[]{:S(2)}) async-start(bf16[8,32,256]{2,1,0:T(8,128)(2,1)} %bitcast.4), calls=%async_computation.1 | async-start | bytes 262144 | tf_op jit(solution)/shard_map/all_to_all | solution.py:211
  96.1 2.9 fusion.37
  99.0 6.2 %all-to-all-done.1 = bf16[8,32,256]{2,1,0:T(8,128)(2,1)S(1)} async-done(((bf16[8,32,256]{2,1,0:T(8,128)(2,1)}), bf16[8,32,256]{2,1,0:T(8,128)(2,1)S(1)}, u32[]{:S(2)}, u32[]{:S(2)}) %all-to-all-start.1) | async-done | bytes 131104 | tf_op jit(solution)/shard_map/all_to_all | solution.py:211
  105.2 3.7 %broadcast_select_fusion.2 = (f32[512,256]{1,0:T(8,128)}, f32[512,256]{1,0:T(8,128)S(1)}) fusion(f32[512,256]{1,0:T(8,128)S(1)} %fusion.37, pred[]{:T(512)S(6)} %eq.53, bf16[512,3072]{1,0:T(8,128)(2,1)} %all-gather.8.cloned.1.call-done.refs_2_.refs_3_, bf16[3072,256]{1,0:T(8,128)(2,1)S(1)} %bitcast.121), kind=kOutput, calls=%fused_computation.27 | convolution fusion | flops 805437440 | bytes 6291457 | tf_op jit(solution)/shard_map/dot_general | solution.py:218
  116.9 5.1 %collective-permute-done.2 = f32[4,32,256]{2,1,0:T(8,128)S(1)} collective-permute-done((f32[4,32,256]{2,1,0:T(8,128)S(1)}, f32[4,32,256]{2,1,0:T(8,128)S(1)}, u32[]{:S(2)}, u32[]{:S(2)}) %collective-permute-start.2) | collective-permute-done | bytes 131104 | tf_op jit(solution)/shard_map/ppermute | solution.py:24
  122.0 6.3 %collective-permute-done.4 = f32[4,32,256]{2,1,0:T(8,128)S(1)} collective-permute-done((f32[4,32,256]{2,1,0:T(8,128)S(1)}, f32[4,32,256]{2,1,0:T(8,128)S(1)}, u32[]{:S(2)}, u32[]{:S(2)}) %collective-permute-start.4) | collective-permute-done | bytes 131104 | tf_op jit(solution)/shard_map/ppermute | solution.py:24
  128.3 19.4 %all_to_all.40 = bf16[8,128,256]{2,1,0:T(8,128)(2,1)S(1)} all-to-all(bf16[8,128,256]{2,1,0:T(8,128)(2,1)S(1)} %broadcast_in_dim.59), channel_id=1, replica_groups=mesh['x'=4,'core'=2,'y'=4,'zh'=2,'zl'=4] {'zh','zl'}, dimensions={0} | all-to-all | bytes 1048576 | tf_op jit(solution)/shard_map/all_to_all | solution.py:16
  152.0 8.2 %all-gather.10.cloned.1.call-done = bf16[2048,1024]{1,0:T(8,128)(2,1)} async-done(((bf16[2048,256]{1,0:T(8,128)(2,1)}), bf16[2048,1024]{1,0:T(8,128)(2,1)}) %all-gather.10.cloned.1.call-update) | async-done | bytes 4194320 | tf_op jit(solution)/shard_map/all_gather | solution.py:213
  160.2 3.4 %fusion = f32[4,64,1024]{2,1,0:T(8,128)S(1)} fusion(bf16[4,64,2048]{2,1,0:T(8,128)(2,1)S(1)} %bitcast.145, bf16[2048,1024]{1,0:T(8,128)(2,1)} %all-gather.10.cloned.1.call-done), kind=kOutput, calls=%fused_computation.1 | convolution fusion | flops 1073741824 | bytes 6291456 | tf_op jit(solution)/shard_map/dot_general | solution.py:233
  163.8 2.8 collective-permute-start.6
  170.6 3.6 %collective-permute-done.6 = f32[64,1024]{1,0:T(8,128)S(1)} collective-permute-done((f32[64,1024]{1,0:T(8,128)S(1)}, f32[64,1024]{1,0:T(8,128)S(1)}, u32[]{:S(2)}, u32[]{:S(2)}) %collective-permute-start.6) | collective-permute-done | bytes 262176 | tf_op jit(solution)/shard_map/ppermute | solution.py:24
  175.9 4.2 %collective-permute-done.8 = f32[64,1024]{1,0:T(8,128)} collective-permute-done((f32[64,1024]{1,0:T(8,128)S(1)}, f32[64,1024]{1,0:T(8,128)}, u32[]{:S(2)}, u32[]{:S(2)}) %collective-permute-start.8) | collective-permute-done | bytes 262176 | tf_op jit(solution)/shard_map/ppermute | solution.py:24
  182.5 4.9 %all-to-all-start.3 = ((f32[16,1,320]{2,1,0:T(1,128)}), f32[16,1,320]{2,1,0:T(1,128)S(1)}, u32[]{:S(2)}, u32[]{:S(2)}) async-start(f32[16,1,320]{2,1,0:T(1,128)} %reshape.360), calls=%async_computation.3 | async-start | bytes 49152 | tf_op jit(solution)/shard_map/all_to_all | solution.py:16
  187.5 7.5 %all-to-all-done.3 = f32[16,1,320]{2,1,0:T(1,128)S(1)} async-done(((f32[16,1,320]{2,1,0:T(1,128)}), f32[16,1,320]{2,1,0:T(1,128)S(1)}, u32[]{:S(2)}, u32[]{:S(2)}) %all-to-all-start.3) | async-done | bytes 20512 | tf_op jit(solution)/shard_map/all_to_all | solution.py:16
  200.1 3.0 collective-permute-done.9
  208.6 3.9 %fusion.38 = f32[128,2048]{1,0:T(8,128)S(1)} fusion(bf16[128,1024]{1,0:T(8,128)(2,1)S(1)} %bitcast.149, bf16[2048,1024]{1,0:T(8,128)(2,1)} %all-gather.10.cloned.1.call-done), kind=kOutput, calls=%fused_computation.93 | convolution fusion | flops 536870912 | bytes 5505024 | tf_op jit(solution)/shard_map/dot_general | solution.py:280
  212.6 2.6 collective-permute-done.12
  218.4 3.6 %all-to-all-start.4 = ((f32[1,128,8,256]{3,1,0,2:T(8,128)}), f32[1,128,8,256]{3,1,0,2:T(8,128)S(1)}, u32[]{:S(2)}, u32[]{:S(2)}) async-start(f32[1,128,8,256]{3,1,0,2:T(8,128)} %copy.127), calls=%async_computation.4 | async-start | bytes 2097152 | tf_op jit(solution)/shard_map/all_to_all | solution.py:284
  221.9 14.1 %all-gather.14.cloned.1.call-done = bf16[1024,1024]{1,0:T(8,128)(2,1)} async-done(((bf16[256,1024]{1,0:T(8,128)(2,1)}), bf16[1024,1024]{1,0:T(8,128)(2,1)}) %all-gather.14.cloned.1.call-update) | async-done | bytes 2097168 | tf_op jit(solution)/shard_map/all_gather | solution.py:286
  238.0 7.5 %shard_map.103 = (f32[8,256,256]{2,1,0:T(8,128)}, f32[1,256]{1,0:T(1,128)}) custom-call(bf16[1024,2048]{1,0:T(8,128)(2,1)} %all-gather.12.cloned.1.call-done.joined_ref, bf16[1024,256]{1,0:T(8,128)(2,1)} %bitcast.136), custom_call_target="tpu_custom_call" | custom-call | flops 1073741824 | bytes 7340032 | tf_op jit(solution)/shard_map/pallas_call | solution.py:117
  245.5 5.8 %all-to-all-done.4 = f32[1,128,8,256]{3,1,0,2:T(8,128)S(1)} async-done(((f32[1,128,8,256]{3,1,0,2:T(8,128)}), f32[1,128,8,256]{3,1,0,2:T(8,128)S(1)}, u32[]{:S(2)}, u32[]{:S(2)}) %all-to-all-start.4) | async-done | bytes 1048608 | tf_op jit(solution)/shard_map/all_to_all | solution.py:284
  251.3 4.3 %all-to-all-start.5 = ((f32[8,256,256]{2,1,0:T(8,128)}), f32[8,256,256]{2,1,0:T(8,128)}, u32[]{:S(2)}, u32[]{:S(2)}) async-start(f32[8,256,256]{2,1,0:T(8,128)} %get-tuple-element.30), calls=%async_computation.5 | async-start | bytes 4194304 | tf_op jit(solution)/shard_map/all_to_all | solution.py:291
  269.7 3.9 %shard_map.104 = (f32[3072,256]{1,0:T(8,128)S(1)}, f32[1,256]{1,0:T(1,128)S(1)}) custom-call(bf16[512,3072]{1,0:T(8,128)(2,1)S(1)} %copy-done.2, bf16[512,3072]{1,0:T(8,128)(2,1)S(1)} %copy-done.2, bf16[512,3072]{1,0:T(8,128)(2,1)S(1)} %copy-done.1, bf16[512,3072]{1,0:T(8,128)(2,1)S(1)} %copy-done.1, bf16[1024,256]{1,0:T(8,128)(2,1)S(1)} %bitcast.122), custom_call_target="tpu_custom_call" | custom-call | flops 1610612736 | bytes 10485760 | tf_op jit(solution)/shard_map/pallas_call | solution.py:73
  285.0 2.4 collective-permute-start.22
  295.4 8.0 %collective-permute-done.24 = f32[2,256]{1,0:T(2,128)S(1)} collective-permute-done((f32[2,256]{1,0:T(2,128)S(1)}, f32[2,256]{1,0:T(2,128)S(1)}, u32[]{:S(2)}, u32[]{:S(2)}) %collective-permute-start.24) | collective-permute-done | bytes 2080 | tf_op jit(solution)/shard_map/ppermute | solution.py:180
  303.4 4.6 %collective-permute-start.27 = (f32[2,256]{1,0:T(2,128)S(1)}, f32[2,256]{1,0:T(2,128)S(1)}, u32[]{:S(2)}, u32[]{:S(2)}) collective-permute-start(f32[2,256]{1,0:T(2,128)S(1)} %add_add_fusion), channel_id=1, source_target_pairs={{0,4},{1,5},{2,6},{3,7},{4,0},{5,1},{6,2},{7,3},{8,12},{9,13},{10,... | collective-permute-start | bytes 6152 | tf_op jit(solution)/shard_map/ppermute | solution.py:182
  308.0 3.0 collective-permute-done.27
  312.4 5.3 %shard_map.105 = (f32[3072,256]{1,0:T(8,128)}, f32[256,2048]{1,0:T(8,128)}) custom-call(f32[1,1]{1,0:T(1,128)} %bitcast.57.scale_ref, f32[3072,256]{1,0:T(8,128)} %copy-done.3, f32[2,4,256,256]{3,2,1,0:T(8,128)} %bitcast.58.head_ref), custom_call_target="tpu_custom_call" | custom-call | flops 1310720 | bytes 10485760 | tf_op jit(solution)/shard_map/pallas_call | solution.py:151
  (171 shorter events, 77.5 us)
Async XLA Ops:
  7.2 88.9 %all-gather.6.cloned.1.call-start = ((), (), s32[]{:S(2)}) async-start(), calls=%async_computation.6 | async-start | bytes 3932160 | tf_op jit(solution)/shard_map/all_gather | solution.py:201
  10.0 95.2 %all-gather.8.cloned.1.call-start = ((), (), s32[]{:S(2)}) async-start(), calls=%async_computation.7 | async-start | bytes 3932160 | tf_op jit(solution)/shard_map/all_gather | solution.py:202
  10.1 40.7 %collective-permute-start = (bf16[128,3072]{1,0:T(8,128)(2,1)}, bf16[128,3072]{1,0:T(8,128)(2,1)S(1)}, u32[]{:S(2)}, u32[]{:S(2)}) collective-permute-start(bf16[128,3072]{1,0:T(8,128)(2,1)} %copy.116), channel_id=1, source_target_pairs={{0,4},{4,0},{1,5},{5,1},{2,6},{6,2},{3,7},{7,3},{8,12},{12,8},{9,1... | collective-permute-start | bytes 2359304 | tf_op jit(solution)/shard_map/ppermute | solution.py:200
  54.7 35.6 %all-to-all-start = ((bf16[8,256,256]{2,1,0:T(8,128)(2,1)}), bf16[8,256,256]{2,1,0:T(8,128)(2,1)S(1)}, u32[]{:S(2)}, u32[]{:S(2)}) async-start(bf16[8,256,256]{2,1,0:T(8,128)(2,1)} %bitcast.130), calls=%async_computation | async-start | bytes 2097152 | tf_op jit(solution)/shard_map/all_to_all | solution.py:206
  62.4 97.8 %all-gather.10.cloned.1.call-start = ((), (), s32[]{:S(2)}) async-start(), calls=%async_computation.8 | async-start | bytes 5242880 | tf_op jit(solution)/shard_map/all_gather | solution.py:213
  91.3 13.9 %all-to-all-start.1 = ((bf16[8,32,256]{2,1,0:T(8,128)(2,1)}), bf16[8,32,256]{2,1,0:T(8,128)(2,1)S(1)}, u32[]{:S(2)}, u32[]{:S(2)}) async-start(bf16[8,32,256]{2,1,0:T(8,128)(2,1)} %bitcast.4), calls=%async_computation.1 | async-start | bytes 262144 | tf_op jit(solution)/shard_map/all_to_all | solution.py:211
  96.1 110.4 %all-gather.12.cloned.1.call-start = ((), (), s32[]{:S(2)}) async-start(), calls=%async_computation.9 | async-start | bytes 4718592 | tf_op jit(solution)/shard_map/all_gather | solution.py:228
  113.0 8.9 %collective-permute-start.2 = (f32[4,32,256]{2,1,0:T(8,128)S(1)}, f32[4,32,256]{2,1,0:T(8,128)S(1)}, u32[]{:S(2)}, u32[]{:S(2)}) collective-permute-start(f32[4,32,256]{2,1,0:T(8,128)S(1)} %get-tuple-element.54), channel_id=1, source_target_pairs={{0,64},{64,128},{128,192},{192,0},{1,65},{65,129},{129,193},{193,1... | collective-permute-start | bytes 393224 | tf_op jit(solution)/shard_map/ppermute | solution.py:24
  113.8 8.1 %collective-permute-start.3 = (f32[4,32,256]{2,1,0:T(8,128)S(1)}, f32[4,32,256]{2,1,0:T(8,128)S(1)}, u32[]{:S(2)}, u32[]{:S(2)}) collective-permute-start(f32[4,32,256]{2,1,0:T(8,128)S(1)} %get-tuple-element.56), channel_id=1, source_target_pairs={{0,192},{64,0},{128,64},{192,128},{1,193},{65,1},{129,65},{193,129... | collective-permute-start | bytes 393224 | tf_op jit(solution)/shard_map/ppermute | solution.py:24
  115.1 13.1 %collective-permute-start.4 = (f32[4,32,256]{2,1,0:T(8,128)S(1)}, f32[4,32,256]{2,1,0:T(8,128)S(1)}, u32[]{:S(2)}, u32[]{:S(2)}) collective-permute-start(f32[4,32,256]{2,1,0:T(8,128)S(1)} %get-tuple-element.55), channel_id=1, source_target_pairs={{0,128},{64,192},{128,0},{192,64},{1,129},{65,193},{129,1},{193,65... | collective-permute-start | bytes 393224 | tf_op jit(solution)/shard_map/ppermute | solution.py:24
  163.8 10.4 %collective-permute-start.6 = (f32[64,1024]{1,0:T(8,128)S(1)}, f32[64,1024]{1,0:T(8,128)S(1)}, u32[]{:S(2)}, u32[]{:S(2)}) collective-permute-start(f32[64,1024]{1,0:T(8,128)S(1)} %get-tuple-element.45), channel_id=1, source_target_pairs={{0,8},{8,16},{16,24},{24,0},{1,9},{9,17},{17,25},{25,1},{2,10},{10... | collective-permute-start | bytes 786440 | tf_op jit(solution)/shard_map/ppermute | solution.py:24
  166.6 9.4 %collective-permute-start.7 = (f32[64,1024]{1,0:T(8,128)S(1)}, f32[64,1024]{1,0:T(8,128)}, u32[]{:S(2)}, u32[]{:S(2)}) collective-permute-start(f32[64,1024]{1,0:T(8,128)S(1)} %get-tuple-element.47), channel_id=1, source_target_pairs={{0,24},{8,0},{16,8},{24,16},{1,25},{9,1},{17,9},{25,17},{2,26},{10... | collective-permute-start | bytes 786440 | tf_op jit(solution)/shard_map/ppermute | solution.py:24
  167.9 12.2 %collective-permute-start.8 = (f32[64,1024]{1,0:T(8,128)S(1)}, f32[64,1024]{1,0:T(8,128)}, u32[]{:S(2)}, u32[]{:S(2)}) collective-permute-start(f32[64,1024]{1,0:T(8,128)S(1)} %get-tuple-element.46), channel_id=1, source_target_pairs={{0,16},{8,24},{16,0},{24,8},{1,17},{9,25},{17,1},{25,9},{2,18},{10... | collective-permute-start | bytes 786440 | tf_op jit(solution)/shard_map/ppermute | solution.py:24
  182.5 12.6 %all-to-all-start.3 = ((f32[16,1,320]{2,1,0:T(1,128)}), f32[16,1,320]{2,1,0:T(1,128)S(1)}, u32[]{:S(2)}, u32[]{:S(2)}) async-start(f32[16,1,320]{2,1,0:T(1,128)} %reshape.360), calls=%async_computation.3 | async-start | bytes 49152 | tf_op jit(solution)/shard_map/all_to_all | solution.py:16
  187.4 48.7 %all-gather.14.cloned.1.call-start = ((), (), s32[]{:S(2)}) async-start(), calls=%async_computation.10 | async-start | bytes 2621440 | tf_op jit(solution)/shard_map/all_gather | solution.py:286
  196.7 6.5 %collective-permute-start.9 = (bf16[64,1024]{1,0:T(8,128)(2,1)S(1)}, bf16[64,1024]{1,0:T(8,128)(2,1)S(1)}, u32[]{:S(2)}, u32[]{:S(2)}) collective-permute-start(bf16[64,1024]{1,0:T(8,128)(2,1)S(1)} %get-tuple-element.40), channel_id=1, source_target_pairs={{0,8},{8,16},{16,24},{24,0},{1,9},{9,17},{17,25},{25,1},{2,10},{10... | collective-permute-start | bytes 393224 | tf_op jit(solution)/shard_map/ppermute | solution.py:24
  197.9 7.3 %collective-permute-start.10 = (bf16[64,1024]{1,0:T(8,128)(2,1)S(1)}, bf16[64,1024]{1,0:T(8,128)(2,1)S(1)}, u32[]{:S(2)}, u32[]{:S(2)}) collective-permute-start(bf16[64,1024]{1,0:T(8,128)(2,1)S(1)} %get-tuple-element.40), channel_id=1, source_target_pairs={{0,24},{8,0},{16,8},{24,16},{1,25},{9,1},{17,9},{25,17},{2,26},{10... | collective-permute-start | bytes 393224 | tf_op jit(solution)/shard_map/ppermute | solution.py:24
  200.0 6.5 %collective-permute-start.11 = (bf16[64,1024]{1,0:T(8,128)(2,1)S(1)}, bf16[64,1024]{1,0:T(8,128)(2,1)S(1)}, u32[]{:S(2)}, u32[]{:S(2)}) collective-permute-start(bf16[64,1024]{1,0:T(8,128)(2,1)S(1)} %get-tuple-element.40), channel_id=1, source_target_pairs={{0,16},{8,24},{16,0},{24,8},{1,17},{9,25},{17,1},{25,9},{2,18},{10... | collective-permute-start | bytes 393224 | tf_op jit(solution)/shard_map/ppermute | solution.py:24
  218.4 32.9 %all-to-all-start.4 = ((f32[1,128,8,256]{3,1,0,2:T(8,128)}), f32[1,128,8,256]{3,1,0,2:T(8,128)S(1)}, u32[]{:S(2)}, u32[]{:S(2)}) async-start(f32[1,128,8,256]{3,1,0,2:T(8,128)} %copy.127), calls=%async_computation.4 | async-start | bytes 2097152 | tf_op jit(solution)/shard_map/all_to_all | solution.py:284
  251.3 61.1 %all-to-all-start.5 = ((f32[8,256,256]{2,1,0:T(8,128)}), f32[8,256,256]{2,1,0:T(8,128)}, u32[]{:S(2)}, u32[]{:S(2)}) async-start(f32[8,256,256]{2,1,0:T(8,128)} %get-tuple-element.30), calls=%async_computation.5 | async-start | bytes 4194304 | tf_op jit(solution)/shard_map/all_to_all | solution.py:291
  255.7 4.3 %collective-permute-start.13 = (bf16[128,256]{1,0:T(8,128)(2,1)S(1)}, bf16[128,256]{1,0:T(8,128)(2,1)S(1)}, u32[]{:S(2)}, u32[]{:S(2)}) collective-permute-start(bf16[128,256]{1,0:T(8,128)(2,1)S(1)} %reduce_sum.96), channel_id=1, source_target_pairs={{0,64},{64,128},{128,192},{192,0},{1,65},{65,129},{129,193},{193,1... | collective-permute-start | bytes 196616 | tf_op jit(solution)/shard_map/ppermute | solution.py:24
  257.2 4.3 %collective-permute-start.14 = (bf16[128,256]{1,0:T(8,128)(2,1)S(1)}, bf16[128,256]{1,0:T(8,128)(2,1)S(1)}, u32[]{:S(2)}, u32[]{:S(2)}) collective-permute-start(bf16[128,256]{1,0:T(8,128)(2,1)S(1)} %reduce_sum.96), channel_id=1, source_target_pairs={{0,192},{64,0},{128,64},{192,128},{1,193},{65,1},{129,65},{193,129... | collective-permute-start | bytes 196616 | tf_op jit(solution)/shard_map/ppermute | solution.py:24
  257.8 5.8 %collective-permute-start.15 = (bf16[128,256]{1,0:T(8,128)(2,1)S(1)}, bf16[128,256]{1,0:T(8,128)(2,1)S(1)}, u32[]{:S(2)}, u32[]{:S(2)}) collective-permute-start(bf16[128,256]{1,0:T(8,128)(2,1)S(1)} %reduce_sum.96), channel_id=1, source_target_pairs={{0,128},{64,192},{128,0},{192,64},{1,129},{65,193},{129,1},{193,65... | collective-permute-start | bytes 196616 | tf_op jit(solution)/shard_map/ppermute | solution.py:24
  276.7 5.4 %collective-permute-start.18 = (f32[2,256]{1,0:T(2,128)S(1)}, f32[2,256]{1,0:T(2,128)S(1)}, u32[]{:S(2)}, u32[]{:S(2)}) collective-permute-start(f32[2,256]{1,0:T(2,128)S(1)} %fusion.29), channel_id=1, source_target_pairs={{0,128},{64,192},{128,0},{192,64},{1,129},{65,193},{129,1},{193,65... | collective-permute-start | bytes 6152 | tf_op jit(solution)/shard_map/ppermute | solution.py:24
  278.4 3.6 %collective-permute-start.19 = (f32[2,256]{1,0:T(2,128)S(1)}, f32[2,256]{1,0:T(2,128)S(1)}, u32[]{:S(2)}, u32[]{:S(2)}) collective-permute-start(f32[2,256]{1,0:T(2,128)S(1)} %fusion.29), channel_id=1, source_target_pairs={{0,64},{64,128},{128,192},{192,0},{1,65},{65,129},{129,193},{193,1... | collective-permute-start | bytes 6152 | tf_op jit(solution)/shard_map/ppermute | solution.py:24
  280.4 3.6 %collective-permute-start.20 = (f32[2,256]{1,0:T(2,128)S(1)}, f32[2,256]{1,0:T(2,128)S(1)}, u32[]{:S(2)}, u32[]{:S(2)}) collective-permute-start(f32[2,256]{1,0:T(2,128)S(1)} %fusion.29), channel_id=1, source_target_pairs={{0,192},{64,0},{128,64},{192,128},{1,193},{65,1},{129,65},{193,129... | collective-permute-start | bytes 6152 | tf_op jit(solution)/shard_map/ppermute | solution.py:24
  284.0 5.2 %collective-permute-start.21 = (f32[2,256]{1,0:T(2,128)S(1)}, f32[2,256]{1,0:T(2,128)S(1)}, u32[]{:S(2)}, u32[]{:S(2)}) collective-permute-start(f32[2,256]{1,0:T(2,128)S(1)} %add_add_fusion.2), channel_id=1, source_target_pairs={{0,16},{8,24},{16,0},{24,8},{1,17},{9,25},{17,1},{25,9},{2,18},{10... | collective-permute-start | bytes 6152 | tf_op jit(solution)/shard_map/ppermute | solution.py:24
  285.0 4.8 %collective-permute-start.22 = (f32[2,256]{1,0:T(2,128)S(1)}, f32[2,256]{1,0:T(2,128)S(1)}, u32[]{:S(2)}, u32[]{:S(2)}) collective-permute-start(f32[2,256]{1,0:T(2,128)S(1)} %add_add_fusion.2), channel_id=1, source_target_pairs={{0,8},{8,16},{16,24},{24,0},{1,9},{9,17},{17,25},{25,1},{2,10},{10... | collective-permute-start | bytes 6152 | tf_op jit(solution)/shard_map/ppermute | solution.py:24
  291.0 12.4 %collective-permute-start.24 = (f32[2,256]{1,0:T(2,128)S(1)}, f32[2,256]{1,0:T(2,128)S(1)}, u32[]{:S(2)}, u32[]{:S(2)}) collective-permute-start(f32[2,256]{1,0:T(2,128)S(1)} %add_add_fusion.1), channel_id=1, source_target_pairs={{0,1},{1,0},{2,3},{3,2},{4,5},{5,4},{6,7},{7,6},{8,9},{9,8},{10,11... | collective-permute-start | bytes 6152 | tf_op jit(solution)/shard_map/ppermute | solution.py:180
  292.9 10.5 %collective-permute-start.25 = (f32[2,256]{1,0:T(2,128)S(1)}, f32[2,256]{1,0:T(2,128)S(1)}, u32[]{:S(2)}, u32[]{:S(2)}) collective-permute-start(f32[2,256]{1,0:T(2,128)S(1)} %add_add_fusion.1), channel_id=1, source_target_pairs={{0,2},{1,3},{2,0},{3,1},{4,6},{5,7},{6,4},{7,5},{8,10},{9,11},{10,... | collective-permute-start | bytes 6152 | tf_op jit(solution)/shard_map/ppermute | solution.py:180
  295.3 8.1 %collective-permute-start.26 = (f32[2,256]{1,0:T(2,128)S(1)}, f32[2,256]{1,0:T(2,128)S(1)}, u32[]{:S(2)}, u32[]{:S(2)}) collective-permute-start(f32[2,256]{1,0:T(2,128)S(1)} %add_add_fusion.1), channel_id=1, source_target_pairs={{0,3},{1,2},{2,1},{3,0},{4,7},{5,6},{6,5},{7,4},{8,11},{9,10},{10,... | collective-permute-start | bytes 6152 | tf_op jit(solution)/shard_map/ppermute | solution.py:180
  303.4 7.6 %collective-permute-start.27 = (f32[2,256]{1,0:T(2,128)S(1)}, f32[2,256]{1,0:T(2,128)S(1)}, u32[]{:S(2)}, u32[]{:S(2)}) collective-permute-start(f32[2,256]{1,0:T(2,128)S(1)} %add_add_fusion), channel_id=1, source_target_pairs={{0,4},{1,5},{2,6},{3,7},{4,0},{5,1},{6,2},{7,3},{8,12},{9,13},{10,... | collective-permute-start | bytes 6152 | tf_op jit(solution)/shard_map/ppermute | solution.py:182
  (22 other events, 291.2 us)
Sparse Core Ops, SparseCore 0:
  10.4 45.0 all-gather.5
  57.3 42.3 all-gather.7
  102.0 58.1 all-gather.9
  162.5 33.4 all-gather.11
  207.4 28.5 all-gather.13
